TPU v7x, 32 devices: a whole 2x2x4 slice. The times are simulated.
32 devices in a mesh: group: 4 (over y, core), fsdp: 8 (over z, x).
Axes of the slice: x: 2, y: 2, z: 4, core: 2. Of those that a mesh axis runs over, the one named last changes fastest.
Arguments:
- tokens: bfloat16 [4, 3072, 4096], P('group', 'fsdp'), may hold values from -6 to 6
- targets: bfloat16 [4, 3072, 512], P('group', 'fsdp'), may hold values from -6 to 6
- params: float32 [4, 4096, 512], P('group', 'fsdp'), may hold values from -6 to 6
- momentum: float32 [4, 4096, 512], P('group', 'fsdp'), may hold values from -6 to 6
- push_weight: float32 [4], P('group'), may hold values from 0.5 to 2
Outputs:
- new_params: float32 [4, 4096, 512], P('group', 'fsdp')
- new_momentum: float32 [4, 4096, 512], P('group', 'fsdp')
All inputs are finite; a program needn't handle non-finite values.
Results may differ from a plain program's by a relative error of at most 0.0031.
Values may be sent and summed in bfloat16 or wider, within the bound.
No kernel may reach another device: no remote copies, remote signals or barrier semaphores. Data moves between devices by JAX's collectives and lax.ppermute only.
A program may use at most 64 MiB of HBM per device.

v0:
```python
import jax
import jax.numpy as jnp
from jax import lax
from jax.sharding import PartitionSpec as P

STEPS = 2
CHUNKS = 4
OCCUPANCY = {"line": 5.5, "pair": 7.9, "group": 4.0}
LATENCY = 3.2
PREPARE = 0.6
SWAP_ENDS = 36.0


def from_behind(value, axis, steps):
    count = lax.axis_size(axis)
    pairs = [(source, (source + steps) % count) for source in range(count)]
    return lax.ppermute(value, axis, pairs)


def after(value, *earlier):
    return lax.optimization_barrier((value, *earlier))[0]


def issue_order(half):
    hops = ["line"] * (half - 1)
    plan = (hops + ["pair"] + hops + ["group"]) * STEPS
    free = {"line": 0.0, "pair": SWAP_ENDS, "group": 0.0, "core": 0.0}
    ready = [0.01 * c for c in range(CHUNKS)]
    at = [0] * CHUNKS
    order = []
    while len(order) < CHUNKS * len(plan):
        c = min((c for c in range(CHUNKS) if at[c] < len(plan)), key=lambda c: ready[c])
        link = plan[at[c]]
        free["core"] = max(ready[c], free["core"]) + PREPARE
        start = max(free["core"], free[link])
        free[link] = start + OCCUPANCY[link] * 2 / CHUNKS
        ready[c] = free[link] + LATENCY
        at[c] += 1
        order.append(c)
    return order


def shards(tokens, targets, params, momentum, push_weight):
    inputs = tokens[0]
    rows, width = inputs.shape
    features = params.shape[2]
    count = lax.axis_size("fsdp")
    half = count // 2
    block = width // count
    place = lax.div(lax.axis_index("fsdp"), 2)
    lane = lax.rem(lax.axis_index("fsdp"), 2)
    key_scale = width ** (-0.5)
    part = features // CHUNKS
    contract = (((0,), (0,)), ((), ()))
    wide = jnp.float32
    narrow = jnp.bfloat16
    issued = []

    def send(value, link, steps=1):
        if issued:
            value = after(value, issued[-1])
        issued.append(value)
        if link == "pair":
            return lax.ppermute(value, "fsdp", [(i, i ^ 1) for i in range(count)])
        if link == "line":
            return from_behind(value, "fsdp", 2)
        return from_behind(value, "group", steps)

    def chunk(array, c):
        return array[:, c * part : (c + 1) * part]

    def half_columns(side):
        pieces = []
        for back in range(half):
            start = (2 * lax.rem(place - back + half, half) + side) * block
            pieces.append(lax.dynamic_slice_in_dim(inputs, start, block, 1))
        return jnp.concatenate(pieces, axis=1)

    def column_block(back):
        return pair_tokens[:, back * block : (back + 1) * block]

    outgoing = half_columns(1 - lane)
    theirs = send(outgoing, "pair")
    params = after(params, outgoing)
    momentum = after(momentum, outgoing)
    zero = jnp.zeros((), lane.dtype)
    pair_tokens = jnp.zeros((2 * rows, width // 2), inputs.dtype)
    pair_tokens = lax.dynamic_update_slice(
        pair_tokens, half_columns(lane), (lane * rows, zero)
    )
    pair_tokens = lax.dynamic_update_slice(pair_tokens, theirs, ((1 - lane) * rows, zero))
    pair_targets = lax.dynamic_update_slice(
        jnp.zeros((2 * rows, features), targets.dtype), targets[0], (lane * rows, zero)
    )
    replica = lax.axis_index("group")
    every = lax.all_gather(push_weight, "group", axis=0, tiled=True)
    weights = [push_weight]
    for step in range(STEPS):
        every = 0.5 * every + 0.5 * jnp.roll(every, 2**step)
        weights.append(lax.dynamic_slice_in_dim(every, replica, 1))
    kept = [[] for _ in range(STEPS)]
    passed = {}
    results = [jnp.zeros_like(params[0]), jnp.zeros_like(momentum[0])]

    def stream(c):
        state = chunk(params[0], c)
        moment = chunk(momentum[0], c)
        target = chunk(pair_targets, c).astype(wide)
        for step in range(STEPS):
            kept[step].append(state - (0.2 * 0.9) * moment)
            pieces = [(state / weights[step][0]).astype(narrow)]
            for _ in range(half - 1):
                pieces.append((yield pieces[-1], "line"))
            if step == 0:
                keys = jnp.dot(
                    pair_tokens, jnp.concatenate(pieces, axis=0), preferred_element_type=wide
                )
            else:
                keys = sum(
                    jnp.dot(column_block(back), piece, preferred_element_type=wide)
                    for back, piece in enumerate(pieces)
                )
            residual = key_scale * keys - target
            received = yield residual.astype(narrow), "pair"
            grad_out = (key_scale * (residual + received.astype(wide))).astype(narrow)

            def partial(back):
                return lax.dot_general(
                    column_block(back), grad_out, contract, preferred_element_type=wide
                )

            total = partial(1)
            for back in range(2, half + 1):
                arrived = yield total.astype(narrow), "line"
                total = arrived.astype(wide) + partial(back % half)
            behind = yield total.astype(narrow), "group"
            moment = 0.9 * moment + total
            mixed = 0.5 * (kept[step][c] + chunk(passed[step], c).astype(wide))
            state = mixed - 0.1 * (total + behind.astype(wide))
        fresh = [state / weights[STEPS][0], moment]
        for i in range(2):
            results[i] = lax.dynamic_update_slice(results[i], fresh[i], (0, c * part))
        yield None, None

    streams = [stream(c) for c in range(CHUNKS)]
    waiting = [next(running) for running in streams]
    groups_sent = [0] * CHUNKS
    for c in issue_order(half):
        value, link = waiting[c]
        result = send(value, link, 2 ** groups_sent[c])
        groups_sent[c] += link == "group"
        waiting[c] = streams[c].send(result)
        for step in range(STEPS):
            if step not in passed and len(kept[step]) == CHUNKS:
                if step == 0:
                    passed[step] = send(jnp.concatenate(kept[0], axis=1), "group", 1)
                else:
                    whole = jnp.concatenate(kept[step], axis=1).astype(narrow)
                    passed[step] = send(whole, "group", 2**step)
    return results[0][None], results[1][None]


def solution(mesh):
    return jax.shard_map(
        shards,
        mesh=mesh,
        in_specs=(
            P("group", "fsdp", None),
            P("group", "fsdp", None),
            P("group", "fsdp", None),
            P("group", "fsdp", None),
            P("group"),
        ),
        out_specs=(P("group", "fsdp", None), P("group", "fsdp", None)),
        check_vma=False,
    )
```

profile of v0, /device:TPU:0, one launch (start us, length us, event | category | flops | bytes accessed | tf_op | source)
XLA Modules:
  0.0 195.8 jit_solution(3660505089620431370)
XLA Ops:
  0.7 2.8 %dynamic-slice_bitcast_fusion.7 = (bf16[384,512]{1,0:T(8,128)(2,1)S(1)}, bf16[384,512]{1,0:T(8,128)(2,1)S(1)}, bf16[384,512]{1,0:T(8,128)(2,1)S(1)}, bf16[384,51...) fusion(bf16[1,384,4096]{2,1,0:T(8,128)(2,1)} %param.5, ...), kind=kLoop, calls=%fused_computation.86 | loop fusion | bytes 6291488 | tf_op jit(solution)/shard_map/dynamic_slice | solution.py:76
  4.9 2.9 %collective-permute-start.1 = (bf16[384,2048]{1,0:T(8,128)(2,1)}, bf16[384,2048]{1,0:T(8,128)(2,1)}, u32[]{:S(2)}, u32[]{:S(2)}) collective-permute-start(bf16[384,2048]{1,0:T(8,128)(2,1)} %pad_maximum_fusion), channel_id=1, source_target_pairs={{0,1},{1,0},{2,3},{3,2},{4,5},{5,4},{6,7},{7,6},{8,9},{9,8},{10,11... | collective-permute-start | bytes 4718600 | tf_op jit(solution)/shard_map/ppermute | solution.py:64
  16.7 6.0 %all-reduce.2 = f32[4]{0:T(128)S(1)} all-reduce(f32[4]{0:T(128)S(1)} %dynamic-update-slice), channel_id=1, replica_groups=mesh['group'=4,'fsdp'=8] {'group'}, use_global_device_ids=true, to_apply=%add.2 | all-reduce | flops 4 | bytes 32
  30.9 3.4 %collective-permute-done.3 = bf16[512,128]{1,0:T(8,128)(2,1)S(1)} collective-permute-done((bf16[512,128]{1,0:T(8,128)(2,1)}, bf16[512,128]{1,0:T(8,128)(2,1)S(1)}, u32[]{:S(2)}, u32[]{:S(2)}) %collective-permute-start.3) | collective-permute-done | bytes 131104 | tf_op jit(solution)/shard_map/ppermute | solution.py:17
  34.3 2.8 %collective-permute-done.10 = bf16[512,128]{1,0:T(8,128)(2,1)S(1)} collective-permute-done((bf16[512,128]{1,0:T(8,128)(2,1)}, bf16[512,128]{1,0:T(8,128)(2,1)S(1)}, u32[]{:S(2)}, u32[]{:S(2)}) %collective-permute-start.10) | collective-permute-done | bytes 131104 | tf_op jit(solution)/shard_map/ppermute | solution.py:17
  37.1 2.7 %collective-permute-done.9 = bf16[512,128]{1,0:T(8,128)(2,1)S(1)} collective-permute-done((bf16[512,128]{1,0:T(8,128)(2,1)}, bf16[512,128]{1,0:T(8,128)(2,1)S(1)}, u32[]{:S(2)}, u32[]{:S(2)}) %collective-permute-start.9) | collective-permute-done | bytes 131104 | tf_op jit(solution)/shard_map/ppermute | solution.py:17
  39.9 2.2 %collective-permute-done.8 = bf16[512,128]{1,0:T(8,128)(2,1)S(1)} collective-permute-done((bf16[512,128]{1,0:T(8,128)(2,1)}, bf16[512,128]{1,0:T(8,128)(2,1)S(1)}, u32[]{:S(2)}, u32[]{:S(2)}) %collective-permute-start.8) | collective-permute-done | bytes 131104 | tf_op jit(solution)/shard_map/ppermute | solution.py:17
  62.2 4.1 %collective-permute-done.18 = bf16[768,128]{1,0:T(8,128)(2,1)S(1)} collective-permute-done((bf16[768,128]{1,0:T(8,128)(2,1)S(1)}, bf16[768,128]{1,0:T(8,128)(2,1)S(1)}, u32[]{:S(2)}, u32[]{:S(2)}) %collective-permute-start.18) | collective-permute-done | bytes 196640 | tf_op jit(solution)/shard_map/ppermute | solution.py:64
  73.2 2.8 %collective-permute-done.17 = bf16[512,128]{1,0:T(8,128)(2,1)S(1)} collective-permute-done((bf16[512,128]{1,0:T(8,128)(2,1)S(1)}, bf16[512,128]{1,0:T(8,128)(2,1)S(1)}, u32[]{:S(2)}, u32[]{:S(2)}) %collective-permute-start.17) | collective-permute-done | bytes 131104 | tf_op jit(solution)/shard_map/ppermute | solution.py:17
  76.5 2.3 %collective-permute-done.24 = bf16[512,128]{1,0:T(8,128)(2,1)S(1)} collective-permute-done((bf16[512,128]{1,0:T(8,128)(2,1)S(1)}, bf16[512,128]{1,0:T(8,128)(2,1)S(1)}, u32[]{:S(2)}, u32[]{:S(2)}) %collective-permute-start.24) | collective-permute-done | bytes 131104 | tf_op jit(solution)/shard_map/ppermute | solution.py:17
  79.3 2.3 %collective-permute-done.23 = bf16[512,128]{1,0:T(8,128)(2,1)S(1)} collective-permute-done((bf16[512,128]{1,0:T(8,128)(2,1)S(1)}, bf16[512,128]{1,0:T(8,128)(2,1)S(1)}, u32[]{:S(2)}, u32[]{:S(2)}) %collective-permute-start.23) | collective-permute-done | bytes 131104 | tf_op jit(solution)/shard_map/ppermute | solution.py:17
  82.1 2.3 %collective-permute-done.22 = bf16[512,128]{1,0:T(8,128)(2,1)S(1)} collective-permute-done((bf16[512,128]{1,0:T(8,128)(2,1)S(1)}, bf16[512,128]{1,0:T(8,128)(2,1)S(1)}, u32[]{:S(2)}, u32[]{:S(2)}) %collective-permute-start.22) | collective-permute-done | bytes 131104 | tf_op jit(solution)/shard_map/ppermute | solution.py:17
  85.1 2.1 %collective-permute-done.21 = bf16[512,128]{1,0:T(8,128)(2,1)S(1)} collective-permute-done((bf16[512,128]{1,0:T(8,128)(2,1)S(1)}, bf16[512,128]{1,0:T(8,128)(2,1)S(1)}, u32[]{:S(2)}, u32[]{:S(2)}) %collective-permute-start.21) | collective-permute-done | bytes 131104 | tf_op jit(solution)/shard_map/ppermute | solution.py:17
  87.7 2.3 %collective-permute-done.27 = bf16[512,128]{1,0:T(8,128)(2,1)S(1)} collective-permute-done((bf16[512,128]{1,0:T(8,128)(2,1)S(1)}, bf16[512,128]{1,0:T(8,128)(2,1)S(1)}, u32[]{:S(2)}, u32[]{:S(2)}) %collective-permute-start.27) | collective-permute-done | bytes 131104 | tf_op jit(solution)/shard_map/ppermute | solution.py:17
  94.5 2.8 %collective-permute-done.29 = bf16[512,128]{1,0:T(8,128)(2,1)S(1)} collective-permute-done((bf16[512,128]{1,0:T(8,128)(2,1)S(1)}, bf16[512,128]{1,0:T(8,128)(2,1)S(1)}, u32[]{:S(2)}, u32[]{:S(2)}) %collective-permute-start.29) | collective-permute-done | bytes 131104 | tf_op jit(solution)/shard_map/ppermute | solution.py:17
  98.6 3.5 %collective-permute-done.31 = bf16[512,128]{1,0:T(8,128)(2,1)S(1)} collective-permute-done((bf16[512,128]{1,0:T(8,128)(2,1)S(1)}, bf16[512,128]{1,0:T(8,128)(2,1)S(1)}, u32[]{:S(2)}, u32[]{:S(2)}) %collective-permute-start.31) | collective-permute-done | bytes 131104 | tf_op jit(solution)/shard_map/ppermute | solution.py:17
  103.2 3.0 %collective-permute-done.33 = bf16[512,128]{1,0:T(8,128)(2,1)S(1)} collective-permute-done((bf16[512,128]{1,0:T(8,128)(2,1)S(1)}, bf16[512,128]{1,0:T(8,128)(2,1)S(1)}, u32[]{:S(2)}, u32[]{:S(2)}) %collective-permute-start.33) | collective-permute-done | bytes 131104 | tf_op jit(solution)/shard_map/ppermute | solution.py:17
  106.1 2.8 %collective-permute-done.32 = bf16[512,128]{1,0:T(8,128)(2,1)S(1)} collective-permute-done((bf16[512,128]{1,0:T(8,128)(2,1)S(1)}, bf16[512,128]{1,0:T(8,128)(2,1)S(1)}, u32[]{:S(2)}, u32[]{:S(2)}) %collective-permute-start.32) | collective-permute-done | bytes 131104 | tf_op jit(solution)/shard_map/ppermute | solution.py:17
  110.8 3.0 %collective-permute-done.34 = bf16[512,128]{1,0:T(8,128)(2,1)S(1)} collective-permute-done((bf16[512,128]{1,0:T(8,128)(2,1)S(1)}, bf16[512,128]{1,0:T(8,128)(2,1)S(1)}, u32[]{:S(2)}, u32[]{:S(2)}) %collective-permute-start.34) | collective-permute-done | bytes 131104 | tf_op jit(solution)/shard_map/ppermute | solution.py:17
  116.6 2.1 %collective-permute-start.38 = (bf16[512,128]{1,0:T(8,128)(2,1)S(1)}, bf16[512,128]{1,0:T(8,128)(2,1)S(1)}, u32[]{:S(2)}, u32[]{:S(2)}) collective-permute-start(bf16[512,128]{1,0:T(8,128)(2,1)S(1)} %collective-permute-done.36), channel_id=1, source_target_pairs={{0,2},{1,3},{2,4},{3,5},{4,6},{5,7},{6,0},{7,1},{8,10},{9,11},{10,... | collective-permute-start | bytes 393224 | tf_op jit(solution)/shard_map/ppermute | solution.py:17
  118.7 2.8 %collective-permute-start.43 = (bf16[512,128]{1,0:T(8,128)(2,1)S(1)}, bf16[512,128]{1,0:T(8,128)(2,1)S(1)}, u32[]{:S(2)}, u32[]{:S(2)}) collective-permute-start(bf16[512,128]{1,0:T(8,128)(2,1)S(1)} %get-tuple-element.112), channel_id=1, source_target_pairs={{0,2},{1,3},{2,4},{3,5},{4,6},{5,7},{6,0},{7,1},{8,10},{9,11},{10,... | collective-permute-start | bytes 393224 | tf_op jit(solution)/shard_map/ppermute | solution.py:17
  122.3 2.5 %collective-permute-done.40 = bf16[512,128]{1,0:T(8,128)(2,1)S(1)} collective-permute-done((bf16[512,128]{1,0:T(8,128)(2,1)S(1)}, bf16[512,128]{1,0:T(8,128)(2,1)S(1)}, u32[]{:S(2)}, u32[]{:S(2)}) %collective-permute-start.40) | collective-permute-done | bytes 131104 | tf_op jit(solution)/shard_map/ppermute | solution.py:17
  124.8 2.8 %collective-permute-done.39 = bf16[512,128]{1,0:T(8,128)(2,1)S(1)} collective-permute-done((bf16[512,128]{1,0:T(8,128)(2,1)S(1)}, bf16[512,128]{1,0:T(8,128)(2,1)S(1)}, u32[]{:S(2)}, u32[]{:S(2)}) %collective-permute-start.39) | collective-permute-done | bytes 131104 | tf_op jit(solution)/shard_map/ppermute | solution.py:17
  127.6 2.8 %collective-permute-done.38 = bf16[512,128]{1,0:T(8,128)(2,1)S(1)} collective-permute-done((bf16[512,128]{1,0:T(8,128)(2,1)S(1)}, bf16[512,128]{1,0:T(8,128)(2,1)S(1)}, u32[]{:S(2)}, u32[]{:S(2)}) %collective-permute-start.38) | collective-permute-done | bytes 131104 | tf_op jit(solution)/shard_map/ppermute | solution.py:17
  136.1 2.3 %collective-permute-done.45 = bf16[512,128]{1,0:T(8,128)(2,1)S(1)} collective-permute-done((bf16[512,128]{1,0:T(8,128)(2,1)S(1)}, bf16[512,128]{1,0:T(8,128)(2,1)S(1)}, u32[]{:S(2)}, u32[]{:S(2)}) %collective-permute-start.45) | collective-permute-done | bytes 131104 | tf_op jit(solution)/shard_map/ppermute | solution.py:17
  146.5 2.8 %collective-permute-done.52 = bf16[512,128]{1,0:T(8,128)(2,1)S(1)} collective-permute-done((bf16[512,128]{1,0:T(8,128)(2,1)S(1)}, bf16[512,128]{1,0:T(8,128)(2,1)S(1)}, u32[]{:S(2)}, u32[]{:S(2)}) %collective-permute-start.52) | collective-permute-done | bytes 131104 | tf_op jit(solution)/shard_map/ppermute | solution.py:17
  153.9 2.8 %collective-permute-start.55 = (bf16[512,128]{1,0:T(8,128)(2,1)S(1)}, bf16[512,128]{1,0:T(8,128)(2,1)S(1)}, u32[]{:S(2)}, u32[]{:S(2)}) collective-permute-start(bf16[512,128]{1,0:T(8,128)(2,1)S(1)} %convolution_convert_fusion.1), channel_id=1, source_target_pairs={{0,2},{1,3},{2,4},{3,5},{4,6},{5,7},{6,0},{7,1},{8,10},{9,11},{10,... | collective-permute-start | bytes 393224 | tf_op jit(solution)/shard_map/ppermute | solution.py:17
  156.6 2.1 %collective-permute-done.50 = bf16[512,128]{1,0:T(8,128)(2,1)S(1)} collective-permute-done((bf16[512,128]{1,0:T(8,128)(2,1)S(1)}, bf16[512,128]{1,0:T(8,128)(2,1)S(1)}, u32[]{:S(2)}, u32[]{:S(2)}) %collective-permute-start.50) | collective-permute-done | bytes 131104 | tf_op jit(solution)/shard_map/ppermute | solution.py:17
  159.2 2.3 %collective-permute-done.49 = bf16[512,128]{1,0:T(8,128)(2,1)S(1)} collective-permute-done((bf16[512,128]{1,0:T(8,128)(2,1)S(1)}, bf16[512,128]{1,0:T(8,128)(2,1)S(1)}, u32[]{:S(2)}, u32[]{:S(2)}) %collective-permute-start.49) | collective-permute-done | bytes 131104 | tf_op jit(solution)/shard_map/ppermute | solution.py:17
  173.6 2.3 %collective-permute-done.59 = bf16[512,128]{1,0:T(8,128)(2,1)S(1)} collective-permute-done((bf16[512,128]{1,0:T(8,128)(2,1)S(1)}, bf16[512,128]{1,0:T(8,128)(2,1)S(1)}, u32[]{:S(2)}, u32[]{:S(2)}) %collective-permute-start.59) | collective-permute-done | bytes 131104 | tf_op jit(solution)/shard_map/ppermute | solution.py:17
  185.4 2.9 %collective-permute-done.65 = bf16[512,128]{1,0:T(8,128)(2,1)S(1)} collective-permute-done((bf16[512,128]{1,0:T(8,128)(2,1)S(1)}, bf16[512,128]{1,0:T(8,128)(2,1)S(1)}, u32[]{:S(2)}, u32[]{:S(2)}) %collective-permute-start.65) | collective-permute-done | bytes 131104 | tf_op jit(solution)/shard_map/ppermute | solution.py:17
  191.2 2.6 %collective-permute-done.66 = bf16[512,128]{1,0:T(8,128)(2,1)S(1)} collective-permute-done((bf16[512,128]{1,0:T(8,128)(2,1)S(1)}, bf16[512,128]{1,0:T(8,128)(2,1)S(1)}, u32[]{:S(2)}, u32[]{:S(2)}) %collective-permute-start.66) | collective-permute-done | bytes 131104 | tf_op jit(solution)/shard_map/ppermute | solution.py:17
  (210 shorter events, 104.2 us)
Async XLA Ops:
  4.9 37.7 %collective-permute-start.1 = (bf16[384,2048]{1,0:T(8,128)(2,1)}, bf16[384,2048]{1,0:T(8,128)(2,1)}, u32[]{:S(2)}, u32[]{:S(2)}) collective-permute-start(bf16[384,2048]{1,0:T(8,128)(2,1)} %pad_maximum_fusion), channel_id=1, source_target_pairs={{0,1},{1,0},{2,3},{3,2},{4,5},{5,4},{6,7},{7,6},{8,9},{9,8},{10,11... | collective-permute-start | bytes 4718600 | tf_op jit(solution)/shard_map/ppermute | solution.py:64
  9.4 16.4 %collective-permute-start.2 = (bf16[512,128]{1,0:T(8,128)(2,1)}, bf16[512,128]{1,0:T(8,128)(2,1)}, u32[]{:S(2)}, u32[]{:S(2)}) collective-permute-start(bf16[512,128]{1,0:T(8,128)(2,1)} %get-tuple-element.72), channel_id=1, source_target_pairs={{0,2},{1,3},{2,4},{3,5},{4,6},{5,7},{6,0},{7,1},{8,10},{9,11},{10,... | collective-permute-start | bytes 393224 | tf_op jit(solution)/shard_map/ppermute | solution.py:17
  12.0 15.5 %collective-permute-start.6 = (bf16[512,128]{1,0:T(8,128)(2,1)}, bf16[512,128]{1,0:T(8,128)(2,1)}, u32[]{:S(2)}, u32[]{:S(2)}) collective-permute-start(bf16[512,128]{1,0:T(8,128)(2,1)} %get-tuple-element.74), channel_id=1, source_target_pairs={{0,2},{1,3},{2,4},{3,5},{4,6},{5,7},{6,0},{7,1},{8,10},{9,11},{10,... | collective-permute-start | bytes 393224 | tf_op jit(solution)/shard_map/ppermute | solution.py:17
  13.6 15.5 %collective-permute-start.5 = (bf16[512,128]{1,0:T(8,128)(2,1)S(1)}, bf16[512,128]{1,0:T(8,128)(2,1)}, u32[]{:S(2)}, u32[]{:S(2)}) collective-permute-start(bf16[512,128]{1,0:T(8,128)(2,1)S(1)} %get-tuple-element.75), channel_id=1, source_target_pairs={{0,2},{1,3},{2,4},{3,5},{4,6},{5,7},{6,0},{7,1},{8,10},{9,11},{10,... | collective-permute-start | bytes 393224 | tf_op jit(solution)/shard_map/ppermute | solution.py:17
  16.5 14.1 %collective-permute-start.4 = (bf16[512,128]{1,0:T(8,128)(2,1)S(1)}, bf16[512,128]{1,0:T(8,128)(2,1)}, u32[]{:S(2)}, u32[]{:S(2)}) collective-permute-start(bf16[512,128]{1,0:T(8,128)(2,1)S(1)} %get-tuple-element.76), channel_id=1, source_target_pairs={{0,2},{1,3},{2,4},{3,5},{4,6},{5,7},{6,0},{7,1},{8,10},{9,11},{10,... | collective-permute-start | bytes 393224 | tf_op jit(solution)/shard_map/ppermute | solution.py:17
  27.5 9.7 %collective-permute-start.10 = (bf16[512,128]{1,0:T(8,128)(2,1)}, bf16[512,128]{1,0:T(8,128)(2,1)S(1)}, u32[]{:S(2)}, u32[]{:S(2)}) collective-permute-start(bf16[512,128]{1,0:T(8,128)(2,1)} %collective-permute-done.6), channel_id=1, source_target_pairs={{0,2},{1,3},{2,4},{3,5},{4,6},{5,7},{6,0},{7,1},{8,10},{9,11},{10,... | collective-permute-start | bytes 393224 | tf_op jit(solution)/shard_map/ppermute | solution.py:17
  29.0 10.8 %collective-permute-start.9 = (bf16[512,128]{1,0:T(8,128)(2,1)}, bf16[512,128]{1,0:T(8,128)(2,1)S(1)}, u32[]{:S(2)}, u32[]{:S(2)}) collective-permute-start(bf16[512,128]{1,0:T(8,128)(2,1)} %collective-permute-done.5), channel_id=1, source_target_pairs={{0,2},{1,3},{2,4},{3,5},{4,6},{5,7},{6,0},{7,1},{8,10},{9,11},{10,... | collective-permute-start | bytes 393224 | tf_op jit(solution)/shard_map/ppermute | solution.py:17
  30.6 11.5 %collective-permute-start.8 = (bf16[512,128]{1,0:T(8,128)(2,1)}, bf16[512,128]{1,0:T(8,128)(2,1)S(1)}, u32[]{:S(2)}, u32[]{:S(2)}) collective-permute-start(bf16[512,128]{1,0:T(8,128)(2,1)} %collective-permute-done.4), channel_id=1, source_target_pairs={{0,2},{1,3},{2,4},{3,5},{4,6},{5,7},{6,0},{7,1},{8,10},{9,11},{10,... | collective-permute-start | bytes 393224 | tf_op jit(solution)/shard_map/ppermute | solution.py:17
  34.3 59.4 %collective-permute-start = (f32[512,512]{1,0:T(8,128)S(1)}, f32[512,512]{1,0:T(8,128)S(1)}, u32[]{:S(2)}, u32[]{:S(2)}) collective-permute-start(f32[512,512]{1,0:T(8,128)S(1)} %copy-done.4), channel_id=1, source_target_pairs={{0,8},{8,16},{16,24},{24,0},{1,9},{9,17},{17,25},{25,1},{2,10},{10... | collective-permute-start | bytes 3145736 | tf_op jit(solution)/shard_map/ppermute | solution.py:17
  42.1 9.9 %collective-permute-start.13 = (bf16[512,128]{1,0:T(8,128)(2,1)S(1)}, bf16[512,128]{1,0:T(8,128)(2,1)S(1)}, u32[]{:S(2)}, u32[]{:S(2)}) collective-permute-start(bf16[512,128]{1,0:T(8,128)(2,1)S(1)} %collective-permute-done.9), channel_id=1, source_target_pairs={{0,2},{1,3},{2,4},{3,5},{4,6},{5,7},{6,0},{7,1},{8,10},{9,11},{10,... | collective-permute-start | bytes 393224 | tf_op jit(solution)/shard_map/ppermute | solution.py:17
  42.5 12.9 %collective-permute-start.12 = (bf16[512,128]{1,0:T(8,128)(2,1)S(1)}, bf16[512,128]{1,0:T(8,128)(2,1)S(1)}, u32[]{:S(2)}, u32[]{:S(2)}) collective-permute-start(bf16[512,128]{1,0:T(8,128)(2,1)S(1)} %collective-permute-done.8), channel_id=1, source_target_pairs={{0,2},{1,3},{2,4},{3,5},{4,6},{5,7},{6,0},{7,1},{8,10},{9,11},{10,... | collective-permute-start | bytes 393224 | tf_op jit(solution)/shard_map/ppermute | solution.py:17
  47.9 10.0 %collective-permute-start.11 = (bf16[768,128]{1,0:T(8,128)(2,1)S(1)}, bf16[768,128]{1,0:T(8,128)(2,1)S(1)}, u32[]{:S(2)}, u32[]{:S(2)}) collective-permute-start(bf16[768,128]{1,0:T(8,128)(2,1)S(1)} %get-tuple-element.85), channel_id=1, source_target_pairs={{0,1},{1,0},{2,3},{3,2},{4,5},{5,4},{6,7},{7,6},{8,9},{9,8},{10,11... | collective-permute-start | bytes 589832 | tf_op jit(solution)/shard_map/ppermute | solution.py:64
  53.9 12.9 %collective-permute-start.20 = (bf16[768,128]{1,0:T(8,128)(2,1)S(1)}, bf16[768,128]{1,0:T(8,128)(2,1)S(1)}, u32[]{:S(2)}, u32[]{:S(2)}) collective-permute-start(bf16[768,128]{1,0:T(8,128)(2,1)S(1)} %get-tuple-element.87), channel_id=1, source_target_pairs={{0,1},{1,0},{2,3},{3,2},{4,5},{5,4},{6,7},{7,6},{8,9},{9,8},{10,11... | collective-permute-start | bytes 589832 | tf_op jit(solution)/shard_map/ppermute | solution.py:64
  60.6 10.4 %collective-permute-start.19 = (bf16[512,128]{1,0:T(8,128)(2,1)S(1)}, bf16[512,128]{1,0:T(8,128)(2,1)S(1)}, u32[]{:S(2)}, u32[]{:S(2)}) collective-permute-start(bf16[512,128]{1,0:T(8,128)(2,1)S(1)} %convolution_convert_fusion.6), channel_id=1, source_target_pairs={{0,2},{1,3},{2,4},{3,5},{4,6},{5,7},{6,0},{7,1},{8,10},{9,11},{10,... | collective-permute-start | bytes 393224 | tf_op jit(solution)/shard_map/ppermute | solution.py:17
  71.3 10.3 %collective-permute-start.23 = (bf16[512,128]{1,0:T(8,128)(2,1)S(1)}, bf16[512,128]{1,0:T(8,128)(2,1)S(1)}, u32[]{:S(2)}, u32[]{:S(2)}) collective-permute-start(bf16[512,128]{1,0:T(8,128)(2,1)S(1)} %add_convert_fusion.13), channel_id=1, source_target_pairs={{0,2},{1,3},{2,4},{3,5},{4,6},{5,7},{6,0},{7,1},{8,10},{9,11},{10,... | collective-permute-start | bytes 393224 | tf_op jit(solution)/shard_map/ppermute | solution.py:17
  71.5 12.9 %collective-permute-start.22 = (bf16[512,128]{1,0:T(8,128)(2,1)S(1)}, bf16[512,128]{1,0:T(8,128)(2,1)S(1)}, u32[]{:S(2)}, u32[]{:S(2)}) collective-permute-start(bf16[512,128]{1,0:T(8,128)(2,1)S(1)} %convolution_convert_fusion.5), channel_id=1, source_target_pairs={{0,2},{1,3},{2,4},{3,5},{4,6},{5,7},{6,0},{7,1},{8,10},{9,11},{10,... | collective-permute-start | bytes 393224 | tf_op jit(solution)/shard_map/ppermute | solution.py:17
  76.4 10.8 %collective-permute-start.21 = (bf16[512,128]{1,0:T(8,128)(2,1)S(1)}, bf16[512,128]{1,0:T(8,128)(2,1)S(1)}, u32[]{:S(2)}, u32[]{:S(2)}) collective-permute-start(bf16[512,128]{1,0:T(8,128)(2,1)S(1)} %add_convert_fusion.14), channel_id=1, source_target_pairs={{0,2},{1,3},{2,4},{3,5},{4,6},{5,7},{6,0},{7,1},{8,10},{9,11},{10,... | collective-permute-start | bytes 393224 | tf_op jit(solution)/shard_map/ppermute | solution.py:17
  79.2 10.8 %collective-permute-start.27 = (bf16[512,128]{1,0:T(8,128)(2,1)S(1)}, bf16[512,128]{1,0:T(8,128)(2,1)S(1)}, u32[]{:S(2)}, u32[]{:S(2)}) collective-permute-start(bf16[512,128]{1,0:T(8,128)(2,1)S(1)} %add_convert_fusion.10), channel_id=1, source_target_pairs={{0,2},{1,3},{2,4},{3,5},{4,6},{5,7},{6,0},{7,1},{8,10},{9,11},{10,... | collective-permute-start | bytes 393224 | tf_op jit(solution)/shard_map/ppermute | solution.py:17
  82.0 9.8 %collective-permute-start.26 = (bf16[512,128]{1,0:T(8,128)(2,1)S(1)}, bf16[512,128]{1,0:T(8,128)(2,1)S(1)}, u32[]{:S(2)}, u32[]{:S(2)}) collective-permute-start(bf16[512,128]{1,0:T(8,128)(2,1)S(1)} %add_convert_fusion.11), channel_id=1, source_target_pairs={{0,2},{1,3},{2,4},{3,5},{4,6},{5,7},{6,0},{7,1},{8,10},{9,11},{10,... | collective-permute-start | bytes 393224 | tf_op jit(solution)/shard_map/ppermute | solution.py:17
  98.4 10.5 %collective-permute-start.32 = (bf16[512,128]{1,0:T(8,128)(2,1)S(1)}, bf16[512,128]{1,0:T(8,128)(2,1)S(1)}, u32[]{:S(2)}, u32[]{:S(2)}) collective-permute-start(bf16[512,128]{1,0:T(8,128)(2,1)S(1)} %add_convert_fusion.8), channel_id=1, source_target_pairs={{0,2},{1,3},{2,4},{3,5},{4,6},{5,7},{6,0},{7,1},{8,10},{9,11},{10,... | collective-permute-start | bytes 393224 | tf_op jit(solution)/shard_map/ppermute | solution.py:17
  103.1 13.5 %collective-permute-start.37 = (bf16[512,128]{1,0:T(8,128)(2,1)S(1)}, bf16[512,128]{1,0:T(8,128)(2,1)S(1)}, u32[]{:S(2)}, u32[]{:S(2)}) collective-permute-start(bf16[512,128]{1,0:T(8,128)(2,1)S(1)} %get-tuple-element.105), channel_id=1, source_target_pairs={{0,2},{1,3},{2,4},{3,5},{4,6},{5,7},{6,0},{7,1},{8,10},{9,11},{10,... | collective-permute-start | bytes 393224 | tf_op jit(solution)/shard_map/ppermute | solution.py:17
  106.1 10.5 %collective-permute-start.36 = (bf16[512,128]{1,0:T(8,128)(2,1)S(1)}, bf16[512,128]{1,0:T(8,128)(2,1)S(1)}, u32[]{:S(2)}, u32[]{:S(2)}) collective-permute-start(bf16[512,128]{1,0:T(8,128)(2,1)S(1)} %collective-permute-done.33), channel_id=1, source_target_pairs={{0,2},{1,3},{2,4},{3,5},{4,6},{5,7},{6,0},{7,1},{8,10},{9,11},{10,... | collective-permute-start | bytes 393224 | tf_op jit(solution)/shard_map/ppermute | solution.py:17
  114.7 61.7 %collective-permute-start.35 = (bf16[512,512]{1,0:T(8,128)(2,1)S(1)}, bf16[512,512]{1,0:T(8,128)(2,1)S(1)}, u32[]{:S(2)}, u32[]{:S(2)}) collective-permute-start(bf16[512,512]{1,0:T(8,128)(2,1)S(1)} %pad_maximum_fusion.2), channel_id=1, source_target_pairs={{0,16},{8,24},{16,0},{24,8},{1,17},{9,25},{17,1},{25,9},{2,18},{10... | collective-permute-start | bytes 1572872 | tf_op jit(solution)/shard_map/ppermute | solution.py:17
  116.6 11.0 %collective-permute-start.39 = (bf16[512,128]{1,0:T(8,128)(2,1)S(1)}, bf16[512,128]{1,0:T(8,128)(2,1)S(1)}, u32[]{:S(2)}, u32[]{:S(2)}) collective-permute-start(bf16[512,128]{1,0:T(8,128)(2,1)S(1)} %collective-permute-done.37), channel_id=1, source_target_pairs={{0,2},{1,3},{2,4},{3,5},{4,6},{5,7},{6,0},{7,1},{8,10},{9,11},{10,... | collective-permute-start | bytes 393224 | tf_op jit(solution)/shard_map/ppermute | solution.py:17
  116.6 13.8 %collective-permute-start.38 = (bf16[512,128]{1,0:T(8,128)(2,1)S(1)}, bf16[512,128]{1,0:T(8,128)(2,1)S(1)}, u32[]{:S(2)}, u32[]{:S(2)}) collective-permute-start(bf16[512,128]{1,0:T(8,128)(2,1)S(1)} %collective-permute-done.36), channel_id=1, source_target_pairs={{0,2},{1,3},{2,4},{3,5},{4,6},{5,7},{6,0},{7,1},{8,10},{9,11},{10,... | collective-permute-start | bytes 393224 | tf_op jit(solution)/shard_map/ppermute | solution.py:17
  118.7 14.5 %collective-permute-start.43 = (bf16[512,128]{1,0:T(8,128)(2,1)S(1)}, bf16[512,128]{1,0:T(8,128)(2,1)S(1)}, u32[]{:S(2)}, u32[]{:S(2)}) collective-permute-start(bf16[512,128]{1,0:T(8,128)(2,1)S(1)} %get-tuple-element.112), channel_id=1, source_target_pairs={{0,2},{1,3},{2,4},{3,5},{4,6},{5,7},{6,0},{7,1},{8,10},{9,11},{10,... | collective-permute-start | bytes 393224 | tf_op jit(solution)/shard_map/ppermute | solution.py:17
  124.8 11.2 %collective-permute-start.42 = (bf16[512,128]{1,0:T(8,128)(2,1)S(1)}, bf16[512,128]{1,0:T(8,128)(2,1)S(1)}, u32[]{:S(2)}, u32[]{:S(2)}) collective-permute-start(bf16[512,128]{1,0:T(8,128)(2,1)S(1)} %collective-permute-done.40), channel_id=1, source_target_pairs={{0,2},{1,3},{2,4},{3,5},{4,6},{5,7},{6,0},{7,1},{8,10},{9,11},{10,... | collective-permute-start | bytes 393224 | tf_op jit(solution)/shard_map/ppermute | solution.py:17
  127.6 10.7 %collective-permute-start.45 = (bf16[512,128]{1,0:T(8,128)(2,1)S(1)}, bf16[512,128]{1,0:T(8,128)(2,1)S(1)}, u32[]{:S(2)}, u32[]{:S(2)}) collective-permute-start(bf16[512,128]{1,0:T(8,128)(2,1)S(1)} %collective-permute-done.39), channel_id=1, source_target_pairs={{0,2},{1,3},{2,4},{3,5},{4,6},{5,7},{6,0},{7,1},{8,10},{9,11},{10,... | collective-permute-start | bytes 393224 | tf_op jit(solution)/shard_map/ppermute | solution.py:17
  151.0 10.6 %collective-permute-start.49 = (bf16[512,128]{1,0:T(8,128)(2,1)S(1)}, bf16[512,128]{1,0:T(8,128)(2,1)S(1)}, u32[]{:S(2)}, u32[]{:S(2)}) collective-permute-start(bf16[512,128]{1,0:T(8,128)(2,1)S(1)} %add_convert_fusion.7), channel_id=1, source_target_pairs={{0,2},{1,3},{2,4},{3,5},{4,6},{5,7},{6,0},{7,1},{8,10},{9,11},{10,... | collective-permute-start | bytes 393224 | tf_op jit(solution)/shard_map/ppermute | solution.py:17
  153.9 10.5 %collective-permute-start.55 = (bf16[512,128]{1,0:T(8,128)(2,1)S(1)}, bf16[512,128]{1,0:T(8,128)(2,1)S(1)}, u32[]{:S(2)}, u32[]{:S(2)}) collective-permute-start(bf16[512,128]{1,0:T(8,128)(2,1)S(1)} %convolution_convert_fusion.1), channel_id=1, source_target_pairs={{0,2},{1,3},{2,4},{3,5},{4,6},{5,7},{6,0},{7,1},{8,10},{9,11},{10,... | collective-permute-start | bytes 393224 | tf_op jit(solution)/shard_map/ppermute | solution.py:17
  162.6 10.5 %collective-permute-start.60 = (bf16[512,128]{1,0:T(8,128)(2,1)S(1)}, bf16[512,128]{1,0:T(8,128)(2,1)S(1)}, u32[]{:S(2)}, u32[]{:S(2)}) collective-permute-start(bf16[512,128]{1,0:T(8,128)(2,1)S(1)} %convolution_convert_fusion), channel_id=1, source_target_pairs={{0,2},{1,3},{2,4},{3,5},{4,6},{5,7},{6,0},{7,1},{8,10},{9,11},{10,... | collective-permute-start | bytes 393224 | tf_op jit(solution)/shard_map/ppermute | solution.py:17
  164.8 11.1 %collective-permute-start.59 = (bf16[512,128]{1,0:T(8,128)(2,1)S(1)}, bf16[512,128]{1,0:T(8,128)(2,1)S(1)}, u32[]{:S(2)}, u32[]{:S(2)}) collective-permute-start(bf16[512,128]{1,0:T(8,128)(2,1)S(1)} %add_convert_fusion.3), channel_id=1, source_target_pairs={{0,2},{1,3},{2,4},{3,5},{4,6},{5,7},{6,0},{7,1},{8,10},{9,11},{10,... | collective-permute-start | bytes 393224 | tf_op jit(solution)/shard_map/ppermute | solution.py:17
  (43 other events, 304.9 us)
where the time goes:
time: 196 us
  waiting for transfers between devices  86 us (44%)
  starting transfers between devices  54.3 us (28%)
  matrix products  26.9 us (14%)
  other arithmetic  10.5 us (5%)
  local copies, waits for them, and re-layouts  10 us (5%)
  blocking collectives  6.03 us (3%)
  between operations  2.1 us (1%)
    ppermute x58, waiting for transfers between devices, from_behind(): return lax.ppermute(value, axis, pairs)  81.9 us
    ppermute x58, starting transfers between devices, from_behind(): return lax.ppermute(value, axis, pairs)  41.9 us
    dot_general x32, matrix products, partial(): lax.dot_general(column_block(back), grad_out, contract, preferred_element...  13.3 us
    ppermute x9, starting transfers between devices, send(): return lax.ppermute(value, 'fsdp', [(i, i ^ 1) for i in range(count)])  12.4 us
    dot_general x4, matrix products, stream(): jnp.dot(pair_tokens, jnp.concatenate(pieces, axis=0), preferred_element_t...  7.66 us
    unnamed x1, blocking collectives  6.03 us
    dot_general x16, matrix products, stream(): jnp.dot(column_block(back), piece, preferred_element_type=wide)  5.94 us
    ppermute x9, waiting for transfers between devices, send(): return lax.ppermute(value, 'fsdp', [(i, i ^ 1) for i in range(count)])  4.1 us
  transfers between devices with their start and end apart: 67, of which 39 were waited for; matrix products, arithmetic and copies ran while one was open for 21% of the time, Pallas kernels for 0%

commit v1 on v0

v1 whole, which is shorter than its diff:
```python
import jax
import jax.numpy as jnp
from jax import lax
from jax.sharding import PartitionSpec as P

STEPS = 2
CHUNKS = 4
OCCUPANCY = {"gather": 2.75, "scatter": 2.75, "pair": 3.95, "group": 2.0}
PREPARE = {"gather": 0.8, "scatter": 1.2, "pair": 1.6, "group": 1.0}
LATENCY = 3.2


def from_behind(value, axis, steps):
    count = lax.axis_size(axis)
    pairs = [(source, (source + steps) % count) for source in range(count)]
    return lax.ppermute(value, axis, pairs)


def after(value, *earlier):
    return lax.optimization_barrier((value, *earlier))[0]


def issue_order(half):
    hops = half - 1
    plan = (["pair"] + ["scatter"] * hops + ["group"] + ["gather"] * hops) * STEPS
    plan = plan[: len(plan) - hops]
    free = dict.fromkeys(["line", "pair", "group", "core"], 0.0)
    ready = [2.0 * (c // 2) + 0.01 * c for c in range(CHUNKS)]
    at = [0] * CHUNKS
    order = []

    def due(c):
        idle = free["pair"] - OCCUPANCY["pair"] * (len(order) == 1)
        return max(ready[c], idle) if plan[at[c]] == "pair" else ready[c]

    while len(order) < CHUNKS * len(plan):
        c = min((c for c in range(CHUNKS) if at[c] < len(plan)), key=due)
        kind = plan[at[c]]
        link = kind if kind in free else "line"
        free["core"] = max(due(c), free["core"]) + PREPARE[kind]
        start = max(free["core"], free[link])
        free[link] = start + OCCUPANCY[kind]
        ready[c] = free[link] + LATENCY
        at[c] += 1
        order.append(c)
    return order


def shards(tokens, targets, params, momentum, push_weight):
    inputs = tokens[0]
    rows, width = inputs.shape
    features = params.shape[2]
    count = lax.axis_size("fsdp")
    half = count // 2
    block = width // count
    place = lax.div(lax.axis_index("fsdp"), 2)
    lane = lax.rem(lax.axis_index("fsdp"), 2)
    key_scale = width ** (-0.5)
    part = features // CHUNKS
    contract = (((0,), (0,)), ((), ()))
    wide = jnp.float32
    narrow = jnp.bfloat16
    issued = []

    def send(value, link, steps=1):
        if issued:
            value = after(value, issued[-1])
        issued.append(value)
        if link == "pair":
            return lax.ppermute(value, "fsdp", [(i, i ^ 1) for i in range(count)])
        if link == "line":
            return from_behind(value, "fsdp", 2)
        return from_behind(value, "group", steps)

    def chunk(array, c):
        return array[:, c * part : (c + 1) * part]

    def half_columns(source, side):
        pieces = []
        for back in range(half):
            start = (2 * lax.rem(place - back + half, half) + side) * block
            pieces.append(lax.dynamic_slice_in_dim(source, start, block, 1))
        return jnp.concatenate(pieces, axis=1)

    def column_block(back):
        return pair_tokens[:, back * block : (back + 1) * block]

    outgoing = half_columns(inputs, 1 - lane)
    theirs = send(outgoing, "pair")
    params = after(params, outgoing)
    momentum = after(momentum, outgoing)
    zero = jnp.zeros((), lane.dtype)
    pair_tokens = jnp.zeros((2 * rows, width // 2), inputs.dtype)
    pair_tokens = lax.dynamic_update_slice(
        pair_tokens, half_columns(after(inputs, outgoing), lane), (lane * rows, zero)
    )
    pair_tokens = lax.dynamic_update_slice(pair_tokens, theirs, ((1 - lane) * rows, zero))
    pair_targets = lax.dynamic_update_slice(
        jnp.zeros((2 * rows, features), targets.dtype), targets[0], (lane * rows, zero)
    )
    held = params.shape[1]
    results = [jnp.zeros_like(params[0]), jnp.zeros_like(momentum[0])]
    weights = [push_weight]
    kept, passed = [], []

    def debias(state, weight):
        return (state / weight[0]).astype(narrow)

    def exchange_kept(whole, step):
        kept.append(whole)
        if step == 0:
            extra = jnp.broadcast_to(weights[0], (8, features))
        else:
            left = weights[step]
            parts = []
            for _ in range(3):
                parts.append(lax.reduce_precision(left, 8, 7))
                left = left - parts[-1]
            row = lax.broadcasted_iota(jnp.int32, (16, features), 0)
            extra = jnp.where(row == 0, parts[0], jnp.where(row == 1, parts[1], parts[2]))
            whole, extra = whole.astype(narrow), extra.astype(narrow)
        got = send(jnp.concatenate([whole, extra], axis=0), "group", 2**step).astype(wide)
        passed.append(got[:held])
        came = got[held, :1] if step == 0 else jnp.sum(got[held : held + 3, :1], axis=0)
        weights.append(0.5 * weights[step] + 0.5 * came)

    first = [[debias(chunk(params[0], c), push_weight)] for c in range(CHUNKS)]
    for back in range(1, half):
        for c in range(CHUNKS):
            first[c].append(send(first[c][-1], "line"))
        if back == 1:
            exchange_kept(params[0] - (0.2 * 0.9) * momentum[0], 0)
    first_keys = []
    for c in range(0, CHUNKS, 2):
        both = [jnp.concatenate(first[i], axis=0) for i in (c, c + 1)]
        both = after(jnp.concatenate(both, axis=1), *first[c + 1][-1:])
        both = jnp.dot(pair_tokens, both, preferred_element_type=wide)
        first_keys += [both[:, :part], both[:, part:]]

    later = []

    def stream(c):
        moment = chunk(momentum[0], c)
        target = chunk(pair_targets, c).astype(wide)
        keys = first_keys[c]
        for step in range(STEPS):
            residual = key_scale * keys - target
            received = yield residual.astype(narrow), "pair"
            grad_out = (key_scale * (residual + received.astype(wide))).astype(narrow)

            def partial(back):
                return lax.dot_general(
                    column_block(back), grad_out, contract, preferred_element_type=wide
                )

            total = partial(1)
            for back in range(2, half + 1):
                arrived = yield total.astype(narrow), "line"
                total = arrived.astype(wide) + partial(back % half)
            behind = yield total.astype(narrow), "group"
            moment = 0.9 * moment + total
            mixed = 0.5 * (chunk(kept[step], c) + chunk(passed[step], c))
            state = mixed - 0.1 * (total + behind.astype(wide))
            if step == STEPS - 1:
                break
            later.append(state - (0.2 * 0.9) * moment)
            pieces = [debias(state, weights[step + 1])]
            for _ in range(half - 1):
                pieces.append((yield pieces[-1], "line"))
            keys = sum(
                jnp.dot(column_block(back), piece, preferred_element_type=wide)
                for back, piece in enumerate(pieces)
            )
        fresh = [state / weights[STEPS][0], moment]
        for i in range(2):
            results[i] = lax.dynamic_update_slice(results[i], fresh[i], (0, c * part))
        yield None, None

    streams = [stream(c) for c in range(CHUNKS)]
    came = [None] * CHUNKS
    mixings = [0] * CHUNKS
    for c in issue_order(half):
        came[c] = came[c] if came[c] is None else after(came[c], issued[-1])
        value, link = streams[c].send(came[c])
        came[c] = send(value, link, 2 ** mixings[c])
        mixings[c] += link == "group"
        if len(later) == CHUNKS:
            exchange_kept(jnp.concatenate(later, axis=1), mixings[c])
            later.clear()
    for c in range(CHUNKS):
        streams[c].send(came[c])
    return results[0][None], results[1][None]


def solution(mesh):
    return jax.shard_map(
        shards,
        mesh=mesh,
        in_specs=(
            P("group", "fsdp", None),
            P("group", "fsdp", None),
            P("group", "fsdp", None),
            P("group", "fsdp", None),
            P("group"),
        ),
        out_specs=(P("group", "fsdp", None), P("group", "fsdp", None)),
        check_vma=False,
    )
```

time: 196 us -> 198 us (1.010)
  other arithmetic: 10.5 us -> 22.2 us
  starting transfers between devices: 54.3 us -> 47.5 us
  waiting for transfers between devices: 86 us -> 79.8 us
  blocking collectives: 6.03 us -> 0 us
  between operations: 2.1 us -> 6.36 us
  matrix products: 26.9 us -> 29.7 us
    ppermute x58, waiting for transfers between devices: 81.9 us -> 74.4 us  [from_behind(): return lax.ppermute(value, axis, pairs)]
    unnamed x1 -> x0, blocking collectives: 6.03 us -> none
    dot_general x4 -> x2, matrix products: 7.66 us -> 1.98 us  [shards(): both = jnp.dot(pair_tokens, both, preferred_element_type=wide)]
    another operation x3 -> x4, other arithmetic: 0.47 us -> 6.1 us
    dot_general x16, matrix products: 5.94 us -> 10.3 us  [stream(): jnp.dot(column_block(back), piece, preferred_element_type=wide)]
    dot_general x32, matrix products: 13.3 us -> 17.4 us  [partial(): lax.dot_general(column_block(back), grad_out, contract, preferred_element...]
    ppermute x58, starting transfers between devices: 41.9 us -> 37.8 us  [from_behind(): return lax.ppermute(value, axis, pairs)]
    convert_element_type x8 -> x7, other arithmetic: 0.47 us -> 4.23 us  [stream(): grad_out = (key_scale * (residual + received.astype(wide))).astype(narrow)]
  transfers between devices with their start and end apart: 67 -> 67, of which waited for: 39 -> 37; matrix products, arithmetic and copies ran while one was open for 21% -> 28% of each run, Pallas kernels for 0% -> 0%
where the time goes in v1:
time: 198 us; the launch traced here: 197 us
  waiting for transfers between devices  79.8 us (40%)
  starting transfers between devices  47.5 us (24%)
  matrix products  29.7 us (15%)
  other arithmetic  22.2 us (11%)
  local copies, waits for them, and re-layouts  11.9 us (6%)
  between operations  6.36 us (3%)
    ppermute x58, waiting for transfers between devices, from_behind(): return lax.ppermute(value, axis, pairs)  74.4 us
    ppermute x58, starting transfers between devices, from_behind(): return lax.ppermute(value, axis, pairs)  37.8 us
    dot_general x32, matrix products, partial(): lax.dot_general(column_block(back), grad_out, contract, preferred_element...  17.4 us
    dot_general x16, matrix products, stream(): jnp.dot(column_block(back), piece, preferred_element_type=wide)  10.3 us
    ppermute x9, starting transfers between devices, send(): return lax.ppermute(value, 'fsdp', [(i, i ^ 1) for i in range(count)])  9.73 us
    another operation x4, other arithmetic  6.1 us
    ppermute x9, waiting for transfers between devices, send(): return lax.ppermute(value, 'fsdp', [(i, i ^ 1) for i in range(count)])  5.4 us
    convert_element_type x7, other arithmetic, stream(): grad_out = (key_scale * (residual + received.astype(wide))).astype(narrow)  4.23 us
  transfers between devices with their start and end apart: 67, of which 37 were waited for; matrix products, arithmetic and copies ran while one was open for 28% of the time, Pallas kernels for 0%

profile of v1, /device:TPU:0, one launch (start us, length us, event | category | flops | bytes accessed | tf_op | source)
XLA Modules:
  0.0 197.5 jit_solution(8899049277287464848)
XLA Ops:
  3.6 2.9 %collective-permute-start.1 = (bf16[384,2048]{1,0:T(8,128)(2,1)}, bf16[384,2048]{1,0:T(8,128)(2,1)}, u32[]{:S(2)}, u32[]{:S(2)}) collective-permute-start(bf16[384,2048]{1,0:T(8,128)(2,1)} %pad_maximum_fusion), channel_id=1, source_target_pairs={{0,1},{1,0},{2,3},{3,2},{4,5},{5,4},{6,7},{7,6},{8,9},{9,8},{10,11... | collective-permute-start | bytes 4718600 | tf_op jit(solution)/shard_map/ppermute | solution.py:70
  14.4 1.9 collective-permute-done.2
  19.1 2.8 %collective-permute-done.5 = bf16[512,128]{1,0:T(8,128)(2,1)} collective-permute-done((bf16[512,128]{1,0:T(8,128)(2,1)S(1)}, bf16[512,128]{1,0:T(8,128)(2,1)}, u32[]{:S(2)}, u32[]{:S(2)}) %collective-permute-start.5) | collective-permute-done | bytes 131104 | tf_op jit(solution)/shard_map/ppermute | solution.py:16
  21.9 2.8 %collective-permute-done.4 = bf16[512,128]{1,0:T(8,128)(2,1)} collective-permute-done((bf16[512,128]{1,0:T(8,128)(2,1)}, bf16[512,128]{1,0:T(8,128)(2,1)}, u32[]{:S(2)}, u32[]{:S(2)}) %collective-permute-start.4) | collective-permute-done | bytes 131104 | tf_op jit(solution)/shard_map/ppermute | solution.py:16
  24.7 1.9 collective-permute-done.3
  27.9 2.6 %collective-permute-done.8 = bf16[512,128]{1,0:T(8,128)(2,1)} collective-permute-done((bf16[512,128]{1,0:T(8,128)(2,1)}, bf16[512,128]{1,0:T(8,128)(2,1)}, u32[]{:S(2)}, u32[]{:S(2)}) %collective-permute-start.8) | collective-permute-done | bytes 131104 | tf_op jit(solution)/shard_map/ppermute | solution.py:16
  30.4 2.7 %collective-permute-done.11 = bf16[512,128]{1,0:T(8,128)(2,1)} collective-permute-done((bf16[512,128]{1,0:T(8,128)(2,1)}, bf16[512,128]{1,0:T(8,128)(2,1)}, u32[]{:S(2)}, u32[]{:S(2)}) %collective-permute-start.11) | collective-permute-done | bytes 131104 | tf_op jit(solution)/shard_map/ppermute | solution.py:16
  36.6 2.1 %collective-permute-start.9 = (bf16[512,128]{1,0:T(8,128)(2,1)}, bf16[512,128]{1,0:T(8,128)(2,1)S(1)}, u32[]{:S(2)}, u32[]{:S(2)}) collective-permute-start(bf16[512,128]{1,0:T(8,128)(2,1)} %collective-permute-done.8), channel_id=1, source_target_pairs={{0,2},{1,3},{2,4},{3,5},{4,6},{5,7},{6,0},{7,1},{8,10},{9,11},{10,... | collective-permute-start | bytes 393224 | tf_op jit(solution)/shard_map/ppermute | solution.py:16
  38.7 4.7 %collective-permute-done.15 = bf16[512,128]{1,0:T(8,128)(2,1)} collective-permute-done((bf16[512,128]{1,0:T(8,128)(2,1)}, bf16[512,128]{1,0:T(8,128)(2,1)}, u32[]{:S(2)}, u32[]{:S(2)}) %collective-permute-start.15) | collective-permute-done | bytes 131104 | tf_op jit(solution)/shard_map/ppermute | solution.py:16
  45.0 5.4 %collective-permute-done.7 = bf16[512,128]{1,0:T(8,128)(2,1)S(1)} collective-permute-done((bf16[512,128]{1,0:T(8,128)(2,1)}, bf16[512,128]{1,0:T(8,128)(2,1)S(1)}, u32[]{:S(2)}, u32[]{:S(2)}) %collective-permute-start.7) | collective-permute-done | bytes 131104 | tf_op jit(solution)/shard_map/ppermute | solution.py:16
  65.1 3.8 %collective-permute-done.12 = bf16[768,128]{1,0:T(8,128)(2,1)S(1)} collective-permute-done((bf16[768,128]{1,0:T(8,128)(2,1)S(1)}, bf16[768,128]{1,0:T(8,128)(2,1)S(1)}, u32[]{:S(2)}, u32[]{:S(2)}) %collective-permute-start.12) | collective-permute-done | bytes 196640 | tf_op jit(solution)/shard_map/ppermute | solution.py:70
  75.4 2.7 %collective-permute-done.13 = bf16[512,128]{1,0:T(8,128)(2,1)S(1)} collective-permute-done((bf16[512,128]{1,0:T(8,128)(2,1)S(1)}, bf16[512,128]{1,0:T(8,128)(2,1)S(1)}, u32[]{:S(2)}, u32[]{:S(2)}) %collective-permute-start.13) | collective-permute-done | bytes 131104 | tf_op jit(solution)/shard_map/ppermute | solution.py:16
  83.3 3.5 %collective-permute-done.17 = bf16[512,128]{1,0:T(8,128)(2,1)S(1)} collective-permute-done((bf16[512,128]{1,0:T(8,128)(2,1)S(1)}, bf16[512,128]{1,0:T(8,128)(2,1)S(1)}, u32[]{:S(2)}, u32[]{:S(2)}) %collective-permute-start.17) | collective-permute-done | bytes 131104 | tf_op jit(solution)/shard_map/ppermute | solution.py:16
  91.9 2.8 %collective-permute-start.27 = (bf16[512,128]{1,0:T(8,128)(2,1)S(1)}, bf16[512,128]{1,0:T(8,128)(2,1)S(1)}, u32[]{:S(2)}, u32[]{:S(2)}) collective-permute-start(bf16[512,128]{1,0:T(8,128)(2,1)S(1)} %add_convert_fusion.11), channel_id=1, source_target_pairs={{0,2},{1,3},{2,4},{3,5},{4,6},{5,7},{6,0},{7,1},{8,10},{9,11},{10,... | collective-permute-start | bytes 393224 | tf_op jit(solution)/shard_map/ppermute | solution.py:16
  97.6 1.9 collective-permute-done.24
  104.8 1.9 collective-permute-done.29
  113.5 1.8 fusion.60
  118.0 2.2 %collective-permute-done.35 = bf16[512,128]{1,0:T(8,128)(2,1)S(1)} collective-permute-done((bf16[512,128]{1,0:T(8,128)(2,1)S(1)}, bf16[512,128]{1,0:T(8,128)(2,1)S(1)}, u32[]{:S(2)}, u32[]{:S(2)}) %collective-permute-start.35) | collective-permute-done | bytes 131104 | tf_op jit(solution)/shard_map/ppermute | solution.py:16
  124.0 2.8 %collective-permute-start.43 = (bf16[512,128]{1,0:T(8,128)(2,1)S(1)}, bf16[512,128]{1,0:T(8,128)(2,1)S(1)}, u32[]{:S(2)}, u32[]{:S(2)}) collective-permute-start(bf16[512,128]{1,0:T(8,128)(2,1)S(1)} %collective-permute-done.40), channel_id=1, source_target_pairs={{0,2},{1,3},{2,4},{3,5},{4,6},{5,7},{6,0},{7,1},{8,10},{9,11},{10,... | collective-permute-start | bytes 393224 | tf_op jit(solution)/shard_map/ppermute | solution.py:16
  127.1 2.3 %collective-permute-start.42 = (bf16[512,128]{1,0:T(8,128)(2,1)S(1)}, bf16[512,128]{1,0:T(8,128)(2,1)S(1)}, u32[]{:S(2)}, u32[]{:S(2)}) collective-permute-start(bf16[512,128]{1,0:T(8,128)(2,1)S(1)} %collective-permute-done.39), channel_id=1, source_target_pairs={{0,2},{1,3},{2,4},{3,5},{4,6},{5,7},{6,0},{7,1},{8,10},{9,11},{10,... | collective-permute-start | bytes 393224 | tf_op jit(solution)/shard_map/ppermute | solution.py:16
  132.6 2.2 %collective-permute-done.43 = bf16[512,128]{1,0:T(8,128)(2,1)S(1)} collective-permute-done((bf16[512,128]{1,0:T(8,128)(2,1)S(1)}, bf16[512,128]{1,0:T(8,128)(2,1)S(1)}, u32[]{:S(2)}, u32[]{:S(2)}) %collective-permute-start.43) | collective-permute-done | bytes 131104 | tf_op jit(solution)/shard_map/ppermute | solution.py:16
  135.2 2.4 %collective-permute-done.42 = bf16[512,128]{1,0:T(8,128)(2,1)S(1)} collective-permute-done((bf16[512,128]{1,0:T(8,128)(2,1)S(1)}, bf16[512,128]{1,0:T(8,128)(2,1)S(1)}, u32[]{:S(2)}, u32[]{:S(2)}) %collective-permute-start.42) | collective-permute-done | bytes 131104 | tf_op jit(solution)/shard_map/ppermute | solution.py:16
  145.8 2.8 %collective-permute-done.45 = bf16[512,128]{1,0:T(8,128)(2,1)S(1)} collective-permute-done((bf16[512,128]{1,0:T(8,128)(2,1)S(1)}, bf16[512,128]{1,0:T(8,128)(2,1)S(1)}, u32[]{:S(2)}, u32[]{:S(2)}) %collective-permute-start.45) | collective-permute-done | bytes 131104 | tf_op jit(solution)/shard_map/ppermute | solution.py:16
  151.0 2.1 %fusion.193 = (bf16[768,128]{1,0:T(8,128)(2,1)}, f32[768,128]{1,0:T(8,128)}) fusion(bf16[768,512]{1,0:T(8,128)(2,1)} %bitcast_dynamic-update-slice_fusion, f32[768,128]{1,0:T(8,128)S(1)} %fusion.94, f32[768,128]{1,0:T(8,128)S(1)} %fusion.132, f32[768,128]{1,0:T(8,128)S(1)} %fusion.169, bf16[512,128]{1,0:T(8,128)(2,1)S(1)} %get-tuple-element.188, ...), kind=kOutput, calls=%fused_computation.255 | convolution fusion | flops 101351424 | bytes 2883584 | tf_op jit(solution)/shard_map/dot_general | solution.py:171
  159.9 4.3 %collective-permute-start.52 = (bf16[512,128]{1,0:T(8,128)(2,1)S(1)}, bf16[512,128]{1,0:T(8,128)(2,1)S(1)}, u32[]{:S(2)}, u32[]{:S(2)}) collective-permute-start(bf16[512,128]{1,0:T(8,128)(2,1)S(1)} %add_convert_fusion.6), channel_id=1, source_target_pairs={{0,2},{1,3},{2,4},{3,5},{4,6},{5,7},{6,0},{7,1},{8,10},{9,11},{10,... | collective-permute-start | bytes 393224 | tf_op jit(solution)/shard_map/ppermute | solution.py:16
  170.9 2.0 %collective-permute-done.57 = bf16[512,128]{1,0:T(8,128)(2,1)S(1)} collective-permute-done((bf16[512,128]{1,0:T(8,128)(2,1)S(1)}, bf16[512,128]{1,0:T(8,128)(2,1)S(1)}, u32[]{:S(2)}, u32[]{:S(2)}) %collective-permute-start.57) | collective-permute-done | bytes 131104 | tf_op jit(solution)/shard_map/ppermute | solution.py:16
  173.3 2.3 %collective-permute-start.58 = (bf16[512,128]{1,0:T(8,128)(2,1)S(1)}, bf16[512,128]{1,0:T(8,128)(2,1)S(1)}, u32[]{:S(2)}, u32[]{:S(2)}) collective-permute-start(bf16[512,128]{1,0:T(8,128)(2,1)S(1)} %add_convert_fusion.3), channel_id=1, source_target_pairs={{0,2},{1,3},{2,4},{3,5},{4,6},{5,7},{6,0},{7,1},{8,10},{9,11},{10,... | collective-permute-start | bytes 393224 | tf_op jit(solution)/shard_map/ppermute | solution.py:16
  176.2 2.3 %collective-permute-done.59 = bf16[512,128]{1,0:T(8,128)(2,1)S(1)} collective-permute-done((bf16[512,128]{1,0:T(8,128)(2,1)S(1)}, bf16[512,128]{1,0:T(8,128)(2,1)S(1)}, u32[]{:S(2)}, u32[]{:S(2)}) %collective-permute-start.59) | collective-permute-done | bytes 131104 | tf_op jit(solution)/shard_map/ppermute | solution.py:16
  179.0 2.3 %collective-permute-done.58 = bf16[512,128]{1,0:T(8,128)(2,1)S(1)} collective-permute-done((bf16[512,128]{1,0:T(8,128)(2,1)S(1)}, bf16[512,128]{1,0:T(8,128)(2,1)S(1)}, u32[]{:S(2)}, u32[]{:S(2)}) %collective-permute-start.58) | collective-permute-done | bytes 131104 | tf_op jit(solution)/shard_map/ppermute | solution.py:16
  183.9 2.4 %collective-permute-done.62 = bf16[512,128]{1,0:T(8,128)(2,1)S(1)} collective-permute-done((bf16[512,128]{1,0:T(8,128)(2,1)S(1)}, bf16[512,128]{1,0:T(8,128)(2,1)S(1)}, u32[]{:S(2)}, u32[]{:S(2)}) %collective-permute-start.62) | collective-permute-done | bytes 131104 | tf_op jit(solution)/shard_map/ppermute | solution.py:16
  187.8 2.8 %collective-permute-done.65 = bf16[512,128]{1,0:T(8,128)(2,1)S(1)} collective-permute-done((bf16[512,128]{1,0:T(8,128)(2,1)S(1)}, bf16[512,128]{1,0:T(8,128)(2,1)S(1)}, u32[]{:S(2)}, u32[]{:S(2)}) %collective-permute-start.65) | collective-permute-done | bytes 131104 | tf_op jit(solution)/shard_map/ppermute | solution.py:16
  192.1 3.9 %collective-permute-done.66 = bf16[512,128]{1,0:T(8,128)(2,1)S(1)} collective-permute-done((bf16[512,128]{1,0:T(8,128)(2,1)S(1)}, bf16[512,128]{1,0:T(8,128)(2,1)S(1)}, u32[]{:S(2)}, u32[]{:S(2)}) %collective-permute-start.66) | collective-permute-done | bytes 131104 | tf_op jit(solution)/shard_map/ppermute | solution.py:16
  (250 shorter events, 103.6 us)
Async XLA Ops:
  3.6 54.6 %collective-permute-start.1 = (bf16[384,2048]{1,0:T(8,128)(2,1)}, bf16[384,2048]{1,0:T(8,128)(2,1)}, u32[]{:S(2)}, u32[]{:S(2)}) collective-permute-start(bf16[384,2048]{1,0:T(8,128)(2,1)} %pad_maximum_fusion), channel_id=1, source_target_pairs={{0,1},{1,0},{2,3},{3,2},{4,5},{5,4},{6,7},{7,6},{8,9},{9,8},{10,11... | collective-permute-start | bytes 4718600 | tf_op jit(solution)/shard_map/ppermute | solution.py:70
  9.5 9.6 %collective-permute-start.6 = (bf16[512,128]{1,0:T(8,128)(2,1)S(1)}, bf16[512,128]{1,0:T(8,128)(2,1)}, u32[]{:S(2)}, u32[]{:S(2)}) collective-permute-start(bf16[512,128]{1,0:T(8,128)(2,1)S(1)} %get-tuple-element.124), channel_id=1, source_target_pairs={{0,2},{1,3},{2,4},{3,5},{4,6},{5,7},{6,0},{7,1},{8,10},{9,11},{10,... | collective-permute-start | bytes 393224 | tf_op jit(solution)/shard_map/ppermute | solution.py:16
  11.1 10.8 %collective-permute-start.5 = (bf16[512,128]{1,0:T(8,128)(2,1)S(1)}, bf16[512,128]{1,0:T(8,128)(2,1)}, u32[]{:S(2)}, u32[]{:S(2)}) collective-permute-start(bf16[512,128]{1,0:T(8,128)(2,1)S(1)} %get-tuple-element.125), channel_id=1, source_target_pairs={{0,2},{1,3},{2,4},{3,5},{4,6},{5,7},{6,0},{7,1},{8,10},{9,11},{10,... | collective-permute-start | bytes 393224 | tf_op jit(solution)/shard_map/ppermute | solution.py:16
  12.7 12.0 %collective-permute-start.4 = (bf16[512,128]{1,0:T(8,128)(2,1)}, bf16[512,128]{1,0:T(8,128)(2,1)}, u32[]{:S(2)}, u32[]{:S(2)}) collective-permute-start(bf16[512,128]{1,0:T(8,128)(2,1)} %get-tuple-element.126), channel_id=1, source_target_pairs={{0,2},{1,3},{2,4},{3,5},{4,6},{5,7},{6,0},{7,1},{8,10},{9,11},{10,... | collective-permute-start | bytes 393224 | tf_op jit(solution)/shard_map/ppermute | solution.py:16
  16.3 10.3 %collective-permute-start.3 = (bf16[512,128]{1,0:T(8,128)(2,1)}, bf16[512,128]{1,0:T(8,128)(2,1)S(1)}, u32[]{:S(2)}, u32[]{:S(2)}) collective-permute-start(bf16[512,128]{1,0:T(8,128)(2,1)} %collective-permute-done.2), channel_id=1, source_target_pairs={{0,2},{1,3},{2,4},{3,5},{4,6},{5,7},{6,0},{7,1},{8,10},{9,11},{10,... | collective-permute-start | bytes 393224 | tf_op jit(solution)/shard_map/ppermute | solution.py:16
  19.1 32.6 %collective-permute-start = (f32[520,512]{1,0:T(8,128)}, f32[520,512]{1,0:T(8,128)}, u32[]{:S(2)}, u32[]{:S(2)}) collective-permute-start(f32[520,512]{1,0:T(8,128)} %concatenate.35), channel_id=1, source_target_pairs={{0,8},{8,16},{16,24},{24,0},{1,9},{9,17},{17,25},{25,1},{2,10},{10... | collective-permute-start | bytes 3194888 | tf_op jit(solution)/shard_map/ppermute | solution.py:16
  33.1 10.3 %collective-permute-start.14 = (bf16[512,128]{1,0:T(8,128)(2,1)}, bf16[512,128]{1,0:T(8,128)(2,1)}, u32[]{:S(2)}, u32[]{:S(2)}) collective-permute-start(bf16[512,128]{1,0:T(8,128)(2,1)} %collective-permute-done.11), channel_id=1, source_target_pairs={{0,2},{1,3},{2,4},{3,5},{4,6},{5,7},{6,0},{7,1},{8,10},{9,11},{10,... | collective-permute-start | bytes 393224 | tf_op jit(solution)/shard_map/ppermute | solution.py:16
  34.5 8.9 %collective-permute-start.15 = (bf16[512,128]{1,0:T(8,128)(2,1)}, bf16[512,128]{1,0:T(8,128)(2,1)}, u32[]{:S(2)}, u32[]{:S(2)}) collective-permute-start(bf16[512,128]{1,0:T(8,128)(2,1)} %collective-permute-done.10), channel_id=1, source_target_pairs={{0,2},{1,3},{2,4},{3,5},{4,6},{5,7},{6,0},{7,1},{8,10},{9,11},{10,... | collective-permute-start | bytes 393224 | tf_op jit(solution)/shard_map/ppermute | solution.py:16
  62.9 10.2 %collective-permute-start.16 = (bf16[768,128]{1,0:T(8,128)(2,1)S(1)}, bf16[768,128]{1,0:T(8,128)(2,1)S(1)}, u32[]{:S(2)}, u32[]{:S(2)}) collective-permute-start(bf16[768,128]{1,0:T(8,128)(2,1)S(1)} %get-tuple-element.139), channel_id=1, source_target_pairs={{0,1},{1,0},{2,3},{3,2},{4,5},{5,4},{6,7},{7,6},{8,9},{9,8},{10,11... | collective-permute-start | bytes 589832 | tf_op jit(solution)/shard_map/ppermute | solution.py:70
  74.6 12.7 %collective-permute-start.23 = (bf16[768,128]{1,0:T(8,128)(2,1)S(1)}, bf16[768,128]{1,0:T(8,128)(2,1)S(1)}, u32[]{:S(2)}, u32[]{:S(2)}) collective-permute-start(bf16[768,128]{1,0:T(8,128)(2,1)S(1)} %get-tuple-element.146), channel_id=1, source_target_pairs={{0,1},{1,0},{2,3},{3,2},{4,5},{5,4},{6,7},{7,6},{8,9},{9,8},{10,11... | collective-permute-start | bytes 589832 | tf_op jit(solution)/shard_map/ppermute | solution.py:70
  80.0 9.6 %collective-permute-start.22 = (bf16[512,128]{1,0:T(8,128)(2,1)S(1)}, bf16[512,128]{1,0:T(8,128)(2,1)S(1)}, u32[]{:S(2)}, u32[]{:S(2)}) collective-permute-start(bf16[512,128]{1,0:T(8,128)(2,1)S(1)} %convolution_convert_fusion.5), channel_id=1, source_target_pairs={{0,2},{1,3},{2,4},{3,5},{4,6},{5,7},{6,0},{7,1},{8,10},{9,11},{10,... | collective-permute-start | bytes 393224 | tf_op jit(solution)/shard_map/ppermute | solution.py:16
  91.9 9.8 %collective-permute-start.27 = (bf16[512,128]{1,0:T(8,128)(2,1)S(1)}, bf16[512,128]{1,0:T(8,128)(2,1)S(1)}, u32[]{:S(2)}, u32[]{:S(2)}) collective-permute-start(bf16[512,128]{1,0:T(8,128)(2,1)S(1)} %add_convert_fusion.11), channel_id=1, source_target_pairs={{0,2},{1,3},{2,4},{3,5},{4,6},{5,7},{6,0},{7,1},{8,10},{9,11},{10,... | collective-permute-start | bytes 393224 | tf_op jit(solution)/shard_map/ppermute | solution.py:16
  97.4 9.3 %collective-permute-start.29 = (bf16[512,128]{1,0:T(8,128)(2,1)S(1)}, bf16[512,128]{1,0:T(8,128)(2,1)S(1)}, u32[]{:S(2)}, u32[]{:S(2)}) collective-permute-start(bf16[512,128]{1,0:T(8,128)(2,1)S(1)} %add_convert_fusion.9), channel_id=1, source_target_pairs={{0,2},{1,3},{2,4},{3,5},{4,6},{5,7},{6,0},{7,1},{8,10},{9,11},{10,... | collective-permute-start | bytes 393224 | tf_op jit(solution)/shard_map/ppermute | solution.py:16
  101.3 8.9 %collective-permute-start.33 = (bf16[512,128]{1,0:T(8,128)(2,1)S(1)}, bf16[512,128]{1,0:T(8,128)(2,1)S(1)}, u32[]{:S(2)}, u32[]{:S(2)}) collective-permute-start(bf16[512,128]{1,0:T(8,128)(2,1)S(1)} %divide_convert_fusion.3), channel_id=1, source_target_pairs={{0,2},{1,3},{2,4},{3,5},{4,6},{5,7},{6,0},{7,1},{8,10},{9,11},{10,... | collective-permute-start | bytes 393224 | tf_op jit(solution)/shard_map/ppermute | solution.py:16
  110.2 10.1 %collective-permute-start.35 = (bf16[512,128]{1,0:T(8,128)(2,1)S(1)}, bf16[512,128]{1,0:T(8,128)(2,1)S(1)}, u32[]{:S(2)}, u32[]{:S(2)}) collective-permute-start(bf16[512,128]{1,0:T(8,128)(2,1)S(1)} %collective-permute-done.33), channel_id=1, source_target_pairs={{0,2},{1,3},{2,4},{3,5},{4,6},{5,7},{6,0},{7,1},{8,10},{9,11},{10,... | collective-permute-start | bytes 393224 | tf_op jit(solution)/shard_map/ppermute | solution.py:16
  117.4 9.6 %collective-permute-start.39 = (bf16[512,128]{1,0:T(8,128)(2,1)S(1)}, bf16[512,128]{1,0:T(8,128)(2,1)S(1)}, u32[]{:S(2)}, u32[]{:S(2)}) collective-permute-start(bf16[512,128]{1,0:T(8,128)(2,1)S(1)} %collective-permute-done.36), channel_id=1, source_target_pairs={{0,2},{1,3},{2,4},{3,5},{4,6},{5,7},{6,0},{7,1},{8,10},{9,11},{10,... | collective-permute-start | bytes 393224 | tf_op jit(solution)/shard_map/ppermute | solution.py:16
  120.2 9.1 %collective-permute-start.38 = (bf16[512,128]{1,0:T(8,128)(2,1)S(1)}, bf16[512,128]{1,0:T(8,128)(2,1)S(1)}, u32[]{:S(2)}, u32[]{:S(2)}) collective-permute-start(bf16[512,128]{1,0:T(8,128)(2,1)S(1)} %collective-permute-done.35), channel_id=1, source_target_pairs={{0,2},{1,3},{2,4},{3,5},{4,6},{5,7},{6,0},{7,1},{8,10},{9,11},{10,... | collective-permute-start | bytes 393224 | tf_op jit(solution)/shard_map/ppermute | solution.py:16
  122.5 9.7 %collective-permute-start.44 = (bf16[512,128]{1,0:T(8,128)(2,1)S(1)}, bf16[512,128]{1,0:T(8,128)(2,1)S(1)}, u32[]{:S(2)}, u32[]{:S(2)}) collective-permute-start(bf16[512,128]{1,0:T(8,128)(2,1)S(1)} %get-tuple-element.188), channel_id=1, source_target_pairs={{0,2},{1,3},{2,4},{3,5},{4,6},{5,7},{6,0},{7,1},{8,10},{9,11},{10,... | collective-permute-start | bytes 393224 | tf_op jit(solution)/shard_map/ppermute | solution.py:16
  122.7 33.3 %collective-permute-start.37 = (bf16[528,512]{1,0:T(8,128)(2,1)S(1)}, bf16[528,512]{1,0:T(8,128)(2,1)S(1)}, u32[]{:S(2)}, u32[]{:S(2)}) collective-permute-start(bf16[528,512]{1,0:T(8,128)(2,1)S(1)} %pad_maximum_fusion.1), channel_id=1, source_target_pairs={{0,16},{8,24},{16,0},{24,8},{1,17},{9,25},{17,1},{25,9},{2,18},{10... | collective-permute-start | bytes 1622024 | tf_op jit(solution)/shard_map/ppermute | solution.py:16
  124.0 10.9 %collective-permute-start.43 = (bf16[512,128]{1,0:T(8,128)(2,1)S(1)}, bf16[512,128]{1,0:T(8,128)(2,1)S(1)}, u32[]{:S(2)}, u32[]{:S(2)}) collective-permute-start(bf16[512,128]{1,0:T(8,128)(2,1)S(1)} %collective-permute-done.40), channel_id=1, source_target_pairs={{0,2},{1,3},{2,4},{3,5},{4,6},{5,7},{6,0},{7,1},{8,10},{9,11},{10,... | collective-permute-start | bytes 393224 | tf_op jit(solution)/shard_map/ppermute | solution.py:16
  127.1 10.5 %collective-permute-start.42 = (bf16[512,128]{1,0:T(8,128)(2,1)S(1)}, bf16[512,128]{1,0:T(8,128)(2,1)S(1)}, u32[]{:S(2)}, u32[]{:S(2)}) collective-permute-start(bf16[512,128]{1,0:T(8,128)(2,1)S(1)} %collective-permute-done.39), channel_id=1, source_target_pairs={{0,2},{1,3},{2,4},{3,5},{4,6},{5,7},{6,0},{7,1},{8,10},{9,11},{10,... | collective-permute-start | bytes 393224 | tf_op jit(solution)/shard_map/ppermute | solution.py:16
  131.1 8.9 %collective-permute-start.41 = (bf16[768,128]{1,0:T(8,128)(2,1)S(1)}, bf16[768,128]{1,0:T(8,128)(2,1)S(1)}, u32[]{:S(2)}, u32[]{:S(2)}) collective-permute-start(bf16[768,128]{1,0:T(8,128)(2,1)S(1)} %get-tuple-element.195), channel_id=1, source_target_pairs={{0,1},{1,0},{2,3},{3,2},{4,5},{5,4},{6,7},{7,6},{8,9},{9,8},{10,11... | collective-permute-start | bytes 589832 | tf_op jit(solution)/shard_map/ppermute | solution.py:70
  139.3 9.8 %collective-permute-start.51 = (bf16[768,128]{1,0:T(8,128)(2,1)S(1)}, bf16[768,128]{1,0:T(8,128)(2,1)S(1)}, u32[]{:S(2)}, u32[]{:S(2)}) collective-permute-start(bf16[768,128]{1,0:T(8,128)(2,1)S(1)} %get-tuple-element.201), channel_id=1, source_target_pairs={{0,1},{1,0},{2,3},{3,2},{4,5},{5,4},{6,7},{7,6},{8,9},{9,8},{10,11... | collective-permute-start | bytes 589832 | tf_op jit(solution)/shard_map/ppermute | solution.py:70
  140.5 10.1 %collective-permute-start.50 = (bf16[512,128]{1,0:T(8,128)(2,1)S(1)}, bf16[512,128]{1,0:T(8,128)(2,1)S(1)}, u32[]{:S(2)}, u32[]{:S(2)}) collective-permute-start(bf16[512,128]{1,0:T(8,128)(2,1)S(1)} %collective-permute-done.47), channel_id=1, source_target_pairs={{0,2},{1,3},{2,4},{3,5},{4,6},{5,7},{6,0},{7,1},{8,10},{9,11},{10,... | collective-permute-start | bytes 393224 | tf_op jit(solution)/shard_map/ppermute | solution.py:16
  144.7 9.4 %collective-permute-start.49 = (bf16[768,128]{1,0:T(8,128)(2,1)S(1)}, bf16[768,128]{1,0:T(8,128)(2,1)S(1)}, u32[]{:S(2)}, u32[]{:S(2)}) collective-permute-start(bf16[768,128]{1,0:T(8,128)(2,1)S(1)} %get-tuple-element.207), channel_id=1, source_target_pairs={{0,1},{1,0},{2,3},{3,2},{4,5},{5,4},{6,7},{7,6},{8,9},{9,8},{10,11... | collective-permute-start | bytes 589832 | tf_op jit(solution)/shard_map/ppermute | solution.py:70
  149.0 9.3 %collective-permute-start.48 = (bf16[512,128]{1,0:T(8,128)(2,1)S(1)}, bf16[512,128]{1,0:T(8,128)(2,1)}, u32[]{:S(2)}, u32[]{:S(2)}) collective-permute-start(bf16[512,128]{1,0:T(8,128)(2,1)S(1)} %add_convert_fusion.7), channel_id=1, source_target_pairs={{0,2},{1,3},{2,4},{3,5},{4,6},{5,7},{6,0},{7,1},{8,10},{9,11},{10,... | collective-permute-start | bytes 393224 | tf_op jit(solution)/shard_map/ppermute | solution.py:16
  150.3 14.0 %collective-permute-start.55 = (bf16[512,128]{1,0:T(8,128)(2,1)}, bf16[512,128]{1,0:T(8,128)(2,1)}, u32[]{:S(2)}, u32[]{:S(2)}) collective-permute-start(bf16[512,128]{1,0:T(8,128)(2,1)} %convolution_convert_fusion.2), channel_id=1, source_target_pairs={{0,2},{1,3},{2,4},{3,5},{4,6},{5,7},{6,0},{7,1},{8,10},{9,11},{10,... | collective-permute-start | bytes 393224 | tf_op jit(solution)/shard_map/ppermute | solution.py:16
  153.1 12.8 %collective-permute-start.54 = (bf16[768,128]{1,0:T(8,128)(2,1)}, bf16[768,128]{1,0:T(8,128)(2,1)}, u32[]{:S(2)}, u32[]{:S(2)}) collective-permute-start(bf16[768,128]{1,0:T(8,128)(2,1)} %get-tuple-element.213), channel_id=1, source_target_pairs={{0,1},{1,0},{2,3},{3,2},{4,5},{5,4},{6,7},{7,6},{8,9},{9,8},{10,11... | collective-permute-start | bytes 589832 | tf_op jit(solution)/shard_map/ppermute | solution.py:70
  155.3 12.2 %collective-permute-start.53 = (bf16[512,128]{1,0:T(8,128)(2,1)}, bf16[512,128]{1,0:T(8,128)(2,1)}, u32[]{:S(2)}, u32[]{:S(2)}) collective-permute-start(bf16[512,128]{1,0:T(8,128)(2,1)} %convolution_convert_fusion.1), channel_id=1, source_target_pairs={{0,2},{1,3},{2,4},{3,5},{4,6},{5,7},{6,0},{7,1},{8,10},{9,11},{10,... | collective-permute-start | bytes 393224 | tf_op jit(solution)/shard_map/ppermute | solution.py:16
  159.9 9.6 %collective-permute-start.52 = (bf16[512,128]{1,0:T(8,128)(2,1)S(1)}, bf16[512,128]{1,0:T(8,128)(2,1)S(1)}, u32[]{:S(2)}, u32[]{:S(2)}) collective-permute-start(bf16[512,128]{1,0:T(8,128)(2,1)S(1)} %add_convert_fusion.6), channel_id=1, source_target_pairs={{0,2},{1,3},{2,4},{3,5},{4,6},{5,7},{6,0},{7,1},{8,10},{9,11},{10,... | collective-permute-start | bytes 393224 | tf_op jit(solution)/shard_map/ppermute | solution.py:16
  168.8 9.7 %collective-permute-start.59 = (bf16[512,128]{1,0:T(8,128)(2,1)S(1)}, bf16[512,128]{1,0:T(8,128)(2,1)S(1)}, u32[]{:S(2)}, u32[]{:S(2)}) collective-permute-start(bf16[512,128]{1,0:T(8,128)(2,1)S(1)} %add_convert_fusion.4), channel_id=1, source_target_pairs={{0,2},{1,3},{2,4},{3,5},{4,6},{5,7},{6,0},{7,1},{8,10},{9,11},{10,... | collective-permute-start | bytes 393224 | tf_op jit(solution)/shard_map/ppermute | solution.py:16
  169.9 13.0 %collective-permute-start.56 = (bf16[512,128]{1,0:T(8,128)(2,1)S(1)}, bf16[512,128]{1,0:T(8,128)(2,1)S(1)}, u32[]{:S(2)}, u32[]{:S(2)}) collective-permute-start(bf16[512,128]{1,0:T(8,128)(2,1)S(1)} %get-tuple-element.225), channel_id=1, source_target_pairs={{0,16},{8,24},{16,0},{24,8},{1,17},{9,25},{17,1},{25,9},{2,18},{10... | collective-permute-start | bytes 393224 | tf_op jit(solution)/shard_map/ppermute | solution.py:16
  (63 other events, 480.3 us)

commit v2 on v1

--- a/solution.py
+++ b/solution.py
@@ -86,7 +86,7 @@
         return pair_tokens[:, back * block : (back + 1) * block]
 
     outgoing = half_columns(inputs, 1 - lane)
-    theirs = send(outgoing, "pair")
+    theirs = lax.ppermute(outgoing, "fsdp", [(i, i ^ 1) for i in range(count)])
     params = after(params, outgoing)
     momentum = after(momentum, outgoing)
     zero = jnp.zeros((), lane.dtype)
@@ -119,21 +119,25 @@
             row = lax.broadcasted_iota(jnp.int32, (16, features), 0)
             extra = jnp.where(row == 0, parts[0], jnp.where(row == 1, parts[1], parts[2]))
             whole, extra = whole.astype(narrow), extra.astype(narrow)
-        got = send(jnp.concatenate([whole, extra], axis=0), "group", 2**step).astype(wide)
-        passed.append(got[:held])
+        whole = jnp.concatenate([whole, extra], axis=0)
+        passed.append(send(whole, "group", 2**step) if step else from_behind(whole, "group", 1))
+
+    def read_passed(step):
+        got = after(passed[step], issued[-1]).astype(wide)
+        passed[step] = got[:held]
         came = got[held, :1] if step == 0 else jnp.sum(got[held : held + 3, :1], axis=0)
         weights.append(0.5 * weights[step] + 0.5 * came)
 
     first = [[debias(chunk(params[0], c), push_weight)] for c in range(CHUNKS)]
     for back in range(1, half):
         for c in range(CHUNKS):
-            first[c].append(send(first[c][-1], "line"))
+            first[c].append(from_behind(first[c][-1], "fsdp", 2))
         if back == 1:
             exchange_kept(params[0] - (0.2 * 0.9) * momentum[0], 0)
     first_keys = []
     for c in range(0, CHUNKS, 2):
         both = [jnp.concatenate(first[i], axis=0) for i in (c, c + 1)]
-        both = after(jnp.concatenate(both, axis=1), *first[c + 1][-1:])
+        both = after(jnp.concatenate(both, axis=1))
         both = jnp.dot(pair_tokens, both, preferred_element_type=wide)
         first_keys += [both[:, :part], both[:, part:]]
 
@@ -156,6 +160,8 @@
             total = partial(1)
             for back in range(2, half + 1):
                 arrived = yield total.astype(narrow), "line"
+                if c == 0 and back == half:
+                    read_passed(step)
                 total = arrived.astype(wide) + partial(back % half)
             behind = yield total.astype(narrow), "group"
             moment = 0.9 * moment + total
@@ -180,7 +186,8 @@
     came = [None] * CHUNKS
     mixings = [0] * CHUNKS
     for c in issue_order(half):
-        came[c] = came[c] if came[c] is None else after(came[c], issued[-1])
+        if came[c] is not None:
+            came[c] = after(came[c], issued[-1])
         value, link = streams[c].send(came[c])
         came[c] = send(value, link, 2 ** mixings[c])
         mixings[c] += link == "group"

time: 198 us -> 194 us (0.980)
  other arithmetic: 22.2 us -> 17.8 us
  waiting for transfers between devices: 79.8 us -> 76.9 us
  starting transfers between devices: 47.5 us -> 49.5 us
    ppermute x0 -> x1, starting transfers between devices: none -> 2.94 us  [shards(): theirs = lax.ppermute(outgoing, 'fsdp', [(i, i ^ 1) for i in range(count)])]
    another operation x4, other arithmetic: 6.1 us -> 3.29 us
    dot_general x32, matrix products: 17.4 us -> 19.7 us  [partial(): lax.dot_general(column_block(back), grad_out, contract, preferred_element...]
    ppermute x9 -> x8, waiting for transfers between devices: 5.4 us -> 4.46 us  [send(): return lax.ppermute(value, 'fsdp', [(i, i ^ 1) for i in range(count)])]
    ppermute x9 -> x8, starting transfers between devices: 9.73 us -> 9.26 us  [send(): return lax.ppermute(value, 'fsdp', [(i, i ^ 1) for i in range(count)])]
  transfers between devices with their start and end apart: 67 -> 67, of which waited for: 37 -> 38; matrix products, arithmetic and copies ran while one was open for 28% -> 28% of each run, Pallas kernels for 0% -> 0%
where the time goes in v2:
time: 194 us; the launch traced here: 193 us
  waiting for transfers between devices  76.9 us (40%)
  starting transfers between devices  49.5 us (26%)
  matrix products  31.2 us (16%)
  other arithmetic  17.8 us (9%)
  local copies, waits for them, and re-layouts  11 us (6%)
  between operations  6.34 us (3%)
    ppermute x58, waiting for transfers between devices, from_behind(): return lax.ppermute(value, axis, pairs)  72.5 us
    ppermute x58, starting transfers between devices, from_behind(): return lax.ppermute(value, axis, pairs)  37.3 us
    dot_general x32, matrix products, partial(): lax.dot_general(column_block(back), grad_out, contract, preferred_element...  19.7 us
    dot_general x16, matrix products, stream(): jnp.dot(column_block(back), piece, preferred_element_type=wide)  9.57 us
    ppermute x8, starting transfers between devices, send(): return lax.ppermute(value, 'fsdp', [(i, i ^ 1) for i in range(count)])  9.26 us
    ppermute x8, waiting for transfers between devices, send(): return lax.ppermute(value, 'fsdp', [(i, i ^ 1) for i in range(count)])  4.46 us
  transfers between devices with their start and end apart: 67, of which 38 were waited for; matrix products, arithmetic and copies ran while one was open for 28% of the time, Pallas kernels for 0%

profile of v2, /device:TPU:0, one launch (start us, length us, event | category | flops | bytes accessed | tf_op | source)
XLA Modules:
  0.0 192.8 jit_solution(14209613394906857889)
XLA Ops:
  3.6 2.9 %collective-permute-start.1 = (bf16[384,2048]{1,0:T(8,128)(2,1)}, bf16[384,2048]{1,0:T(8,128)(2,1)}, u32[]{:S(2)}, u32[]{:S(2)}) collective-permute-start(bf16[384,2048]{1,0:T(8,128)(2,1)} %pad_maximum_fusion), channel_id=1, source_target_pairs={{0,1},{1,0},{2,3},{3,2},{4,5},{5,4},{6,7},{7,6},{8,9},{9,8},{10,11... | collective-permute-start | bytes 4718600 | tf_op jit(solution)/shard_map/ppermute | solution.py:89
  16.4 2.1 %collective-permute-done.5 = bf16[512,128]{1,0:T(8,128)(2,1)} collective-permute-done((bf16[512,128]{1,0:T(8,128)(2,1)S(1)}, bf16[512,128]{1,0:T(8,128)(2,1)}, u32[]{:S(2)}, u32[]{:S(2)}) %collective-permute-start.5) | collective-permute-done | bytes 131104 | tf_op jit(solution)/shard_map/ppermute | solution.py:16
  19.1 2.2 %collective-permute-done.9 = bf16[512,128]{1,0:T(8,128)(2,1)} collective-permute-done((bf16[512,128]{1,0:T(8,128)(2,1)S(1)}, bf16[512,128]{1,0:T(8,128)(2,1)}, u32[]{:S(2)}, u32[]{:S(2)}) %collective-permute-start.9) | collective-permute-done | bytes 131104 | tf_op jit(solution)/shard_map/ppermute | solution.py:16
  21.3 2.8 %collective-permute-done.12 = bf16[512,128]{1,0:T(8,128)(2,1)} collective-permute-done((bf16[512,128]{1,0:T(8,128)(2,1)S(1)}, bf16[512,128]{1,0:T(8,128)(2,1)}, u32[]{:S(2)}, u32[]{:S(2)}) %collective-permute-start.12) | collective-permute-done | bytes 131104 | tf_op jit(solution)/shard_map/ppermute | solution.py:16
  24.1 2.8 %collective-permute-done.3 = bf16[512,128]{1,0:T(8,128)(2,1)} collective-permute-done((bf16[512,128]{1,0:T(8,128)(2,1)}, bf16[512,128]{1,0:T(8,128)(2,1)}, u32[]{:S(2)}, u32[]{:S(2)}) %collective-permute-start.3) | collective-permute-done | bytes 131104 | tf_op jit(solution)/shard_map/ppermute | solution.py:16
  27.0 2.8 %collective-permute-done.6 = bf16[512,128]{1,0:T(8,128)(2,1)} collective-permute-done((bf16[512,128]{1,0:T(8,128)(2,1)}, bf16[512,128]{1,0:T(8,128)(2,1)}, u32[]{:S(2)}, u32[]{:S(2)}) %collective-permute-start.6) | collective-permute-done | bytes 131104 | tf_op jit(solution)/shard_map/ppermute | solution.py:16
  32.9 2.5 %collective-permute-done.13 = bf16[512,128]{1,0:T(8,128)(2,1)} collective-permute-done((bf16[512,128]{1,0:T(8,128)(2,1)}, bf16[512,128]{1,0:T(8,128)(2,1)}, u32[]{:S(2)}, u32[]{:S(2)}) %collective-permute-start.13) | collective-permute-done | bytes 131104 | tf_op jit(solution)/shard_map/ppermute | solution.py:16
  35.4 2.8 %collective-permute-done.4 = bf16[512,128]{1,0:T(8,128)(2,1)} collective-permute-done((bf16[512,128]{1,0:T(8,128)(2,1)}, bf16[512,128]{1,0:T(8,128)(2,1)}, u32[]{:S(2)}, u32[]{:S(2)}) %collective-permute-start.4) | collective-permute-done | bytes 131104 | tf_op jit(solution)/shard_map/ppermute | solution.py:16
  41.0 2.7 %collective-permute-done.11 = bf16[512,128]{1,0:T(8,128)(2,1)S(1)} collective-permute-done((bf16[512,128]{1,0:T(8,128)(2,1)}, bf16[512,128]{1,0:T(8,128)(2,1)S(1)}, u32[]{:S(2)}, u32[]{:S(2)}) %collective-permute-start.11) | collective-permute-done | bytes 131104 | tf_op jit(solution)/shard_map/ppermute | solution.py:16
  53.2 4.4 %collective-permute-done.15 = bf16[768,128]{1,0:T(8,128)(2,1)S(1)} collective-permute-done((bf16[768,128]{1,0:T(8,128)(2,1)S(1)}, bf16[768,128]{1,0:T(8,128)(2,1)S(1)}, u32[]{:S(2)}, u32[]{:S(2)}) %collective-permute-start.15) | collective-permute-done | bytes 196640 | tf_op jit(solution)/shard_map/ppermute | solution.py:70
  64.6 3.0 %collective-permute-done.18 = bf16[512,128]{1,0:T(8,128)(2,1)S(1)} collective-permute-done((bf16[512,128]{1,0:T(8,128)(2,1)S(1)}, bf16[512,128]{1,0:T(8,128)(2,1)S(1)}, u32[]{:S(2)}, u32[]{:S(2)}) %collective-permute-start.18) | collective-permute-done | bytes 131104 | tf_op jit(solution)/shard_map/ppermute | solution.py:16
  71.4 3.5 %collective-permute-done.22 = bf16[512,128]{1,0:T(8,128)(2,1)S(1)} collective-permute-done((bf16[512,128]{1,0:T(8,128)(2,1)S(1)}, bf16[512,128]{1,0:T(8,128)(2,1)S(1)}, u32[]{:S(2)}, u32[]{:S(2)}) %collective-permute-start.22) | collective-permute-done | bytes 131104 | tf_op jit(solution)/shard_map/ppermute | solution.py:16
  78.3 2.3 %collective-permute-done.19 = bf16[512,128]{1,0:T(8,128)(2,1)S(1)} collective-permute-done((bf16[512,128]{1,0:T(8,128)(2,1)S(1)}, bf16[512,128]{1,0:T(8,128)(2,1)S(1)}, u32[]{:S(2)}, u32[]{:S(2)}) %collective-permute-start.19) | collective-permute-done | bytes 131104 | tf_op jit(solution)/shard_map/ppermute | solution.py:16
  81.0 1.7 collective-permute-start.27
  91.4 2.3 %collective-permute-done.24 = bf16[512,128]{1,0:T(8,128)(2,1)S(1)} collective-permute-done((bf16[512,128]{1,0:T(8,128)(2,1)S(1)}, bf16[512,128]{1,0:T(8,128)(2,1)S(1)}, u32[]{:S(2)}, u32[]{:S(2)}) %collective-permute-start.24) | collective-permute-done | bytes 131104 | tf_op jit(solution)/shard_map/ppermute | solution.py:16
  99.8 2.2 %collective-permute-start.31 = (bf16[512,128]{1,0:T(8,128)(2,1)S(1)}, bf16[512,128]{1,0:T(8,128)(2,1)S(1)}, u32[]{:S(2)}, u32[]{:S(2)}) collective-permute-start(bf16[512,128]{1,0:T(8,128)(2,1)S(1)} %get-tuple-element.145), channel_id=1, source_target_pairs={{0,8},{8,16},{16,24},{24,0},{1,9},{9,17},{17,25},{25,1},{2,10},{10... | collective-permute-start | bytes 393224 | tf_op jit(solution)/shard_map/ppermute | solution.py:16
  103.9 1.8 collective-permute-done.32
  108.3 2.5 %collective-permute-done.36 = bf16[512,128]{1,0:T(8,128)(2,1)S(1)} collective-permute-done((bf16[512,128]{1,0:T(8,128)(2,1)S(1)}, bf16[512,128]{1,0:T(8,128)(2,1)S(1)}, u32[]{:S(2)}, u32[]{:S(2)}) %collective-permute-start.36) | collective-permute-done | bytes 131104 | tf_op jit(solution)/shard_map/ppermute | solution.py:16
  110.7 2.8 %collective-permute-done.35 = bf16[512,128]{1,0:T(8,128)(2,1)S(1)} collective-permute-done((bf16[512,128]{1,0:T(8,128)(2,1)S(1)}, bf16[512,128]{1,0:T(8,128)(2,1)S(1)}, u32[]{:S(2)}, u32[]{:S(2)}) %collective-permute-start.35) | collective-permute-done | bytes 131104 | tf_op jit(solution)/shard_map/ppermute | solution.py:16
  116.4 2.2 %collective-permute-start.39 = (bf16[512,128]{1,0:T(8,128)(2,1)S(1)}, bf16[512,128]{1,0:T(8,128)(2,1)S(1)}, u32[]{:S(2)}, u32[]{:S(2)}) collective-permute-start(bf16[512,128]{1,0:T(8,128)(2,1)S(1)} %collective-permute-done.38), channel_id=1, source_target_pairs={{0,2},{1,3},{2,4},{3,5},{4,6},{5,7},{6,0},{7,1},{8,10},{9,11},{10,... | collective-permute-start | bytes 393224 | tf_op jit(solution)/shard_map/ppermute | solution.py:16
  119.2 2.8 %collective-permute-done.41 = bf16[512,128]{1,0:T(8,128)(2,1)S(1)} collective-permute-done((bf16[512,128]{1,0:T(8,128)(2,1)S(1)}, bf16[512,128]{1,0:T(8,128)(2,1)S(1)}, u32[]{:S(2)}, u32[]{:S(2)}) %collective-permute-start.41) | collective-permute-done | bytes 131104 | tf_op jit(solution)/shard_map/ppermute | solution.py:16
  128.9 4.5 %collective-permute-done.46 = bf16[512,128]{1,0:T(8,128)(2,1)S(1)} collective-permute-done((bf16[512,128]{1,0:T(8,128)(2,1)S(1)}, bf16[512,128]{1,0:T(8,128)(2,1)S(1)}, u32[]{:S(2)}, u32[]{:S(2)}) %collective-permute-start.46) | collective-permute-done | bytes 131104 | tf_op jit(solution)/shard_map/ppermute | solution.py:16
  136.8 2.1 %collective-permute-done.43 = bf16[512,128]{1,0:T(8,128)(2,1)S(1)} collective-permute-done((bf16[512,128]{1,0:T(8,128)(2,1)S(1)}, bf16[512,128]{1,0:T(8,128)(2,1)S(1)}, u32[]{:S(2)}, u32[]{:S(2)}) %collective-permute-start.43) | collective-permute-done | bytes 131104 | tf_op jit(solution)/shard_map/ppermute | solution.py:16
  141.8 2.7 %collective-permute-done.50 = bf16[512,128]{1,0:T(8,128)(2,1)S(1)} collective-permute-done((bf16[512,128]{1,0:T(8,128)(2,1)S(1)}, bf16[512,128]{1,0:T(8,128)(2,1)S(1)}, u32[]{:S(2)}, u32[]{:S(2)}) %collective-permute-start.50) | collective-permute-done | bytes 131104 | tf_op jit(solution)/shard_map/ppermute | solution.py:16
  149.9 1.9 collective-permute-done.54
  152.8 2.4 %collective-permute-start.55 = (bf16[512,128]{1,0:T(8,128)(2,1)}, bf16[512,128]{1,0:T(8,128)(2,1)S(1)}, u32[]{:S(2)}, u32[]{:S(2)}) collective-permute-start(bf16[512,128]{1,0:T(8,128)(2,1)} %add_convert_fusion.6), channel_id=1, source_target_pairs={{0,2},{1,3},{2,4},{3,5},{4,6},{5,7},{6,0},{7,1},{8,10},{9,11},{10,... | collective-permute-start | bytes 393224 | tf_op jit(solution)/shard_map/ppermute | solution.py:16
  159.0 2.0 %collective-permute-start.59 = (bf16[512,128]{1,0:T(8,128)(2,1)}, bf16[512,128]{1,0:T(8,128)(2,1)}, u32[]{:S(2)}, u32[]{:S(2)}) collective-permute-start(bf16[512,128]{1,0:T(8,128)(2,1)} %add_convert_fusion.4), channel_id=1, source_target_pairs={{0,2},{1,3},{2,4},{3,5},{4,6},{5,7},{6,0},{7,1},{8,10},{9,11},{10,... | collective-permute-start | bytes 393224 | tf_op jit(solution)/shard_map/ppermute | solution.py:16
  164.8 1.8 collective-permute-start.56
  168.1 1.8 collective-permute-start.58
  176.6 2.1 %collective-permute-done.63 = bf16[512,128]{1,0:T(8,128)(2,1)S(1)} collective-permute-done((bf16[512,128]{1,0:T(8,128)(2,1)S(1)}, bf16[512,128]{1,0:T(8,128)(2,1)S(1)}, u32[]{:S(2)}, u32[]{:S(2)}) %collective-permute-start.63) | collective-permute-done | bytes 131104 | tf_op jit(solution)/shard_map/ppermute | solution.py:16
  182.4 3.6 %collective-permute-done.65 = bf16[512,128]{1,0:T(8,128)(2,1)S(1)} collective-permute-done((bf16[512,128]{1,0:T(8,128)(2,1)S(1)}, bf16[512,128]{1,0:T(8,128)(2,1)S(1)}, u32[]{:S(2)}, u32[]{:S(2)}) %collective-permute-start.65) | collective-permute-done | bytes 131104 | tf_op jit(solution)/shard_map/ppermute | solution.py:16
  188.2 3.2 %collective-permute-done.66 = bf16[512,128]{1,0:T(8,128)(2,1)S(1)} collective-permute-done((bf16[512,128]{1,0:T(8,128)(2,1)S(1)}, bf16[512,128]{1,0:T(8,128)(2,1)S(1)}, u32[]{:S(2)}, u32[]{:S(2)}) %collective-permute-start.66) | collective-permute-done | bytes 131104 | tf_op jit(solution)/shard_map/ppermute | solution.py:16
  (250 shorter events, 103.2 us)
Async XLA Ops:
  3.6 42.8 %collective-permute-start.1 = (bf16[384,2048]{1,0:T(8,128)(2,1)}, bf16[384,2048]{1,0:T(8,128)(2,1)}, u32[]{:S(2)}, u32[]{:S(2)}) collective-permute-start(bf16[384,2048]{1,0:T(8,128)(2,1)} %pad_maximum_fusion), channel_id=1, source_target_pairs={{0,1},{1,0},{2,3},{3,2},{4,5},{5,4},{6,7},{7,6},{8,9},{9,8},{10,11... | collective-permute-start | bytes 4718600 | tf_op jit(solution)/shard_map/ppermute | solution.py:89
  9.0 9.6 %collective-permute-start.5 = (bf16[512,128]{1,0:T(8,128)(2,1)S(1)}, bf16[512,128]{1,0:T(8,128)(2,1)}, u32[]{:S(2)}, u32[]{:S(2)}) collective-permute-start(bf16[512,128]{1,0:T(8,128)(2,1)S(1)} %get-tuple-element.238), channel_id=1, source_target_pairs={{0,2},{1,3},{2,4},{3,5},{4,6},{5,7},{6,0},{7,1},{8,10},{9,11},{10,... | collective-permute-start | bytes 393224 | tf_op jit(solution)/shard_map/ppermute | solution.py:16
  10.5 10.8 %collective-permute-start.9 = (bf16[512,128]{1,0:T(8,128)(2,1)S(1)}, bf16[512,128]{1,0:T(8,128)(2,1)}, u32[]{:S(2)}, u32[]{:S(2)}) collective-permute-start(bf16[512,128]{1,0:T(8,128)(2,1)S(1)} %get-tuple-element.237), channel_id=1, source_target_pairs={{0,2},{1,3},{2,4},{3,5},{4,6},{5,7},{6,0},{7,1},{8,10},{9,11},{10,... | collective-permute-start | bytes 393224 | tf_op jit(solution)/shard_map/ppermute | solution.py:16
  12.1 12.0 %collective-permute-start.12 = (bf16[512,128]{1,0:T(8,128)(2,1)S(1)}, bf16[512,128]{1,0:T(8,128)(2,1)}, u32[]{:S(2)}, u32[]{:S(2)}) collective-permute-start(bf16[512,128]{1,0:T(8,128)(2,1)S(1)} %get-tuple-element.240), channel_id=1, source_target_pairs={{0,2},{1,3},{2,4},{3,5},{4,6},{5,7},{6,0},{7,1},{8,10},{9,11},{10,... | collective-permute-start | bytes 393224 | tf_op jit(solution)/shard_map/ppermute | solution.py:16
  15.7 11.2 %collective-permute-start.3 = (bf16[512,128]{1,0:T(8,128)(2,1)}, bf16[512,128]{1,0:T(8,128)(2,1)}, u32[]{:S(2)}, u32[]{:S(2)}) collective-permute-start(bf16[512,128]{1,0:T(8,128)(2,1)} %collective-permute-done.2), channel_id=1, source_target_pairs={{0,2},{1,3},{2,4},{3,5},{4,6},{5,7},{6,0},{7,1},{8,10},{9,11},{10,... | collective-permute-start | bytes 393224 | tf_op jit(solution)/shard_map/ppermute | solution.py:16
  18.5 11.2 %collective-permute-start.6 = (bf16[512,128]{1,0:T(8,128)(2,1)}, bf16[512,128]{1,0:T(8,128)(2,1)}, u32[]{:S(2)}, u32[]{:S(2)}) collective-permute-start(bf16[512,128]{1,0:T(8,128)(2,1)} %collective-permute-done.5), channel_id=1, source_target_pairs={{0,2},{1,3},{2,4},{3,5},{4,6},{5,7},{6,0},{7,1},{8,10},{9,11},{10,... | collective-permute-start | bytes 393224 | tf_op jit(solution)/shard_map/ppermute | solution.py:16
  21.3 11.4 %collective-permute-start.10 = (bf16[512,128]{1,0:T(8,128)(2,1)}, bf16[512,128]{1,0:T(8,128)(2,1)}, u32[]{:S(2)}, u32[]{:S(2)}) collective-permute-start(bf16[512,128]{1,0:T(8,128)(2,1)} %collective-permute-done.9), channel_id=1, source_target_pairs={{0,2},{1,3},{2,4},{3,5},{4,6},{5,7},{6,0},{7,1},{8,10},{9,11},{10,... | collective-permute-start | bytes 393224 | tf_op jit(solution)/shard_map/ppermute | solution.py:16
  24.1 11.2 %collective-permute-start.13 = (bf16[512,128]{1,0:T(8,128)(2,1)}, bf16[512,128]{1,0:T(8,128)(2,1)}, u32[]{:S(2)}, u32[]{:S(2)}) collective-permute-start(bf16[512,128]{1,0:T(8,128)(2,1)} %collective-permute-done.12), channel_id=1, source_target_pairs={{0,2},{1,3},{2,4},{3,5},{4,6},{5,7},{6,0},{7,1},{8,10},{9,11},{10,... | collective-permute-start | bytes 393224 | tf_op jit(solution)/shard_map/ppermute | solution.py:16
  26.9 11.2 %collective-permute-start.4 = (bf16[512,128]{1,0:T(8,128)(2,1)}, bf16[512,128]{1,0:T(8,128)(2,1)}, u32[]{:S(2)}, u32[]{:S(2)}) collective-permute-start(bf16[512,128]{1,0:T(8,128)(2,1)} %collective-permute-done.3), channel_id=1, source_target_pairs={{0,2},{1,3},{2,4},{3,5},{4,6},{5,7},{6,0},{7,1},{8,10},{9,11},{10,... | collective-permute-start | bytes 393224 | tf_op jit(solution)/shard_map/ppermute | solution.py:16
  29.8 9.9 %collective-permute-start.7 = (bf16[512,128]{1,0:T(8,128)(2,1)}, bf16[512,128]{1,0:T(8,128)(2,1)}, u32[]{:S(2)}, u32[]{:S(2)}) collective-permute-start(bf16[512,128]{1,0:T(8,128)(2,1)} %collective-permute-done.6), channel_id=1, source_target_pairs={{0,2},{1,3},{2,4},{3,5},{4,6},{5,7},{6,0},{7,1},{8,10},{9,11},{10,... | collective-permute-start | bytes 393224 | tf_op jit(solution)/shard_map/ppermute | solution.py:16
  32.8 50.0 %collective-permute-start = (f32[520,512]{1,0:T(8,128)S(1)}, f32[520,512]{1,0:T(8,128)S(1)}, u32[]{:S(2)}, u32[]{:S(2)}) collective-permute-start(f32[520,512]{1,0:T(8,128)S(1)} %concatenate.35), channel_id=1, source_target_pairs={{0,8},{8,16},{16,24},{24,0},{1,9},{9,17},{17,25},{25,1},{2,10},{10... | collective-permute-start | bytes 3194888 | tf_op jit(solution)/shard_map/ppermute | solution.py:16
  50.7 9.7 %collective-permute-start.8 = (bf16[768,128]{1,0:T(8,128)(2,1)S(1)}, bf16[768,128]{1,0:T(8,128)(2,1)S(1)}, u32[]{:S(2)}, u32[]{:S(2)}) collective-permute-start(bf16[768,128]{1,0:T(8,128)(2,1)S(1)} %get-tuple-element.110), channel_id=1, source_target_pairs={{0,1},{1,0},{2,3},{3,2},{4,5},{5,4},{6,7},{7,6},{8,9},{9,8},{10,11... | collective-permute-start | bytes 589832 | tf_op jit(solution)/shard_map/ppermute | solution.py:70
  63.1 12.4 %collective-permute-start.21 = (bf16[768,128]{1,0:T(8,128)(2,1)S(1)}, bf16[768,128]{1,0:T(8,128)(2,1)S(1)}, u32[]{:S(2)}, u32[]{:S(2)}) collective-permute-start(bf16[768,128]{1,0:T(8,128)(2,1)S(1)} %get-tuple-element.116), channel_id=1, source_target_pairs={{0,1},{1,0},{2,3},{3,2},{4,5},{5,4},{6,7},{7,6},{8,9},{9,8},{10,11... | collective-permute-start | bytes 589832 | tf_op jit(solution)/shard_map/ppermute | solution.py:70
  70.9 9.7 %collective-permute-start.19 = (bf16[512,128]{1,0:T(8,128)(2,1)S(1)}, bf16[512,128]{1,0:T(8,128)(2,1)S(1)}, u32[]{:S(2)}, u32[]{:S(2)}) collective-permute-start(bf16[512,128]{1,0:T(8,128)(2,1)S(1)} %add_convert_fusion.14), channel_id=1, source_target_pairs={{0,2},{1,3},{2,4},{3,5},{4,6},{5,7},{6,0},{7,1},{8,10},{9,11},{10,... | collective-permute-start | bytes 393224 | tf_op jit(solution)/shard_map/ppermute | solution.py:16
  75.3 13.5 %collective-permute-start.23 = (bf16[512,128]{1,0:T(8,128)(2,1)S(1)}, bf16[512,128]{1,0:T(8,128)(2,1)S(1)}, u32[]{:S(2)}, u32[]{:S(2)}) collective-permute-start(bf16[512,128]{1,0:T(8,128)(2,1)S(1)} %add_convert_fusion.13), channel_id=1, source_target_pairs={{0,2},{1,3},{2,4},{3,5},{4,6},{5,7},{6,0},{7,1},{8,10},{9,11},{10,... | collective-permute-start | bytes 393224 | tf_op jit(solution)/shard_map/ppermute | solution.py:16
  77.0 12.3 %collective-permute-start.26 = (bf16[512,128]{1,0:T(8,128)(2,1)S(1)}, bf16[512,128]{1,0:T(8,128)(2,1)S(1)}, u32[]{:S(2)}, u32[]{:S(2)}) collective-permute-start(bf16[512,128]{1,0:T(8,128)(2,1)S(1)} %convolution_convert_fusion.4), channel_id=1, source_target_pairs={{0,2},{1,3},{2,4},{3,5},{4,6},{5,7},{6,0},{7,1},{8,10},{9,11},{10,... | collective-permute-start | bytes 393224 | tf_op jit(solution)/shard_map/ppermute | solution.py:16
  78.2 11.7 %collective-permute-start.25 = (bf16[512,128]{1,0:T(8,128)(2,1)S(1)}, bf16[512,128]{1,0:T(8,128)(2,1)S(1)}, u32[]{:S(2)}, u32[]{:S(2)}) collective-permute-start(bf16[512,128]{1,0:T(8,128)(2,1)S(1)} %add_convert_fusion.12), channel_id=1, source_target_pairs={{0,2},{1,3},{2,4},{3,5},{4,6},{5,7},{6,0},{7,1},{8,10},{9,11},{10,... | collective-permute-start | bytes 393224 | tf_op jit(solution)/shard_map/ppermute | solution.py:16
  81.0 13.7 %collective-permute-start.27 = (bf16[512,128]{1,0:T(8,128)(2,1)S(1)}, bf16[512,128]{1,0:T(8,128)(2,1)S(1)}, u32[]{:S(2)}, u32[]{:S(2)}) collective-permute-start(bf16[512,128]{1,0:T(8,128)(2,1)S(1)} %add_convert_fusion.11), channel_id=1, source_target_pairs={{0,2},{1,3},{2,4},{3,5},{4,6},{5,7},{6,0},{7,1},{8,10},{9,11},{10,... | collective-permute-start | bytes 393224 | tf_op jit(solution)/shard_map/ppermute | solution.py:16
  103.0 10.6 %collective-permute-start.35 = (bf16[512,128]{1,0:T(8,128)(2,1)S(1)}, bf16[512,128]{1,0:T(8,128)(2,1)S(1)}, u32[]{:S(2)}, u32[]{:S(2)}) collective-permute-start(bf16[512,128]{1,0:T(8,128)(2,1)S(1)} %collective-permute-done.33), channel_id=1, source_target_pairs={{0,2},{1,3},{2,4},{3,5},{4,6},{5,7},{6,0},{7,1},{8,10},{9,11},{10,... | collective-permute-start | bytes 393224 | tf_op jit(solution)/shard_map/ppermute | solution.py:16
  114.8 9.9 %collective-permute-start.40 = (bf16[512,128]{1,0:T(8,128)(2,1)S(1)}, bf16[512,128]{1,0:T(8,128)(2,1)S(1)}, u32[]{:S(2)}, u32[]{:S(2)}) collective-permute-start(bf16[512,128]{1,0:T(8,128)(2,1)S(1)} %get-tuple-element.159), channel_id=1, source_target_pairs={{0,2},{1,3},{2,4},{3,5},{4,6},{5,7},{6,0},{7,1},{8,10},{9,11},{10,... | collective-permute-start | bytes 393224 | tf_op jit(solution)/shard_map/ppermute | solution.py:16
  114.9 46.2 %collective-permute-start.37 = (bf16[528,512]{1,0:T(8,128)(2,1)S(1)}, bf16[528,512]{1,0:T(8,128)(2,1)S(1)}, u32[]{:S(2)}, u32[]{:S(2)}) collective-permute-start(bf16[528,512]{1,0:T(8,128)(2,1)S(1)} %pad_maximum_fusion.1), channel_id=1, source_target_pairs={{0,16},{8,24},{16,0},{24,8},{1,17},{9,25},{17,1},{25,9},{2,18},{10... | collective-permute-start | bytes 1622024 | tf_op jit(solution)/shard_map/ppermute | solution.py:16
  116.4 11.2 %collective-permute-start.39 = (bf16[512,128]{1,0:T(8,128)(2,1)S(1)}, bf16[512,128]{1,0:T(8,128)(2,1)S(1)}, u32[]{:S(2)}, u32[]{:S(2)}) collective-permute-start(bf16[512,128]{1,0:T(8,128)(2,1)S(1)} %collective-permute-done.38), channel_id=1, source_target_pairs={{0,2},{1,3},{2,4},{3,5},{4,6},{5,7},{6,0},{7,1},{8,10},{9,11},{10,... | collective-permute-start | bytes 393224 | tf_op jit(solution)/shard_map/ppermute | solution.py:16
  125.2 11.0 %collective-permute-start.45 = (bf16[768,128]{1,0:T(8,128)(2,1)S(1)}, bf16[768,128]{1,0:T(8,128)(2,1)S(1)}, u32[]{:S(2)}, u32[]{:S(2)}) collective-permute-start(bf16[768,128]{1,0:T(8,128)(2,1)S(1)} %get-tuple-element.166), channel_id=1, source_target_pairs={{0,1},{1,0},{2,3},{3,2},{4,5},{5,4},{6,7},{7,6},{8,9},{9,8},{10,11... | collective-permute-start | bytes 589832 | tf_op jit(solution)/shard_map/ppermute | solution.py:70
  126.4 10.3 %collective-permute-start.44 = (bf16[512,128]{1,0:T(8,128)(2,1)S(1)}, bf16[512,128]{1,0:T(8,128)(2,1)S(1)}, u32[]{:S(2)}, u32[]{:S(2)}) collective-permute-start(bf16[512,128]{1,0:T(8,128)(2,1)S(1)} %collective-permute-done.40), channel_id=1, source_target_pairs={{0,2},{1,3},{2,4},{3,5},{4,6},{5,7},{6,0},{7,1},{8,10},{9,11},{10,... | collective-permute-start | bytes 393224 | tf_op jit(solution)/shard_map/ppermute | solution.py:16
  127.6 11.3 %collective-permute-start.43 = (bf16[512,128]{1,0:T(8,128)(2,1)S(1)}, bf16[512,128]{1,0:T(8,128)(2,1)S(1)}, u32[]{:S(2)}, u32[]{:S(2)}) collective-permute-start(bf16[512,128]{1,0:T(8,128)(2,1)S(1)} %collective-permute-done.39), channel_id=1, source_target_pairs={{0,2},{1,3},{2,4},{3,5},{4,6},{5,7},{6,0},{7,1},{8,10},{9,11},{10,... | collective-permute-start | bytes 393224 | tf_op jit(solution)/shard_map/ppermute | solution.py:16
  135.0 9.9 %collective-permute-start.49 = (bf16[768,128]{1,0:T(8,128)(2,1)S(1)}, bf16[768,128]{1,0:T(8,128)(2,1)S(1)}, u32[]{:S(2)}, u32[]{:S(2)}) collective-permute-start(bf16[768,128]{1,0:T(8,128)(2,1)S(1)} %get-tuple-element.172), channel_id=1, source_target_pairs={{0,1},{1,0},{2,3},{3,2},{4,5},{5,4},{6,7},{7,6},{8,9},{9,8},{10,11... | collective-permute-start | bytes 589832 | tf_op jit(solution)/shard_map/ppermute | solution.py:70
  145.5 9.7 %collective-permute-start.53 = (bf16[512,128]{1,0:T(8,128)(2,1)S(1)}, bf16[512,128]{1,0:T(8,128)(2,1)S(1)}, u32[]{:S(2)}, u32[]{:S(2)}) collective-permute-start(bf16[512,128]{1,0:T(8,128)(2,1)S(1)} %convolution_convert_fusion.2), channel_id=1, source_target_pairs={{0,2},{1,3},{2,4},{3,5},{4,6},{5,7},{6,0},{7,1},{8,10},{9,11},{10,... | collective-permute-start | bytes 393224 | tf_op jit(solution)/shard_map/ppermute | solution.py:16
  152.8 10.6 %collective-permute-start.55 = (bf16[512,128]{1,0:T(8,128)(2,1)}, bf16[512,128]{1,0:T(8,128)(2,1)S(1)}, u32[]{:S(2)}, u32[]{:S(2)}) collective-permute-start(bf16[512,128]{1,0:T(8,128)(2,1)} %add_convert_fusion.6), channel_id=1, source_target_pairs={{0,2},{1,3},{2,4},{3,5},{4,6},{5,7},{6,0},{7,1},{8,10},{9,11},{10,... | collective-permute-start | bytes 393224 | tf_op jit(solution)/shard_map/ppermute | solution.py:16
  156.3 10.4 %collective-permute-start.57 = (bf16[512,128]{1,0:T(8,128)(2,1)}, bf16[512,128]{1,0:T(8,128)(2,1)}, u32[]{:S(2)}, u32[]{:S(2)}) collective-permute-start(bf16[512,128]{1,0:T(8,128)(2,1)} %add_convert_fusion.5), channel_id=1, source_target_pairs={{0,2},{1,3},{2,4},{3,5},{4,6},{5,7},{6,0},{7,1},{8,10},{9,11},{10,... | collective-permute-start | bytes 393224 | tf_op jit(solution)/shard_map/ppermute | solution.py:16
  157.5 12.4 %collective-permute-start.60 = (bf16[512,128]{1,0:T(8,128)(2,1)}, bf16[512,128]{1,0:T(8,128)(2,1)}, u32[]{:S(2)}, u32[]{:S(2)}) collective-permute-start(bf16[512,128]{1,0:T(8,128)(2,1)} %convolution_convert_fusion), channel_id=1, source_target_pairs={{0,2},{1,3},{2,4},{3,5},{4,6},{5,7},{6,0},{7,1},{8,10},{9,11},{10,... | collective-permute-start | bytes 393224 | tf_op jit(solution)/shard_map/ppermute | solution.py:16
  159.0 12.3 %collective-permute-start.59 = (bf16[512,128]{1,0:T(8,128)(2,1)}, bf16[512,128]{1,0:T(8,128)(2,1)}, u32[]{:S(2)}, u32[]{:S(2)}) collective-permute-start(bf16[512,128]{1,0:T(8,128)(2,1)} %add_convert_fusion.4), channel_id=1, source_target_pairs={{0,2},{1,3},{2,4},{3,5},{4,6},{5,7},{6,0},{7,1},{8,10},{9,11},{10,... | collective-permute-start | bytes 393224 | tf_op jit(solution)/shard_map/ppermute | solution.py:16
  164.8 11.3 %collective-permute-start.56 = (bf16[512,128]{1,0:T(8,128)(2,1)S(1)}, bf16[512,128]{1,0:T(8,128)(2,1)S(1)}, u32[]{:S(2)}, u32[]{:S(2)}) collective-permute-start(bf16[512,128]{1,0:T(8,128)(2,1)S(1)} %get-tuple-element.197), channel_id=1, source_target_pairs={{0,16},{8,24},{16,0},{24,8},{1,17},{9,25},{17,1},{25,9},{2,18},{10... | collective-permute-start | bytes 393224 | tf_op jit(solution)/shard_map/ppermute | solution.py:16
  (63 other events, 516.9 us)

commit v3 on v2

--- a/solution.py
+++ b/solution.py
@@ -100,18 +100,18 @@
     )
     held = params.shape[1]
     results = [jnp.zeros_like(params[0]), jnp.zeros_like(momentum[0])]
-    weights = [push_weight]
+    weights = [jnp.broadcast_to(push_weight, (1, features))]
     kept, passed = [], []
 
     def debias(state, weight):
-        return (state / weight[0]).astype(narrow)
+        return (state / weight).astype(narrow)
 
     def exchange_kept(whole, step):
         kept.append(whole)
         if step == 0:
             extra = jnp.broadcast_to(weights[0], (8, features))
         else:
-            left = weights[step]
+            left = jnp.broadcast_to(weights[step], (16, features))
             parts = []
             for _ in range(3):
                 parts.append(lax.reduce_precision(left, 8, 7))
@@ -125,10 +125,12 @@
     def read_passed(step):
         got = after(passed[step], issued[-1]).astype(wide)
         passed[step] = got[:held]
-        came = got[held, :1] if step == 0 else jnp.sum(got[held : held + 3, :1], axis=0)
+        came = got[held : held + 1]
+        if step > 0:
+            came = came + got[held + 1 : held + 2] + got[held + 2 : held + 3]
         weights.append(0.5 * weights[step] + 0.5 * came)
 
-    first = [[debias(chunk(params[0], c), push_weight)] for c in range(CHUNKS)]
+    first = [[debias(chunk(params[0], c), push_weight[0])] for c in range(CHUNKS)]
     for back in range(1, half):
         for c in range(CHUNKS):
             first[c].append(from_behind(first[c][-1], "fsdp", 2))
@@ -160,7 +162,7 @@
             total = partial(1)
             for back in range(2, half + 1):
                 arrived = yield total.astype(narrow), "line"
-                if c == 0 and back == half:
+                if step > 0 and c == 0 and back == half:
                     read_passed(step)
                 total = arrived.astype(wide) + partial(back % half)
             behind = yield total.astype(narrow), "group"
@@ -170,14 +172,14 @@
             if step == STEPS - 1:
                 break
             later.append(state - (0.2 * 0.9) * moment)
-            pieces = [debias(state, weights[step + 1])]
+            pieces = [debias(state, chunk(weights[step + 1], c))]
             for _ in range(half - 1):
                 pieces.append((yield pieces[-1], "line"))
             keys = sum(
                 jnp.dot(column_block(back), piece, preferred_element_type=wide)
                 for back, piece in enumerate(pieces)
             )
-        fresh = [state / weights[STEPS][0], moment]
+        fresh = [state / chunk(weights[STEPS], c), moment]
         for i in range(2):
             results[i] = lax.dynamic_update_slice(results[i], fresh[i], (0, c * part))
         yield None, None
@@ -190,6 +192,9 @@
             came[c] = after(came[c], issued[-1])
         value, link = streams[c].send(came[c])
         came[c] = send(value, link, 2 ** mixings[c])
+        if len(issued) == 2:
+            read_passed(0)
+            issued.append(weights[1])
         mixings[c] += link == "group"
         if len(later) == CHUNKS:
             exchange_kept(jnp.concatenate(later, axis=1), mixings[c])

time: 194 us -> 184 us (0.948)
  waiting for transfers between devices: 76.9 us -> 97.6 us
  starting transfers between devices: 49.5 us -> 36.8 us
  matrix products: 31.2 us -> 24.7 us
  other arithmetic: 17.8 us -> 12.6 us
  between operations: 6.34 us -> 2.17 us
    ppermute x58, waiting for transfers between devices: 72.5 us -> 93.2 us  [from_behind(): return lax.ppermute(value, axis, pairs)]
    ppermute x58, starting transfers between devices: 37.3 us -> 26.5 us  [from_behind(): return lax.ppermute(value, axis, pairs)]
    dot_general x32, matrix products: 19.7 us -> 13.1 us  [partial(): lax.dot_general(column_block(back), grad_out, contract, preferred_element...]
    another operation x4, other arithmetic: 3.29 us -> 0.48 us
    ppermute x8, starting transfers between devices: 9.26 us -> 7.31 us  [send(): return lax.ppermute(value, 'fsdp', [(i, i ^ 1) for i in range(count)])]
  transfers between devices with their start and end apart: 67 -> 67, of which waited for: 38 -> 45; matrix products, arithmetic and copies ran while one was open for 28% -> 23% of each run, Pallas kernels for 0% -> 0%
where the time goes in v3:
time: 184 us; the launch traced here: 183 us
  waiting for transfers between devices  97.6 us (53%)
  starting transfers between devices  36.8 us (20%)
  matrix products  24.7 us (13%)
  other arithmetic  12.6 us (7%)
  local copies, waits for them, and re-layouts  9.39 us (5%)
  between operations  2.17 us (1%)
    ppermute x58, waiting for transfers between devices, from_behind(): return lax.ppermute(value, axis, pairs)  93.2 us
    ppermute x58, starting transfers between devices, from_behind(): return lax.ppermute(value, axis, pairs)  26.5 us
    dot_general x32, matrix products, partial(): lax.dot_general(column_block(back), grad_out, contract, preferred_element...  13.1 us
    dot_general x16, matrix products, stream(): jnp.dot(column_block(back), piece, preferred_element_type=wide)  9.62 us
    ppermute x8, starting transfers between devices, send(): return lax.ppermute(value, 'fsdp', [(i, i ^ 1) for i in range(count)])  7.31 us
    ppermute x8, waiting for transfers between devices, send(): return lax.ppermute(value, 'fsdp', [(i, i ^ 1) for i in range(count)])  4.33 us
  transfers between devices with their start and end apart: 67, of which 45 were waited for; matrix products, arithmetic and copies ran while one was open for 23% of the time, Pallas kernels for 0%

profile of v3, /device:TPU:0, one launch (start us, length us, event | category | flops | bytes accessed | tf_op | source)
XLA Modules:
  0.0 183.2 jit_solution(14057657779768709292)
XLA Ops:
  3.6 2.9 %collective-permute-start.1 = (bf16[384,2048]{1,0:T(8,128)(2,1)}, bf16[384,2048]{1,0:T(8,128)(2,1)}, u32[]{:S(2)}, u32[]{:S(2)}) collective-permute-start(bf16[384,2048]{1,0:T(8,128)(2,1)} %pad_maximum_fusion), channel_id=1, source_target_pairs={{0,1},{1,0},{2,3},{3,2},{4,5},{5,4},{6,7},{7,6},{8,9},{9,8},{10,11... | collective-permute-start | bytes 4718600 | tf_op jit(solution)/shard_map/ppermute | solution.py:89
  16.4 2.1 %collective-permute-done.5 = bf16[512,128]{1,0:T(8,128)(2,1)} collective-permute-done((bf16[512,128]{1,0:T(8,128)(2,1)S(1)}, bf16[512,128]{1,0:T(8,128)(2,1)}, u32[]{:S(2)}, u32[]{:S(2)}) %collective-permute-start.5) | collective-permute-done | bytes 131104 | tf_op jit(solution)/shard_map/ppermute | solution.py:16
  19.1 2.2 %collective-permute-done.10 = bf16[512,128]{1,0:T(8,128)(2,1)} collective-permute-done((bf16[512,128]{1,0:T(8,128)(2,1)S(1)}, bf16[512,128]{1,0:T(8,128)(2,1)}, u32[]{:S(2)}, u32[]{:S(2)}) %collective-permute-start.10) | collective-permute-done | bytes 131104 | tf_op jit(solution)/shard_map/ppermute | solution.py:16
  21.3 2.8 %collective-permute-done.13 = bf16[512,128]{1,0:T(8,128)(2,1)} collective-permute-done((bf16[512,128]{1,0:T(8,128)(2,1)S(1)}, bf16[512,128]{1,0:T(8,128)(2,1)}, u32[]{:S(2)}, u32[]{:S(2)}) %collective-permute-start.13) | collective-permute-done | bytes 131104 | tf_op jit(solution)/shard_map/ppermute | solution.py:16
  24.2 2.8 %collective-permute-done.3 = bf16[512,128]{1,0:T(8,128)(2,1)} collective-permute-done((bf16[512,128]{1,0:T(8,128)(2,1)}, bf16[512,128]{1,0:T(8,128)(2,1)}, u32[]{:S(2)}, u32[]{:S(2)}) %collective-permute-start.3) | collective-permute-done | bytes 131104 | tf_op jit(solution)/shard_map/ppermute | solution.py:16
  27.0 2.8 %collective-permute-done.6 = bf16[512,128]{1,0:T(8,128)(2,1)} collective-permute-done((bf16[512,128]{1,0:T(8,128)(2,1)}, bf16[512,128]{1,0:T(8,128)(2,1)}, u32[]{:S(2)}, u32[]{:S(2)}) %collective-permute-start.6) | collective-permute-done | bytes 131104 | tf_op jit(solution)/shard_map/ppermute | solution.py:16
  32.9 2.5 %collective-permute-done.14 = bf16[512,128]{1,0:T(8,128)(2,1)} collective-permute-done((bf16[512,128]{1,0:T(8,128)(2,1)}, bf16[512,128]{1,0:T(8,128)(2,1)}, u32[]{:S(2)}, u32[]{:S(2)}) %collective-permute-start.14) | collective-permute-done | bytes 131104 | tf_op jit(solution)/shard_map/ppermute | solution.py:16
  35.4 2.8 %collective-permute-done.4 = bf16[512,128]{1,0:T(8,128)(2,1)} collective-permute-done((bf16[512,128]{1,0:T(8,128)(2,1)}, bf16[512,128]{1,0:T(8,128)(2,1)}, u32[]{:S(2)}, u32[]{:S(2)}) %collective-permute-start.4) | collective-permute-done | bytes 131104 | tf_op jit(solution)/shard_map/ppermute | solution.py:16
  41.0 2.7 %collective-permute-done.12 = bf16[512,128]{1,0:T(8,128)(2,1)S(1)} collective-permute-done((bf16[512,128]{1,0:T(8,128)(2,1)}, bf16[512,128]{1,0:T(8,128)(2,1)S(1)}, u32[]{:S(2)}, u32[]{:S(2)}) %collective-permute-start.12) | collective-permute-done | bytes 131104 | tf_op jit(solution)/shard_map/ppermute | solution.py:16
  53.4 4.3 %collective-permute-done.8 = bf16[768,128]{1,0:T(8,128)(2,1)S(1)} collective-permute-done((bf16[768,128]{1,0:T(8,128)(2,1)S(1)}, bf16[768,128]{1,0:T(8,128)(2,1)S(1)}, u32[]{:S(2)}, u32[]{:S(2)}) %collective-permute-start.8) | collective-permute-done | bytes 196640 | tf_op jit(solution)/shard_map/ppermute | solution.py:70
  64.6 3.0 %collective-permute-done.9 = bf16[512,128]{1,0:T(8,128)(2,1)S(1)} collective-permute-done((bf16[512,128]{1,0:T(8,128)(2,1)S(1)}, bf16[512,128]{1,0:T(8,128)(2,1)S(1)}, u32[]{:S(2)}, u32[]{:S(2)}) %collective-permute-start.9) | collective-permute-done | bytes 131104 | tf_op jit(solution)/shard_map/ppermute | solution.py:16
  71.4 3.5 %collective-permute-done.17 = bf16[512,128]{1,0:T(8,128)(2,1)S(1)} collective-permute-done((bf16[512,128]{1,0:T(8,128)(2,1)S(1)}, bf16[512,128]{1,0:T(8,128)(2,1)S(1)}, u32[]{:S(2)}, u32[]{:S(2)}) %collective-permute-start.17) | collective-permute-done | bytes 131104 | tf_op jit(solution)/shard_map/ppermute | solution.py:16
  78.3 2.3 %collective-permute-done.21 = bf16[512,128]{1,0:T(8,128)(2,1)S(1)} collective-permute-done((bf16[512,128]{1,0:T(8,128)(2,1)S(1)}, bf16[512,128]{1,0:T(8,128)(2,1)S(1)}, u32[]{:S(2)}, u32[]{:S(2)}) %collective-permute-start.21) | collective-permute-done | bytes 131104 | tf_op jit(solution)/shard_map/ppermute | solution.py:16
  81.0 1.7 collective-permute-start.27
  84.1 2.1 %collective-permute-done.26 = bf16[512,128]{1,0:T(8,128)(2,1)S(1)} collective-permute-done((bf16[512,128]{1,0:T(8,128)(2,1)S(1)}, bf16[512,128]{1,0:T(8,128)(2,1)S(1)}, u32[]{:S(2)}, u32[]{:S(2)}) %collective-permute-start.26) | collective-permute-done | bytes 131104 | tf_op jit(solution)/shard_map/ppermute | solution.py:16
  89.8 5.0 %collective-permute-done.30 = bf16[512,128]{1,0:T(8,128)(2,1)S(1)} collective-permute-done((bf16[512,128]{1,0:T(8,128)(2,1)S(1)}, bf16[512,128]{1,0:T(8,128)(2,1)S(1)}, u32[]{:S(2)}, u32[]{:S(2)}) %collective-permute-start.30) | collective-permute-done | bytes 131104 | tf_op jit(solution)/shard_map/ppermute | solution.py:16
  95.3 2.3 %collective-permute-done.29 = bf16[512,128]{1,0:T(8,128)(2,1)S(1)} collective-permute-done((bf16[512,128]{1,0:T(8,128)(2,1)S(1)}, bf16[512,128]{1,0:T(8,128)(2,1)S(1)}, u32[]{:S(2)}, u32[]{:S(2)}) %collective-permute-start.29) | collective-permute-done | bytes 131104 | tf_op jit(solution)/shard_map/ppermute | solution.py:16
  98.3 2.0 %collective-permute-done.33 = bf16[512,128]{1,0:T(8,128)(2,1)S(1)} collective-permute-done((bf16[512,128]{1,0:T(8,128)(2,1)S(1)}, bf16[512,128]{1,0:T(8,128)(2,1)S(1)}, u32[]{:S(2)}, u32[]{:S(2)}) %collective-permute-start.33) | collective-permute-done | bytes 131104 | tf_op jit(solution)/shard_map/ppermute | solution.py:16
  103.1 3.3 %collective-permute-done.36 = bf16[512,128]{1,0:T(8,128)(2,1)S(1)} collective-permute-done((bf16[512,128]{1,0:T(8,128)(2,1)S(1)}, bf16[512,128]{1,0:T(8,128)(2,1)S(1)}, u32[]{:S(2)}, u32[]{:S(2)}) %collective-permute-start.36) | collective-permute-done | bytes 131104 | tf_op jit(solution)/shard_map/ppermute | solution.py:16
  106.4 2.8 %collective-permute-done.35 = bf16[512,128]{1,0:T(8,128)(2,1)S(1)} collective-permute-done((bf16[512,128]{1,0:T(8,128)(2,1)S(1)}, bf16[512,128]{1,0:T(8,128)(2,1)S(1)}, u32[]{:S(2)}, u32[]{:S(2)}) %collective-permute-start.35) | collective-permute-done | bytes 131104 | tf_op jit(solution)/shard_map/ppermute | solution.py:16
  113.0 1.9 %collective-permute-done.42 = bf16[512,128]{1,0:T(8,128)(2,1)S(1)} collective-permute-done((bf16[512,128]{1,0:T(8,128)(2,1)S(1)}, bf16[512,128]{1,0:T(8,128)(2,1)S(1)}, u32[]{:S(2)}, u32[]{:S(2)}) %collective-permute-start.42) | collective-permute-done | bytes 131104 | tf_op jit(solution)/shard_map/ppermute | solution.py:16
  114.9 2.8 %collective-permute-done.41 = bf16[512,128]{1,0:T(8,128)(2,1)S(1)} collective-permute-done((bf16[512,128]{1,0:T(8,128)(2,1)S(1)}, bf16[512,128]{1,0:T(8,128)(2,1)S(1)}, u32[]{:S(2)}, u32[]{:S(2)}) %collective-permute-start.41) | collective-permute-done | bytes 131104 | tf_op jit(solution)/shard_map/ppermute | solution.py:16
  123.2 5.9 %collective-permute-done.46 = bf16[512,128]{1,0:T(8,128)(2,1)S(1)} collective-permute-done((bf16[512,128]{1,0:T(8,128)(2,1)S(1)}, bf16[512,128]{1,0:T(8,128)(2,1)S(1)}, u32[]{:S(2)}, u32[]{:S(2)}) %collective-permute-start.46) | collective-permute-done | bytes 131104 | tf_op jit(solution)/shard_map/ppermute | solution.py:16
  135.7 3.0 %collective-permute-done.50 = bf16[512,128]{1,0:T(8,128)(2,1)S(1)} collective-permute-done((bf16[512,128]{1,0:T(8,128)(2,1)S(1)}, bf16[512,128]{1,0:T(8,128)(2,1)S(1)}, u32[]{:S(2)}, u32[]{:S(2)}) %collective-permute-start.50) | collective-permute-done | bytes 131104 | tf_op jit(solution)/shard_map/ppermute | solution.py:16
  139.6 1.9 %collective-permute-start.53 = (bf16[512,128]{1,0:T(8,128)(2,1)S(1)}, bf16[512,128]{1,0:T(8,128)(2,1)S(1)}, u32[]{:S(2)}, u32[]{:S(2)}) collective-permute-start(bf16[512,128]{1,0:T(8,128)(2,1)S(1)} %convolution_convert_fusion.2), channel_id=1, source_target_pairs={{0,2},{1,3},{2,4},{3,5},{4,6},{5,7},{6,0},{7,1},{8,10},{9,11},{10,... | collective-permute-start | bytes 393224 | tf_op jit(solution)/shard_map/ppermute | solution.py:16
  154.1 2.1 %collective-permute-done.55 = bf16[512,128]{1,0:T(8,128)(2,1)S(1)} collective-permute-done((bf16[512,128]{1,0:T(8,128)(2,1)S(1)}, bf16[512,128]{1,0:T(8,128)(2,1)S(1)}, u32[]{:S(2)}, u32[]{:S(2)}) %collective-permute-start.55) | collective-permute-done | bytes 131104 | tf_op jit(solution)/shard_map/ppermute | solution.py:16
  160.2 1.8 collective-permute-done.59
  163.1 3.1 %collective-permute-done.58 = bf16[512,128]{1,0:T(8,128)(2,1)S(1)} collective-permute-done((bf16[512,128]{1,0:T(8,128)(2,1)S(1)}, bf16[512,128]{1,0:T(8,128)(2,1)S(1)}, u32[]{:S(2)}, u32[]{:S(2)}) %collective-permute-start.58) | collective-permute-done | bytes 131104 | tf_op jit(solution)/shard_map/ppermute | solution.py:16
  166.6 2.1 %collective-permute-start.61 = (bf16[512,128]{1,0:T(8,128)(2,1)S(1)}, bf16[512,128]{1,0:T(8,128)(2,1)S(1)}, u32[]{:S(2)}, u32[]{:S(2)}) collective-permute-start(bf16[512,128]{1,0:T(8,128)(2,1)S(1)} %get-tuple-element.205), channel_id=1, source_target_pairs={{0,16},{8,24},{16,0},{24,8},{1,17},{9,25},{17,1},{25,9},{2,18},{10... | collective-permute-start | bytes 393224 | tf_op jit(solution)/shard_map/ppermute | solution.py:16
  170.0 2.8 %collective-permute-start.64 = (bf16[512,128]{1,0:T(8,128)(2,1)S(1)}, bf16[512,128]{1,0:T(8,128)(2,1)S(1)}, u32[]{:S(2)}, u32[]{:S(2)}) collective-permute-start(bf16[512,128]{1,0:T(8,128)(2,1)S(1)} %get-tuple-element.209), channel_id=1, source_target_pairs={{0,16},{8,24},{16,0},{24,8},{1,17},{9,25},{17,1},{25,9},{2,18},{10... | collective-permute-start | bytes 393224 | tf_op jit(solution)/shard_map/ppermute | solution.py:16
  173.0 3.4 %collective-permute-done.65 = bf16[512,128]{1,0:T(8,128)(2,1)S(1)} collective-permute-done((bf16[512,128]{1,0:T(8,128)(2,1)S(1)}, bf16[512,128]{1,0:T(8,128)(2,1)S(1)}, u32[]{:S(2)}, u32[]{:S(2)}) %collective-permute-start.65) | collective-permute-done | bytes 131104 | tf_op jit(solution)/shard_map/ppermute | solution.py:16
  178.5 3.2 %collective-permute-done.66 = bf16[512,128]{1,0:T(8,128)(2,1)S(1)} collective-permute-done((bf16[512,128]{1,0:T(8,128)(2,1)S(1)}, bf16[512,128]{1,0:T(8,128)(2,1)S(1)}, u32[]{:S(2)}, u32[]{:S(2)}) %collective-permute-start.66) | collective-permute-done | bytes 131104 | tf_op jit(solution)/shard_map/ppermute | solution.py:16
  (215 shorter events, 90.9 us)
Async XLA Ops:
  3.6 42.8 %collective-permute-start.1 = (bf16[384,2048]{1,0:T(8,128)(2,1)}, bf16[384,2048]{1,0:T(8,128)(2,1)}, u32[]{:S(2)}, u32[]{:S(2)}) collective-permute-start(bf16[384,2048]{1,0:T(8,128)(2,1)} %pad_maximum_fusion), channel_id=1, source_target_pairs={{0,1},{1,0},{2,3},{3,2},{4,5},{5,4},{6,7},{7,6},{8,9},{9,8},{10,11... | collective-permute-start | bytes 4718600 | tf_op jit(solution)/shard_map/ppermute | solution.py:89
  9.0 9.6 %collective-permute-start.5 = (bf16[512,128]{1,0:T(8,128)(2,1)S(1)}, bf16[512,128]{1,0:T(8,128)(2,1)}, u32[]{:S(2)}, u32[]{:S(2)}) collective-permute-start(bf16[512,128]{1,0:T(8,128)(2,1)S(1)} %get-tuple-element.238), channel_id=1, source_target_pairs={{0,2},{1,3},{2,4},{3,5},{4,6},{5,7},{6,0},{7,1},{8,10},{9,11},{10,... | collective-permute-start | bytes 393224 | tf_op jit(solution)/shard_map/ppermute | solution.py:16
  10.6 10.8 %collective-permute-start.10 = (bf16[512,128]{1,0:T(8,128)(2,1)S(1)}, bf16[512,128]{1,0:T(8,128)(2,1)}, u32[]{:S(2)}, u32[]{:S(2)}) collective-permute-start(bf16[512,128]{1,0:T(8,128)(2,1)S(1)} %get-tuple-element.237), channel_id=1, source_target_pairs={{0,2},{1,3},{2,4},{3,5},{4,6},{5,7},{6,0},{7,1},{8,10},{9,11},{10,... | collective-permute-start | bytes 393224 | tf_op jit(solution)/shard_map/ppermute | solution.py:16
  12.1 12.0 %collective-permute-start.13 = (bf16[512,128]{1,0:T(8,128)(2,1)S(1)}, bf16[512,128]{1,0:T(8,128)(2,1)}, u32[]{:S(2)}, u32[]{:S(2)}) collective-permute-start(bf16[512,128]{1,0:T(8,128)(2,1)S(1)} %get-tuple-element.240), channel_id=1, source_target_pairs={{0,2},{1,3},{2,4},{3,5},{4,6},{5,7},{6,0},{7,1},{8,10},{9,11},{10,... | collective-permute-start | bytes 393224 | tf_op jit(solution)/shard_map/ppermute | solution.py:16
  15.7 11.2 %collective-permute-start.3 = (bf16[512,128]{1,0:T(8,128)(2,1)}, bf16[512,128]{1,0:T(8,128)(2,1)}, u32[]{:S(2)}, u32[]{:S(2)}) collective-permute-start(bf16[512,128]{1,0:T(8,128)(2,1)} %collective-permute-done.2), channel_id=1, source_target_pairs={{0,2},{1,3},{2,4},{3,5},{4,6},{5,7},{6,0},{7,1},{8,10},{9,11},{10,... | collective-permute-start | bytes 393224 | tf_op jit(solution)/shard_map/ppermute | solution.py:16
  18.5 11.2 %collective-permute-start.6 = (bf16[512,128]{1,0:T(8,128)(2,1)}, bf16[512,128]{1,0:T(8,128)(2,1)}, u32[]{:S(2)}, u32[]{:S(2)}) collective-permute-start(bf16[512,128]{1,0:T(8,128)(2,1)} %collective-permute-done.5), channel_id=1, source_target_pairs={{0,2},{1,3},{2,4},{3,5},{4,6},{5,7},{6,0},{7,1},{8,10},{9,11},{10,... | collective-permute-start | bytes 393224 | tf_op jit(solution)/shard_map/ppermute | solution.py:16
  21.3 11.4 %collective-permute-start.11 = (bf16[512,128]{1,0:T(8,128)(2,1)}, bf16[512,128]{1,0:T(8,128)(2,1)}, u32[]{:S(2)}, u32[]{:S(2)}) collective-permute-start(bf16[512,128]{1,0:T(8,128)(2,1)} %collective-permute-done.10), channel_id=1, source_target_pairs={{0,2},{1,3},{2,4},{3,5},{4,6},{5,7},{6,0},{7,1},{8,10},{9,11},{10,... | collective-permute-start | bytes 393224 | tf_op jit(solution)/shard_map/ppermute | solution.py:16
  24.1 11.2 %collective-permute-start.14 = (bf16[512,128]{1,0:T(8,128)(2,1)}, bf16[512,128]{1,0:T(8,128)(2,1)}, u32[]{:S(2)}, u32[]{:S(2)}) collective-permute-start(bf16[512,128]{1,0:T(8,128)(2,1)} %collective-permute-done.13), channel_id=1, source_target_pairs={{0,2},{1,3},{2,4},{3,5},{4,6},{5,7},{6,0},{7,1},{8,10},{9,11},{10,... | collective-permute-start | bytes 393224 | tf_op jit(solution)/shard_map/ppermute | solution.py:16
  27.0 11.2 %collective-permute-start.4 = (bf16[512,128]{1,0:T(8,128)(2,1)}, bf16[512,128]{1,0:T(8,128)(2,1)}, u32[]{:S(2)}, u32[]{:S(2)}) collective-permute-start(bf16[512,128]{1,0:T(8,128)(2,1)} %collective-permute-done.3), channel_id=1, source_target_pairs={{0,2},{1,3},{2,4},{3,5},{4,6},{5,7},{6,0},{7,1},{8,10},{9,11},{10,... | collective-permute-start | bytes 393224 | tf_op jit(solution)/shard_map/ppermute | solution.py:16
  29.8 9.9 %collective-permute-start.7 = (bf16[512,128]{1,0:T(8,128)(2,1)}, bf16[512,128]{1,0:T(8,128)(2,1)}, u32[]{:S(2)}, u32[]{:S(2)}) collective-permute-start(bf16[512,128]{1,0:T(8,128)(2,1)} %collective-permute-done.6), channel_id=1, source_target_pairs={{0,2},{1,3},{2,4},{3,5},{4,6},{5,7},{6,0},{7,1},{8,10},{9,11},{10,... | collective-permute-start | bytes 393224 | tf_op jit(solution)/shard_map/ppermute | solution.py:16
  32.8 19.5 %collective-permute-start = (f32[520,512]{1,0:T(8,128)S(1)}, f32[520,512]{1,0:T(8,128)S(1)}, u32[]{:S(2)}, u32[]{:S(2)}) collective-permute-start(f32[520,512]{1,0:T(8,128)S(1)} %concatenate.35), channel_id=1, source_target_pairs={{0,8},{8,16},{16,24},{24,0},{1,9},{9,17},{17,25},{25,1},{2,10},{10... | collective-permute-start | bytes 3194888 | tf_op jit(solution)/shard_map/ppermute | solution.py:16
  50.7 9.7 %collective-permute-start.16 = (bf16[768,128]{1,0:T(8,128)(2,1)S(1)}, bf16[768,128]{1,0:T(8,128)(2,1)S(1)}, u32[]{:S(2)}, u32[]{:S(2)}) collective-permute-start(bf16[768,128]{1,0:T(8,128)(2,1)S(1)} %get-tuple-element.110), channel_id=1, source_target_pairs={{0,1},{1,0},{2,3},{3,2},{4,5},{5,4},{6,7},{7,6},{8,9},{9,8},{10,11... | collective-permute-start | bytes 589832 | tf_op jit(solution)/shard_map/ppermute | solution.py:70
  63.1 12.4 %collective-permute-start.23 = (bf16[768,128]{1,0:T(8,128)(2,1)S(1)}, bf16[768,128]{1,0:T(8,128)(2,1)S(1)}, u32[]{:S(2)}, u32[]{:S(2)}) collective-permute-start(bf16[768,128]{1,0:T(8,128)(2,1)S(1)} %get-tuple-element.117), channel_id=1, source_target_pairs={{0,1},{1,0},{2,3},{3,2},{4,5},{5,4},{6,7},{7,6},{8,9},{9,8},{10,11... | collective-permute-start | bytes 589832 | tf_op jit(solution)/shard_map/ppermute | solution.py:70
  70.9 9.7 %collective-permute-start.21 = (bf16[512,128]{1,0:T(8,128)(2,1)S(1)}, bf16[512,128]{1,0:T(8,128)(2,1)S(1)}, u32[]{:S(2)}, u32[]{:S(2)}) collective-permute-start(bf16[512,128]{1,0:T(8,128)(2,1)S(1)} %add_convert_fusion.14), channel_id=1, source_target_pairs={{0,2},{1,3},{2,4},{3,5},{4,6},{5,7},{6,0},{7,1},{8,10},{9,11},{10,... | collective-permute-start | bytes 393224 | tf_op jit(solution)/shard_map/ppermute | solution.py:16
  77.0 9.2 %collective-permute-start.26 = (bf16[512,128]{1,0:T(8,128)(2,1)S(1)}, bf16[512,128]{1,0:T(8,128)(2,1)S(1)}, u32[]{:S(2)}, u32[]{:S(2)}) collective-permute-start(bf16[512,128]{1,0:T(8,128)(2,1)S(1)} %convolution_convert_fusion.4), channel_id=1, source_target_pairs={{0,2},{1,3},{2,4},{3,5},{4,6},{5,7},{6,0},{7,1},{8,10},{9,11},{10,... | collective-permute-start | bytes 393224 | tf_op jit(solution)/shard_map/ppermute | solution.py:16
  78.2 9.3 %collective-permute-start.25 = (bf16[512,128]{1,0:T(8,128)(2,1)S(1)}, bf16[512,128]{1,0:T(8,128)(2,1)S(1)}, u32[]{:S(2)}, u32[]{:S(2)}) collective-permute-start(bf16[512,128]{1,0:T(8,128)(2,1)S(1)} %add_convert_fusion.12), channel_id=1, source_target_pairs={{0,2},{1,3},{2,4},{3,5},{4,6},{5,7},{6,0},{7,1},{8,10},{9,11},{10,... | collective-permute-start | bytes 393224 | tf_op jit(solution)/shard_map/ppermute | solution.py:16
  87.9 9.7 %collective-permute-start.29 = (bf16[512,128]{1,0:T(8,128)(2,1)S(1)}, bf16[512,128]{1,0:T(8,128)(2,1)S(1)}, u32[]{:S(2)}, u32[]{:S(2)}) collective-permute-start(bf16[512,128]{1,0:T(8,128)(2,1)S(1)} %add_convert_fusion.9), channel_id=1, source_target_pairs={{0,2},{1,3},{2,4},{3,5},{4,6},{5,7},{6,0},{7,1},{8,10},{9,11},{10,... | collective-permute-start | bytes 393224 | tf_op jit(solution)/shard_map/ppermute | solution.py:16
  88.6 11.7 %collective-permute-start.33 = (bf16[512,128]{1,0:T(8,128)(2,1)S(1)}, bf16[512,128]{1,0:T(8,128)(2,1)S(1)}, u32[]{:S(2)}, u32[]{:S(2)}) collective-permute-start(bf16[512,128]{1,0:T(8,128)(2,1)S(1)} %divide_convert_fusion.3), channel_id=1, source_target_pairs={{0,2},{1,3},{2,4},{3,5},{4,6},{5,7},{6,0},{7,1},{8,10},{9,11},{10,... | collective-permute-start | bytes 393224 | tf_op jit(solution)/shard_map/ppermute | solution.py:16
  100.4 8.9 %collective-permute-start.35 = (bf16[512,128]{1,0:T(8,128)(2,1)S(1)}, bf16[512,128]{1,0:T(8,128)(2,1)S(1)}, u32[]{:S(2)}, u32[]{:S(2)}) collective-permute-start(bf16[512,128]{1,0:T(8,128)(2,1)S(1)} %collective-permute-done.33), channel_id=1, source_target_pairs={{0,2},{1,3},{2,4},{3,5},{4,6},{5,7},{6,0},{7,1},{8,10},{9,11},{10,... | collective-permute-start | bytes 393224 | tf_op jit(solution)/shard_map/ppermute | solution.py:16
  103.1 9.0 %collective-permute-start.38 = (bf16[512,128]{1,0:T(8,128)(2,1)S(1)}, bf16[512,128]{1,0:T(8,128)(2,1)S(1)}, u32[]{:S(2)}, u32[]{:S(2)}) collective-permute-start(bf16[512,128]{1,0:T(8,128)(2,1)S(1)} %divide_convert_fusion.1), channel_id=1, source_target_pairs={{0,2},{1,3},{2,4},{3,5},{4,6},{5,7},{6,0},{7,1},{8,10},{9,11},{10,... | collective-permute-start | bytes 393224 | tf_op jit(solution)/shard_map/ppermute | solution.py:16
  109.8 10.7 %collective-permute-start.40 = (bf16[512,128]{1,0:T(8,128)(2,1)S(1)}, bf16[512,128]{1,0:T(8,128)(2,1)S(1)}, u32[]{:S(2)}, u32[]{:S(2)}) collective-permute-start(bf16[512,128]{1,0:T(8,128)(2,1)S(1)} %get-tuple-element.159), channel_id=1, source_target_pairs={{0,2},{1,3},{2,4},{3,5},{4,6},{5,7},{6,0},{7,1},{8,10},{9,11},{10,... | collective-permute-start | bytes 393224 | tf_op jit(solution)/shard_map/ppermute | solution.py:16
  109.9 44.0 %collective-permute-start.37 = (bf16[528,512]{1,0:T(8,128)(2,1)S(1)}, bf16[528,512]{1,0:T(8,128)(2,1)S(1)}, u32[]{:S(2)}, u32[]{:S(2)}) collective-permute-start(bf16[528,512]{1,0:T(8,128)(2,1)S(1)} %pad_maximum_fusion.1), channel_id=1, source_target_pairs={{0,16},{8,24},{16,0},{24,8},{1,17},{9,25},{17,1},{25,9},{2,18},{10... | collective-permute-start | bytes 1622024 | tf_op jit(solution)/shard_map/ppermute | solution.py:16
  112.0 10.8 %collective-permute-start.39 = (bf16[512,128]{1,0:T(8,128)(2,1)S(1)}, bf16[512,128]{1,0:T(8,128)(2,1)S(1)}, u32[]{:S(2)}, u32[]{:S(2)}) collective-permute-start(bf16[512,128]{1,0:T(8,128)(2,1)S(1)} %collective-permute-done.38), channel_id=1, source_target_pairs={{0,2},{1,3},{2,4},{3,5},{4,6},{5,7},{6,0},{7,1},{8,10},{9,11},{10,... | collective-permute-start | bytes 393224 | tf_op jit(solution)/shard_map/ppermute | solution.py:16
  120.9 10.5 %collective-permute-start.45 = (bf16[768,128]{1,0:T(8,128)(2,1)S(1)}, bf16[768,128]{1,0:T(8,128)(2,1)S(1)}, u32[]{:S(2)}, u32[]{:S(2)}) collective-permute-start(bf16[768,128]{1,0:T(8,128)(2,1)S(1)} %get-tuple-element.166), channel_id=1, source_target_pairs={{0,1},{1,0},{2,3},{3,2},{4,5},{5,4},{6,7},{7,6},{8,9},{9,8},{10,11... | collective-permute-start | bytes 589832 | tf_op jit(solution)/shard_map/ppermute | solution.py:70
  121.6 10.3 %collective-permute-start.44 = (bf16[512,128]{1,0:T(8,128)(2,1)S(1)}, bf16[512,128]{1,0:T(8,128)(2,1)S(1)}, u32[]{:S(2)}, u32[]{:S(2)}) collective-permute-start(bf16[512,128]{1,0:T(8,128)(2,1)S(1)} %collective-permute-done.40), channel_id=1, source_target_pairs={{0,2},{1,3},{2,4},{3,5},{4,6},{5,7},{6,0},{7,1},{8,10},{9,11},{10,... | collective-permute-start | bytes 393224 | tf_op jit(solution)/shard_map/ppermute | solution.py:16
  122.8 10.5 %collective-permute-start.43 = (bf16[512,128]{1,0:T(8,128)(2,1)S(1)}, bf16[512,128]{1,0:T(8,128)(2,1)S(1)}, u32[]{:S(2)}, u32[]{:S(2)}) collective-permute-start(bf16[512,128]{1,0:T(8,128)(2,1)S(1)} %collective-permute-done.39), channel_id=1, source_target_pairs={{0,2},{1,3},{2,4},{3,5},{4,6},{5,7},{6,0},{7,1},{8,10},{9,11},{10,... | collective-permute-start | bytes 393224 | tf_op jit(solution)/shard_map/ppermute | solution.py:16
  131.9 9.6 %collective-permute-start.48 = (bf16[512,128]{1,0:T(8,128)(2,1)S(1)}, bf16[512,128]{1,0:T(8,128)(2,1)S(1)}, u32[]{:S(2)}, u32[]{:S(2)}) collective-permute-start(bf16[512,128]{1,0:T(8,128)(2,1)S(1)} %collective-permute-done.44), channel_id=1, source_target_pairs={{0,2},{1,3},{2,4},{3,5},{4,6},{5,7},{6,0},{7,1},{8,10},{9,11},{10,... | collective-permute-start | bytes 393224 | tf_op jit(solution)/shard_map/ppermute | solution.py:16
  135.1 9.6 %collective-permute-start.47 = (bf16[768,128]{1,0:T(8,128)(2,1)S(1)}, bf16[768,128]{1,0:T(8,128)(2,1)S(1)}, u32[]{:S(2)}, u32[]{:S(2)}) collective-permute-start(bf16[768,128]{1,0:T(8,128)(2,1)S(1)} %get-tuple-element.178), channel_id=1, source_target_pairs={{0,1},{1,0},{2,3},{3,2},{4,5},{5,4},{6,7},{7,6},{8,9},{9,8},{10,11... | collective-permute-start | bytes 589832 | tf_op jit(solution)/shard_map/ppermute | solution.py:70
  139.6 10.0 %collective-permute-start.53 = (bf16[512,128]{1,0:T(8,128)(2,1)S(1)}, bf16[512,128]{1,0:T(8,128)(2,1)S(1)}, u32[]{:S(2)}, u32[]{:S(2)}) collective-permute-start(bf16[512,128]{1,0:T(8,128)(2,1)S(1)} %convolution_convert_fusion.2), channel_id=1, source_target_pairs={{0,2},{1,3},{2,4},{3,5},{4,6},{5,7},{6,0},{7,1},{8,10},{9,11},{10,... | collective-permute-start | bytes 393224 | tf_op jit(solution)/shard_map/ppermute | solution.py:16
  147.2 9.0 %collective-permute-start.55 = (bf16[512,128]{1,0:T(8,128)(2,1)S(1)}, bf16[512,128]{1,0:T(8,128)(2,1)S(1)}, u32[]{:S(2)}, u32[]{:S(2)}) collective-permute-start(bf16[512,128]{1,0:T(8,128)(2,1)S(1)} %add_convert_fusion.6), channel_id=1, source_target_pairs={{0,2},{1,3},{2,4},{3,5},{4,6},{5,7},{6,0},{7,1},{8,10},{9,11},{10,... | collective-permute-start | bytes 393224 | tf_op jit(solution)/shard_map/ppermute | solution.py:16
  156.6 12.1 %collective-permute-start.56 = (bf16[512,128]{1,0:T(8,128)(2,1)S(1)}, bf16[512,128]{1,0:T(8,128)(2,1)S(1)}, u32[]{:S(2)}, u32[]{:S(2)}) collective-permute-start(bf16[512,128]{1,0:T(8,128)(2,1)S(1)} %get-tuple-element.197), channel_id=1, source_target_pairs={{0,16},{8,24},{16,0},{24,8},{1,17},{9,25},{17,1},{25,9},{2,18},{10... | collective-permute-start | bytes 393224 | tf_op jit(solution)/shard_map/ppermute | solution.py:16
  159.7 9.4 %collective-permute-start.63 = (bf16[512,128]{1,0:T(8,128)(2,1)S(1)}, bf16[512,128]{1,0:T(8,128)(2,1)S(1)}, u32[]{:S(2)}, u32[]{:S(2)}) collective-permute-start(bf16[512,128]{1,0:T(8,128)(2,1)S(1)} %add_convert_fusion.2), channel_id=1, source_target_pairs={{0,2},{1,3},{2,4},{3,5},{4,6},{5,7},{6,0},{7,1},{8,10},{9,11},{10,... | collective-permute-start | bytes 393224 | tf_op jit(solution)/shard_map/ppermute | solution.py:16
  (44 other events, 327.0 us)

commit v4 on v3

--- a/solution.py
+++ b/solution.py
@@ -137,12 +137,18 @@
         if back == 1:
             exchange_kept(params[0] - (0.2 * 0.9) * momentum[0], 0)
     first_keys = []
-    for c in range(0, CHUNKS, 2):
-        both = [jnp.concatenate(first[i], axis=0) for i in (c, c + 1)]
+
+    def multiply_first():
+        c = len(first_keys)
+        both = []
+        for pieces in first[c : c + 2]:
+            last = after(pieces[-1], issued[-1]) if issued else pieces[-1]
+            both.append(jnp.concatenate(pieces[:-1] + [last], axis=0))
         both = after(jnp.concatenate(both, axis=1))
         both = jnp.dot(pair_tokens, both, preferred_element_type=wide)
-        first_keys += [both[:, :part], both[:, part:]]
-
+        first_keys.extend([both[:, :part], both[:, part:]])
+
+    multiply_first()
     later = []
 
     def stream(c):
@@ -193,6 +199,8 @@
         value, link = streams[c].send(came[c])
         came[c] = send(value, link, 2 ** mixings[c])
         if len(issued) == 2:
+            while len(first_keys) < CHUNKS:
+                multiply_first()
             read_passed(0)
             issued.append(weights[1])
         mixings[c] += link == "group"

time: 184 us -> 181 us (0.984)
  waiting for transfers between devices: 97.6 us -> 90.9 us
  starting transfers between devices: 36.8 us -> 40.2 us
    ppermute x58, waiting for transfers between devices: 93.2 us -> 87.2 us  [from_behind(): return lax.ppermute(value, axis, pairs)]
    ppermute x8, starting transfers between devices: 7.31 us -> 9.35 us  [send(): return lax.ppermute(value, 'fsdp', [(i, i ^ 1) for i in range(count)])]
  transfers between devices with their start and end apart: 67 -> 67, of which waited for: 45 -> 47; matrix products, arithmetic and copies ran while one was open for 23% -> 23% of each run, Pallas kernels for 0% -> 0%
where the time goes in v4:
time: 181 us; the launch traced here: 180 us
  waiting for transfers between devices  90.9 us (50%)
  starting transfers between devices  40.2 us (22%)
  matrix products  24.7 us (14%)
  other arithmetic  12.6 us (7%)
  local copies, waits for them, and re-layouts  9.38 us (5%)
  between operations  2.18 us (1%)
    ppermute x58, waiting for transfers between devices, from_behind(): return lax.ppermute(value, axis, pairs)  87.2 us
    ppermute x58, starting transfers between devices, from_behind(): return lax.ppermute(value, axis, pairs)  27.9 us
    dot_general x32, matrix products, partial(): lax.dot_general(column_block(back), grad_out, contract, preferred_element...  13.1 us
    dot_general x16, matrix products, stream(): jnp.dot(column_block(back), piece, preferred_element_type=wide)  9.62 us
    ppermute x8, starting transfers between devices, send(): return lax.ppermute(value, 'fsdp', [(i, i ^ 1) for i in range(count)])  9.35 us
  transfers between devices with their start and end apart: 67, of which 47 were waited for; matrix products, arithmetic and copies ran while one was open for 23% of the time, Pallas kernels for 0%

profile of v4, /device:TPU:0, one launch (start us, length us, event | category | flops | bytes accessed | tf_op | source)
XLA Modules:
  0.0 180.0 jit_solution(11437277909411552099)
XLA Ops:
  3.6 2.9 %collective-permute-start.1 = (bf16[384,2048]{1,0:T(8,128)(2,1)}, bf16[384,2048]{1,0:T(8,128)(2,1)}, u32[]{:S(2)}, u32[]{:S(2)}) collective-permute-start(bf16[384,2048]{1,0:T(8,128)(2,1)} %pad_maximum_fusion), channel_id=1, source_target_pairs={{0,1},{1,0},{2,3},{3,2},{4,5},{5,4},{6,7},{7,6},{8,9},{9,8},{10,11... | collective-permute-start | bytes 4718600 | tf_op jit(solution)/shard_map/ppermute | solution.py:89
  16.4 2.1 %collective-permute-done.5 = bf16[512,128]{1,0:T(8,128)(2,1)} collective-permute-done((bf16[512,128]{1,0:T(8,128)(2,1)S(1)}, bf16[512,128]{1,0:T(8,128)(2,1)}, u32[]{:S(2)}, u32[]{:S(2)}) %collective-permute-start.5) | collective-permute-done | bytes 131104 | tf_op jit(solution)/shard_map/ppermute | solution.py:16
  19.1 2.2 %collective-permute-done.10 = bf16[512,128]{1,0:T(8,128)(2,1)} collective-permute-done((bf16[512,128]{1,0:T(8,128)(2,1)S(1)}, bf16[512,128]{1,0:T(8,128)(2,1)}, u32[]{:S(2)}, u32[]{:S(2)}) %collective-permute-start.10) | collective-permute-done | bytes 131104 | tf_op jit(solution)/shard_map/ppermute | solution.py:16
  21.3 2.8 %collective-permute-done.13 = bf16[512,128]{1,0:T(8,128)(2,1)} collective-permute-done((bf16[512,128]{1,0:T(8,128)(2,1)S(1)}, bf16[512,128]{1,0:T(8,128)(2,1)}, u32[]{:S(2)}, u32[]{:S(2)}) %collective-permute-start.13) | collective-permute-done | bytes 131104 | tf_op jit(solution)/shard_map/ppermute | solution.py:16
  24.2 2.8 %collective-permute-done.3 = bf16[512,128]{1,0:T(8,128)(2,1)} collective-permute-done((bf16[512,128]{1,0:T(8,128)(2,1)}, bf16[512,128]{1,0:T(8,128)(2,1)}, u32[]{:S(2)}, u32[]{:S(2)}) %collective-permute-start.3) | collective-permute-done | bytes 131104 | tf_op jit(solution)/shard_map/ppermute | solution.py:16
  27.0 2.8 %collective-permute-done.6 = bf16[512,128]{1,0:T(8,128)(2,1)} collective-permute-done((bf16[512,128]{1,0:T(8,128)(2,1)}, bf16[512,128]{1,0:T(8,128)(2,1)}, u32[]{:S(2)}, u32[]{:S(2)}) %collective-permute-start.6) | collective-permute-done | bytes 131104 | tf_op jit(solution)/shard_map/ppermute | solution.py:16
  32.9 2.5 %collective-permute-done.14 = bf16[512,128]{1,0:T(8,128)(2,1)} collective-permute-done((bf16[512,128]{1,0:T(8,128)(2,1)}, bf16[512,128]{1,0:T(8,128)(2,1)}, u32[]{:S(2)}, u32[]{:S(2)}) %collective-permute-start.14) | collective-permute-done | bytes 131104 | tf_op jit(solution)/shard_map/ppermute | solution.py:16
  35.4 2.8 %collective-permute-done.4 = bf16[512,128]{1,0:T(8,128)(2,1)} collective-permute-done((bf16[512,128]{1,0:T(8,128)(2,1)}, bf16[512,128]{1,0:T(8,128)(2,1)}, u32[]{:S(2)}, u32[]{:S(2)}) %collective-permute-start.4) | collective-permute-done | bytes 131104 | tf_op jit(solution)/shard_map/ppermute | solution.py:16
  45.1 1.8 %collective-permute-start.8 = (bf16[768,128]{1,0:T(8,128)(2,1)S(1)}, bf16[768,128]{1,0:T(8,128)(2,1)S(1)}, u32[]{:S(2)}, u32[]{:S(2)}) collective-permute-start(bf16[768,128]{1,0:T(8,128)(2,1)S(1)} %get-tuple-element.239), channel_id=1, source_target_pairs={{0,1},{1,0},{2,3},{3,2},{4,5},{5,4},{6,7},{7,6},{8,9},{9,8},{10,11... | collective-permute-start | bytes 589832 | tf_op jit(solution)/shard_map/ppermute | solution.py:70
  49.6 3.4 %collective-permute-done.8 = bf16[768,128]{1,0:T(8,128)(2,1)S(1)} collective-permute-done((bf16[768,128]{1,0:T(8,128)(2,1)S(1)}, bf16[768,128]{1,0:T(8,128)(2,1)S(1)}, u32[]{:S(2)}, u32[]{:S(2)}) %collective-permute-start.8) | collective-permute-done | bytes 196640 | tf_op jit(solution)/shard_map/ppermute | solution.py:70
  54.7 1.9 %collective-permute-start.9 = (bf16[512,128]{1,0:T(8,128)(2,1)S(1)}, bf16[512,128]{1,0:T(8,128)(2,1)S(1)}, u32[]{:S(2)}, u32[]{:S(2)}) collective-permute-start(bf16[512,128]{1,0:T(8,128)(2,1)S(1)} %convolution_convert_fusion.7), channel_id=1, source_target_pairs={{0,2},{1,3},{2,4},{3,5},{4,6},{5,7},{6,0},{7,1},{8,10},{9,11},{10,... | collective-permute-start | bytes 393224 | tf_op jit(solution)/shard_map/ppermute | solution.py:16
  68.6 2.8 %collective-permute-done.17 = bf16[512,128]{1,0:T(8,128)(2,1)S(1)} collective-permute-done((bf16[512,128]{1,0:T(8,128)(2,1)S(1)}, bf16[512,128]{1,0:T(8,128)(2,1)S(1)}, u32[]{:S(2)}, u32[]{:S(2)}) %collective-permute-start.17) | collective-permute-done | bytes 131104 | tf_op jit(solution)/shard_map/ppermute | solution.py:16
  77.4 1.9 %collective-permute-start.27 = (bf16[512,128]{1,0:T(8,128)(2,1)S(1)}, bf16[512,128]{1,0:T(8,128)(2,1)S(1)}, u32[]{:S(2)}, u32[]{:S(2)}) collective-permute-start(bf16[512,128]{1,0:T(8,128)(2,1)S(1)} %add_convert_fusion.11), channel_id=1, source_target_pairs={{0,2},{1,3},{2,4},{3,5},{4,6},{5,7},{6,0},{7,1},{8,10},{9,11},{10,... | collective-permute-start | bytes 393224 | tf_op jit(solution)/shard_map/ppermute | solution.py:16
  85.6 4.8 %collective-permute-done.30 = bf16[512,128]{1,0:T(8,128)(2,1)S(1)} collective-permute-done((bf16[512,128]{1,0:T(8,128)(2,1)S(1)}, bf16[512,128]{1,0:T(8,128)(2,1)S(1)}, u32[]{:S(2)}, u32[]{:S(2)}) %collective-permute-start.30) | collective-permute-done | bytes 131104 | tf_op jit(solution)/shard_map/ppermute | solution.py:16
  90.9 2.3 %collective-permute-done.29 = bf16[512,128]{1,0:T(8,128)(2,1)S(1)} collective-permute-done((bf16[512,128]{1,0:T(8,128)(2,1)S(1)}, bf16[512,128]{1,0:T(8,128)(2,1)S(1)}, u32[]{:S(2)}, u32[]{:S(2)}) %collective-permute-start.29) | collective-permute-done | bytes 131104 | tf_op jit(solution)/shard_map/ppermute | solution.py:16
  94.0 2.1 %collective-permute-done.33 = bf16[512,128]{1,0:T(8,128)(2,1)S(1)} collective-permute-done((bf16[512,128]{1,0:T(8,128)(2,1)S(1)}, bf16[512,128]{1,0:T(8,128)(2,1)S(1)}, u32[]{:S(2)}, u32[]{:S(2)}) %collective-permute-start.33) | collective-permute-done | bytes 131104 | tf_op jit(solution)/shard_map/ppermute | solution.py:16
  98.9 2.6 %collective-permute-done.36 = bf16[512,128]{1,0:T(8,128)(2,1)S(1)} collective-permute-done((bf16[512,128]{1,0:T(8,128)(2,1)S(1)}, bf16[512,128]{1,0:T(8,128)(2,1)S(1)}, u32[]{:S(2)}, u32[]{:S(2)}) %collective-permute-start.36) | collective-permute-done | bytes 131104 | tf_op jit(solution)/shard_map/ppermute | solution.py:16
  101.5 2.8 %collective-permute-done.35 = bf16[512,128]{1,0:T(8,128)(2,1)S(1)} collective-permute-done((bf16[512,128]{1,0:T(8,128)(2,1)S(1)}, bf16[512,128]{1,0:T(8,128)(2,1)S(1)}, u32[]{:S(2)}, u32[]{:S(2)}) %collective-permute-start.35) | collective-permute-done | bytes 131104 | tf_op jit(solution)/shard_map/ppermute | solution.py:16
  105.0 2.2 %collective-permute-start.37 = (bf16[528,512]{1,0:T(8,128)(2,1)S(1)}, bf16[528,512]{1,0:T(8,128)(2,1)S(1)}, u32[]{:S(2)}, u32[]{:S(2)}) collective-permute-start(bf16[528,512]{1,0:T(8,128)(2,1)S(1)} %pad_maximum_fusion.1), channel_id=1, source_target_pairs={{0,16},{8,24},{16,0},{24,8},{1,17},{9,25},{17,1},{25,9},{2,18},{10... | collective-permute-start | bytes 1622024 | tf_op jit(solution)/shard_map/ppermute | solution.py:16
  107.6 2.2 %collective-permute-start.39 = (bf16[512,128]{1,0:T(8,128)(2,1)S(1)}, bf16[512,128]{1,0:T(8,128)(2,1)S(1)}, u32[]{:S(2)}, u32[]{:S(2)}) collective-permute-start(bf16[512,128]{1,0:T(8,128)(2,1)S(1)} %collective-permute-done.38), channel_id=1, source_target_pairs={{0,2},{1,3},{2,4},{3,5},{4,6},{5,7},{6,0},{7,1},{8,10},{9,11},{10,... | collective-permute-start | bytes 393224 | tf_op jit(solution)/shard_map/ppermute | solution.py:16
  110.2 2.6 %collective-permute-done.41 = bf16[512,128]{1,0:T(8,128)(2,1)S(1)} collective-permute-done((bf16[512,128]{1,0:T(8,128)(2,1)S(1)}, bf16[512,128]{1,0:T(8,128)(2,1)S(1)}, u32[]{:S(2)}, u32[]{:S(2)}) %collective-permute-start.41) | collective-permute-done | bytes 131104 | tf_op jit(solution)/shard_map/ppermute | solution.py:16
  118.8 4.9 %collective-permute-done.46 = bf16[512,128]{1,0:T(8,128)(2,1)S(1)} collective-permute-done((bf16[512,128]{1,0:T(8,128)(2,1)S(1)}, bf16[512,128]{1,0:T(8,128)(2,1)S(1)}, u32[]{:S(2)}, u32[]{:S(2)}) %collective-permute-start.46) | collective-permute-done | bytes 131104 | tf_op jit(solution)/shard_map/ppermute | solution.py:16
  127.4 1.9 %collective-permute-done.43 = bf16[512,128]{1,0:T(8,128)(2,1)S(1)} collective-permute-done((bf16[512,128]{1,0:T(8,128)(2,1)S(1)}, bf16[512,128]{1,0:T(8,128)(2,1)S(1)}, u32[]{:S(2)}, u32[]{:S(2)}) %collective-permute-start.43) | collective-permute-done | bytes 131104 | tf_op jit(solution)/shard_map/ppermute | solution.py:16
  132.1 3.5 %collective-permute-done.50 = bf16[512,128]{1,0:T(8,128)(2,1)S(1)} collective-permute-done((bf16[512,128]{1,0:T(8,128)(2,1)S(1)}, bf16[512,128]{1,0:T(8,128)(2,1)S(1)}, u32[]{:S(2)}, u32[]{:S(2)}) %collective-permute-start.50) | collective-permute-done | bytes 131104 | tf_op jit(solution)/shard_map/ppermute | solution.py:16
  138.6 1.8 collective-permute-start.52
  141.0 1.8 %collective-permute-done.54 = bf16[512,128]{1,0:T(8,128)(2,1)S(1)} collective-permute-done((bf16[512,128]{1,0:T(8,128)(2,1)S(1)}, bf16[512,128]{1,0:T(8,128)(2,1)S(1)}, u32[]{:S(2)}, u32[]{:S(2)}) %collective-permute-start.54) | collective-permute-done | bytes 131104 | tf_op jit(solution)/shard_map/ppermute | solution.py:16
  150.1 1.9 %collective-permute-done.55 = bf16[512,128]{1,0:T(8,128)(2,1)S(1)} collective-permute-done((bf16[512,128]{1,0:T(8,128)(2,1)S(1)}, bf16[512,128]{1,0:T(8,128)(2,1)S(1)}, u32[]{:S(2)}, u32[]{:S(2)}) %collective-permute-start.55) | collective-permute-done | bytes 131104 | tf_op jit(solution)/shard_map/ppermute | solution.py:16
  155.3 2.3 %collective-permute-done.60 = bf16[512,128]{1,0:T(8,128)(2,1)S(1)} collective-permute-done((bf16[512,128]{1,0:T(8,128)(2,1)S(1)}, bf16[512,128]{1,0:T(8,128)(2,1)S(1)}, u32[]{:S(2)}, u32[]{:S(2)}) %collective-permute-start.60) | collective-permute-done | bytes 131104 | tf_op jit(solution)/shard_map/ppermute | solution.py:16
  158.1 2.3 %collective-permute-done.59 = bf16[512,128]{1,0:T(8,128)(2,1)S(1)} collective-permute-done((bf16[512,128]{1,0:T(8,128)(2,1)S(1)}, bf16[512,128]{1,0:T(8,128)(2,1)S(1)}, u32[]{:S(2)}, u32[]{:S(2)}) %collective-permute-start.59) | collective-permute-done | bytes 131104 | tf_op jit(solution)/shard_map/ppermute | solution.py:16
  160.9 2.6 %collective-permute-done.58 = bf16[512,128]{1,0:T(8,128)(2,1)S(1)} collective-permute-done((bf16[512,128]{1,0:T(8,128)(2,1)S(1)}, bf16[512,128]{1,0:T(8,128)(2,1)S(1)}, u32[]{:S(2)}, u32[]{:S(2)}) %collective-permute-start.58) | collective-permute-done | bytes 131104 | tf_op jit(solution)/shard_map/ppermute | solution.py:16
  169.3 3.9 %collective-permute-done.65 = bf16[512,128]{1,0:T(8,128)(2,1)S(1)} collective-permute-done((bf16[512,128]{1,0:T(8,128)(2,1)S(1)}, bf16[512,128]{1,0:T(8,128)(2,1)S(1)}, u32[]{:S(2)}, u32[]{:S(2)}) %collective-permute-start.65) | collective-permute-done | bytes 131104 | tf_op jit(solution)/shard_map/ppermute | solution.py:16
  174.3 4.3 %collective-permute-done.66 = bf16[512,128]{1,0:T(8,128)(2,1)S(1)} collective-permute-done((bf16[512,128]{1,0:T(8,128)(2,1)S(1)}, bf16[512,128]{1,0:T(8,128)(2,1)S(1)}, u32[]{:S(2)}, u32[]{:S(2)}) %collective-permute-start.66) | collective-permute-done | bytes 131104 | tf_op jit(solution)/shard_map/ppermute | solution.py:16
  (215 shorter events, 92.4 us)
Async XLA Ops:
  3.6 37.6 %collective-permute-start.1 = (bf16[384,2048]{1,0:T(8,128)(2,1)}, bf16[384,2048]{1,0:T(8,128)(2,1)}, u32[]{:S(2)}, u32[]{:S(2)}) collective-permute-start(bf16[384,2048]{1,0:T(8,128)(2,1)} %pad_maximum_fusion), channel_id=1, source_target_pairs={{0,1},{1,0},{2,3},{3,2},{4,5},{5,4},{6,7},{7,6},{8,9},{9,8},{10,11... | collective-permute-start | bytes 4718600 | tf_op jit(solution)/shard_map/ppermute | solution.py:89
  9.0 9.6 %collective-permute-start.5 = (bf16[512,128]{1,0:T(8,128)(2,1)S(1)}, bf16[512,128]{1,0:T(8,128)(2,1)}, u32[]{:S(2)}, u32[]{:S(2)}) collective-permute-start(bf16[512,128]{1,0:T(8,128)(2,1)S(1)} %get-tuple-element.242), channel_id=1, source_target_pairs={{0,2},{1,3},{2,4},{3,5},{4,6},{5,7},{6,0},{7,1},{8,10},{9,11},{10,... | collective-permute-start | bytes 393224 | tf_op jit(solution)/shard_map/ppermute | solution.py:16
  10.6 10.8 %collective-permute-start.10 = (bf16[512,128]{1,0:T(8,128)(2,1)S(1)}, bf16[512,128]{1,0:T(8,128)(2,1)}, u32[]{:S(2)}, u32[]{:S(2)}) collective-permute-start(bf16[512,128]{1,0:T(8,128)(2,1)S(1)} %get-tuple-element.241), channel_id=1, source_target_pairs={{0,2},{1,3},{2,4},{3,5},{4,6},{5,7},{6,0},{7,1},{8,10},{9,11},{10,... | collective-permute-start | bytes 393224 | tf_op jit(solution)/shard_map/ppermute | solution.py:16
  12.1 12.0 %collective-permute-start.13 = (bf16[512,128]{1,0:T(8,128)(2,1)S(1)}, bf16[512,128]{1,0:T(8,128)(2,1)}, u32[]{:S(2)}, u32[]{:S(2)}) collective-permute-start(bf16[512,128]{1,0:T(8,128)(2,1)S(1)} %get-tuple-element.244), channel_id=1, source_target_pairs={{0,2},{1,3},{2,4},{3,5},{4,6},{5,7},{6,0},{7,1},{8,10},{9,11},{10,... | collective-permute-start | bytes 393224 | tf_op jit(solution)/shard_map/ppermute | solution.py:16
  15.7 11.2 %collective-permute-start.3 = (bf16[512,128]{1,0:T(8,128)(2,1)}, bf16[512,128]{1,0:T(8,128)(2,1)}, u32[]{:S(2)}, u32[]{:S(2)}) collective-permute-start(bf16[512,128]{1,0:T(8,128)(2,1)} %collective-permute-done.2), channel_id=1, source_target_pairs={{0,2},{1,3},{2,4},{3,5},{4,6},{5,7},{6,0},{7,1},{8,10},{9,11},{10,... | collective-permute-start | bytes 393224 | tf_op jit(solution)/shard_map/ppermute | solution.py:16
  18.5 11.2 %collective-permute-start.6 = (bf16[512,128]{1,0:T(8,128)(2,1)}, bf16[512,128]{1,0:T(8,128)(2,1)}, u32[]{:S(2)}, u32[]{:S(2)}) collective-permute-start(bf16[512,128]{1,0:T(8,128)(2,1)} %collective-permute-done.5), channel_id=1, source_target_pairs={{0,2},{1,3},{2,4},{3,5},{4,6},{5,7},{6,0},{7,1},{8,10},{9,11},{10,... | collective-permute-start | bytes 393224 | tf_op jit(solution)/shard_map/ppermute | solution.py:16
  21.3 11.4 %collective-permute-start.11 = (bf16[512,128]{1,0:T(8,128)(2,1)}, bf16[512,128]{1,0:T(8,128)(2,1)}, u32[]{:S(2)}, u32[]{:S(2)}) collective-permute-start(bf16[512,128]{1,0:T(8,128)(2,1)} %collective-permute-done.10), channel_id=1, source_target_pairs={{0,2},{1,3},{2,4},{3,5},{4,6},{5,7},{6,0},{7,1},{8,10},{9,11},{10,... | collective-permute-start | bytes 393224 | tf_op jit(solution)/shard_map/ppermute | solution.py:16
  24.1 11.2 %collective-permute-start.14 = (bf16[512,128]{1,0:T(8,128)(2,1)}, bf16[512,128]{1,0:T(8,128)(2,1)}, u32[]{:S(2)}, u32[]{:S(2)}) collective-permute-start(bf16[512,128]{1,0:T(8,128)(2,1)} %collective-permute-done.13), channel_id=1, source_target_pairs={{0,2},{1,3},{2,4},{3,5},{4,6},{5,7},{6,0},{7,1},{8,10},{9,11},{10,... | collective-permute-start | bytes 393224 | tf_op jit(solution)/shard_map/ppermute | solution.py:16
  27.0 11.2 %collective-permute-start.4 = (bf16[512,128]{1,0:T(8,128)(2,1)}, bf16[512,128]{1,0:T(8,128)(2,1)}, u32[]{:S(2)}, u32[]{:S(2)}) collective-permute-start(bf16[512,128]{1,0:T(8,128)(2,1)} %collective-permute-done.3), channel_id=1, source_target_pairs={{0,2},{1,3},{2,4},{3,5},{4,6},{5,7},{6,0},{7,1},{8,10},{9,11},{10,... | collective-permute-start | bytes 393224 | tf_op jit(solution)/shard_map/ppermute | solution.py:16
  29.8 9.9 %collective-permute-start.7 = (bf16[512,128]{1,0:T(8,128)(2,1)}, bf16[512,128]{1,0:T(8,128)(2,1)}, u32[]{:S(2)}, u32[]{:S(2)}) collective-permute-start(bf16[512,128]{1,0:T(8,128)(2,1)} %collective-permute-done.6), channel_id=1, source_target_pairs={{0,2},{1,3},{2,4},{3,5},{4,6},{5,7},{6,0},{7,1},{8,10},{9,11},{10,... | collective-permute-start | bytes 393224 | tf_op jit(solution)/shard_map/ppermute | solution.py:16
  32.8 14.5 %collective-permute-start = (f32[520,512]{1,0:T(8,128)S(1)}, f32[520,512]{1,0:T(8,128)S(1)}, u32[]{:S(2)}, u32[]{:S(2)}) collective-permute-start(f32[520,512]{1,0:T(8,128)S(1)} %concatenate.35), channel_id=1, source_target_pairs={{0,8},{8,16},{16,24},{24,0},{1,9},{9,17},{17,25},{25,1},{2,10},{10... | collective-permute-start | bytes 3194888 | tf_op jit(solution)/shard_map/ppermute | solution.py:16
  35.4 11.9 %collective-permute-start.12 = (bf16[512,128]{1,0:T(8,128)(2,1)}, bf16[512,128]{1,0:T(8,128)(2,1)S(1)}, u32[]{:S(2)}, u32[]{:S(2)}) collective-permute-start(bf16[512,128]{1,0:T(8,128)(2,1)} %collective-permute-done.11), channel_id=1, source_target_pairs={{0,2},{1,3},{2,4},{3,5},{4,6},{5,7},{6,0},{7,1},{8,10},{9,11},{10,... | collective-permute-start | bytes 393224 | tf_op jit(solution)/shard_map/ppermute | solution.py:16
  38.2 9.1 %collective-permute-start.15 = (bf16[512,128]{1,0:T(8,128)(2,1)}, bf16[512,128]{1,0:T(8,128)(2,1)S(1)}, u32[]{:S(2)}, u32[]{:S(2)}) collective-permute-start(bf16[512,128]{1,0:T(8,128)(2,1)} %collective-permute-done.14), channel_id=1, source_target_pairs={{0,2},{1,3},{2,4},{3,5},{4,6},{5,7},{6,0},{7,1},{8,10},{9,11},{10,... | collective-permute-start | bytes 393224 | tf_op jit(solution)/shard_map/ppermute | solution.py:16
  46.9 11.2 %collective-permute-start.16 = (bf16[768,128]{1,0:T(8,128)(2,1)S(1)}, bf16[768,128]{1,0:T(8,128)(2,1)S(1)}, u32[]{:S(2)}, u32[]{:S(2)}) collective-permute-start(bf16[768,128]{1,0:T(8,128)(2,1)S(1)} %get-tuple-element.112), channel_id=1, source_target_pairs={{0,1},{1,0},{2,3},{3,2},{4,5},{5,4},{6,7},{7,6},{8,9},{9,8},{10,11... | collective-permute-start | bytes 589832 | tf_op jit(solution)/shard_map/ppermute | solution.py:70
  61.2 10.7 %collective-permute-start.23 = (bf16[768,128]{1,0:T(8,128)(2,1)S(1)}, bf16[768,128]{1,0:T(8,128)(2,1)S(1)}, u32[]{:S(2)}, u32[]{:S(2)}) collective-permute-start(bf16[768,128]{1,0:T(8,128)(2,1)S(1)} %get-tuple-element.121), channel_id=1, source_target_pairs={{0,1},{1,0},{2,3},{3,2},{4,5},{5,4},{6,7},{7,6},{8,9},{9,8},{10,11... | collective-permute-start | bytes 589832 | tf_op jit(solution)/shard_map/ppermute | solution.py:70
  65.2 8.9 %collective-permute-start.22 = (bf16[512,128]{1,0:T(8,128)(2,1)S(1)}, bf16[512,128]{1,0:T(8,128)(2,1)S(1)}, u32[]{:S(2)}, u32[]{:S(2)}) collective-permute-start(bf16[512,128]{1,0:T(8,128)(2,1)S(1)} %convolution_convert_fusion.5), channel_id=1, source_target_pairs={{0,2},{1,3},{2,4},{3,5},{4,6},{5,7},{6,0},{7,1},{8,10},{9,11},{10,... | collective-permute-start | bytes 393224 | tf_op jit(solution)/shard_map/ppermute | solution.py:16
  68.1 8.9 %collective-permute-start.21 = (bf16[512,128]{1,0:T(8,128)(2,1)S(1)}, bf16[512,128]{1,0:T(8,128)(2,1)S(1)}, u32[]{:S(2)}, u32[]{:S(2)}) collective-permute-start(bf16[512,128]{1,0:T(8,128)(2,1)S(1)} %add_convert_fusion.14), channel_id=1, source_target_pairs={{0,2},{1,3},{2,4},{3,5},{4,6},{5,7},{6,0},{7,1},{8,10},{9,11},{10,... | collective-permute-start | bytes 393224 | tf_op jit(solution)/shard_map/ppermute | solution.py:16
  83.6 9.6 %collective-permute-start.29 = (bf16[512,128]{1,0:T(8,128)(2,1)S(1)}, bf16[512,128]{1,0:T(8,128)(2,1)S(1)}, u32[]{:S(2)}, u32[]{:S(2)}) collective-permute-start(bf16[512,128]{1,0:T(8,128)(2,1)S(1)} %add_convert_fusion.9), channel_id=1, source_target_pairs={{0,2},{1,3},{2,4},{3,5},{4,6},{5,7},{6,0},{7,1},{8,10},{9,11},{10,... | collective-permute-start | bytes 393224 | tf_op jit(solution)/shard_map/ppermute | solution.py:16
  85.1 11.0 %collective-permute-start.33 = (bf16[512,128]{1,0:T(8,128)(2,1)S(1)}, bf16[512,128]{1,0:T(8,128)(2,1)S(1)}, u32[]{:S(2)}, u32[]{:S(2)}) collective-permute-start(bf16[512,128]{1,0:T(8,128)(2,1)S(1)} %divide_convert_fusion.3), channel_id=1, source_target_pairs={{0,2},{1,3},{2,4},{3,5},{4,6},{5,7},{6,0},{7,1},{8,10},{9,11},{10,... | collective-permute-start | bytes 393224 | tf_op jit(solution)/shard_map/ppermute | solution.py:16
  104.9 10.7 %collective-permute-start.40 = (bf16[512,128]{1,0:T(8,128)(2,1)S(1)}, bf16[512,128]{1,0:T(8,128)(2,1)S(1)}, u32[]{:S(2)}, u32[]{:S(2)}) collective-permute-start(bf16[512,128]{1,0:T(8,128)(2,1)S(1)} %get-tuple-element.163), channel_id=1, source_target_pairs={{0,2},{1,3},{2,4},{3,5},{4,6},{5,7},{6,0},{7,1},{8,10},{9,11},{10,... | collective-permute-start | bytes 393224 | tf_op jit(solution)/shard_map/ppermute | solution.py:16
  105.0 44.9 %collective-permute-start.37 = (bf16[528,512]{1,0:T(8,128)(2,1)S(1)}, bf16[528,512]{1,0:T(8,128)(2,1)S(1)}, u32[]{:S(2)}, u32[]{:S(2)}) collective-permute-start(bf16[528,512]{1,0:T(8,128)(2,1)S(1)} %pad_maximum_fusion.1), channel_id=1, source_target_pairs={{0,16},{8,24},{16,0},{24,8},{1,17},{9,25},{17,1},{25,9},{2,18},{10... | collective-permute-start | bytes 1622024 | tf_op jit(solution)/shard_map/ppermute | solution.py:16
  107.6 10.7 %collective-permute-start.39 = (bf16[512,128]{1,0:T(8,128)(2,1)S(1)}, bf16[512,128]{1,0:T(8,128)(2,1)S(1)}, u32[]{:S(2)}, u32[]{:S(2)}) collective-permute-start(bf16[512,128]{1,0:T(8,128)(2,1)S(1)} %collective-permute-done.38), channel_id=1, source_target_pairs={{0,2},{1,3},{2,4},{3,5},{4,6},{5,7},{6,0},{7,1},{8,10},{9,11},{10,... | collective-permute-start | bytes 393224 | tf_op jit(solution)/shard_map/ppermute | solution.py:16
  116.0 10.9 %collective-permute-start.45 = (bf16[768,128]{1,0:T(8,128)(2,1)S(1)}, bf16[768,128]{1,0:T(8,128)(2,1)S(1)}, u32[]{:S(2)}, u32[]{:S(2)}) collective-permute-start(bf16[768,128]{1,0:T(8,128)(2,1)S(1)} %get-tuple-element.170), channel_id=1, source_target_pairs={{0,1},{1,0},{2,3},{3,2},{4,5},{5,4},{6,7},{7,6},{8,9},{9,8},{10,11... | collective-permute-start | bytes 589832 | tf_op jit(solution)/shard_map/ppermute | solution.py:70
  117.4 10.0 %collective-permute-start.44 = (bf16[512,128]{1,0:T(8,128)(2,1)S(1)}, bf16[512,128]{1,0:T(8,128)(2,1)S(1)}, u32[]{:S(2)}, u32[]{:S(2)}) collective-permute-start(bf16[512,128]{1,0:T(8,128)(2,1)S(1)} %collective-permute-done.40), channel_id=1, source_target_pairs={{0,2},{1,3},{2,4},{3,5},{4,6},{5,7},{6,0},{7,1},{8,10},{9,11},{10,... | collective-permute-start | bytes 393224 | tf_op jit(solution)/shard_map/ppermute | solution.py:16
  118.3 11.0 %collective-permute-start.43 = (bf16[512,128]{1,0:T(8,128)(2,1)S(1)}, bf16[512,128]{1,0:T(8,128)(2,1)S(1)}, u32[]{:S(2)}, u32[]{:S(2)}) collective-permute-start(bf16[512,128]{1,0:T(8,128)(2,1)S(1)} %collective-permute-done.39), channel_id=1, source_target_pairs={{0,2},{1,3},{2,4},{3,5},{4,6},{5,7},{6,0},{7,1},{8,10},{9,11},{10,... | collective-permute-start | bytes 393224 | tf_op jit(solution)/shard_map/ppermute | solution.py:16
  125.5 10.6 %collective-permute-start.49 = (bf16[768,128]{1,0:T(8,128)(2,1)S(1)}, bf16[768,128]{1,0:T(8,128)(2,1)S(1)}, u32[]{:S(2)}, u32[]{:S(2)}) collective-permute-start(bf16[768,128]{1,0:T(8,128)(2,1)S(1)} %get-tuple-element.176), channel_id=1, source_target_pairs={{0,1},{1,0},{2,3},{3,2},{4,5},{5,4},{6,7},{7,6},{8,9},{9,8},{10,11... | collective-permute-start | bytes 589832 | tf_op jit(solution)/shard_map/ppermute | solution.py:70
  127.4 9.6 %collective-permute-start.48 = (bf16[512,128]{1,0:T(8,128)(2,1)S(1)}, bf16[512,128]{1,0:T(8,128)(2,1)S(1)}, u32[]{:S(2)}, u32[]{:S(2)}) collective-permute-start(bf16[512,128]{1,0:T(8,128)(2,1)S(1)} %collective-permute-done.44), channel_id=1, source_target_pairs={{0,2},{1,3},{2,4},{3,5},{4,6},{5,7},{6,0},{7,1},{8,10},{9,11},{10,... | collective-permute-start | bytes 393224 | tf_op jit(solution)/shard_map/ppermute | solution.py:16
  131.1 9.3 %collective-permute-start.47 = (bf16[768,128]{1,0:T(8,128)(2,1)S(1)}, bf16[768,128]{1,0:T(8,128)(2,1)S(1)}, u32[]{:S(2)}, u32[]{:S(2)}) collective-permute-start(bf16[768,128]{1,0:T(8,128)(2,1)S(1)} %get-tuple-element.182), channel_id=1, source_target_pairs={{0,1},{1,0},{2,3},{3,2},{4,5},{5,4},{6,7},{7,6},{8,9},{9,8},{10,11... | collective-permute-start | bytes 589832 | tf_op jit(solution)/shard_map/ppermute | solution.py:70
  145.3 9.5 %collective-permute-start.57 = (bf16[512,128]{1,0:T(8,128)(2,1)S(1)}, bf16[512,128]{1,0:T(8,128)(2,1)S(1)}, u32[]{:S(2)}, u32[]{:S(2)}) collective-permute-start(bf16[512,128]{1,0:T(8,128)(2,1)S(1)} %add_convert_fusion.5), channel_id=1, source_target_pairs={{0,2},{1,3},{2,4},{3,5},{4,6},{5,7},{6,0},{7,1},{8,10},{9,11},{10,... | collective-permute-start | bytes 393224 | tf_op jit(solution)/shard_map/ppermute | solution.py:16
  146.1 11.5 %collective-permute-start.60 = (bf16[512,128]{1,0:T(8,128)(2,1)S(1)}, bf16[512,128]{1,0:T(8,128)(2,1)S(1)}, u32[]{:S(2)}, u32[]{:S(2)}) collective-permute-start(bf16[512,128]{1,0:T(8,128)(2,1)S(1)} %convolution_convert_fusion), channel_id=1, source_target_pairs={{0,2},{1,3},{2,4},{3,5},{4,6},{5,7},{6,0},{7,1},{8,10},{9,11},{10,... | collective-permute-start | bytes 393224 | tf_op jit(solution)/shard_map/ppermute | solution.py:16
  149.6 10.8 %collective-permute-start.59 = (bf16[512,128]{1,0:T(8,128)(2,1)S(1)}, bf16[512,128]{1,0:T(8,128)(2,1)S(1)}, u32[]{:S(2)}, u32[]{:S(2)}) collective-permute-start(bf16[512,128]{1,0:T(8,128)(2,1)S(1)} %add_convert_fusion.4), channel_id=1, source_target_pairs={{0,2},{1,3},{2,4},{3,5},{4,6},{5,7},{6,0},{7,1},{8,10},{9,11},{10,... | collective-permute-start | bytes 393224 | tf_op jit(solution)/shard_map/ppermute | solution.py:16
  152.4 12.1 %collective-permute-start.56 = (bf16[512,128]{1,0:T(8,128)(2,1)S(1)}, bf16[512,128]{1,0:T(8,128)(2,1)S(1)}, u32[]{:S(2)}, u32[]{:S(2)}) collective-permute-start(bf16[512,128]{1,0:T(8,128)(2,1)S(1)} %get-tuple-element.201), channel_id=1, source_target_pairs={{0,16},{8,24},{16,0},{24,8},{1,17},{9,25},{17,1},{25,9},{2,18},{10... | collective-permute-start | bytes 393224 | tf_op jit(solution)/shard_map/ppermute | solution.py:16
  (44 other events, 324.9 us)

commit v5 on v4

--- a/solution.py
+++ b/solution.py
@@ -6,7 +6,7 @@
 STEPS = 2
 CHUNKS = 4
 OCCUPANCY = {"gather": 2.75, "scatter": 2.75, "pair": 3.95, "group": 2.0}
-PREPARE = {"gather": 0.8, "scatter": 1.2, "pair": 1.6, "group": 1.0}
+PREPARE = {"gather": 1.4, "scatter": 1.8, "pair": 2.6, "group": 2.2}
 LATENCY = 3.2
 
 

time: 181 us -> 179 us (0.989)
  waiting for transfers between devices: 90.9 us -> 86 us
  starting transfers between devices: 40.2 us -> 44.1 us
    ppermute x58, waiting for transfers between devices: 87.2 us -> 82 us  [from_behind(): return lax.ppermute(value, axis, pairs)]
    ppermute x58, starting transfers between devices: 27.9 us -> 32.2 us  [from_behind(): return lax.ppermute(value, axis, pairs)]
where the time goes in v5:
time: 179 us
  waiting for transfers between devices  86 us (48%)
  starting transfers between devices  44.1 us (25%)
  matrix products  24.7 us (14%)
  other arithmetic  12.6 us (7%)
  local copies, waits for them, and re-layouts  9.38 us (5%)
  between operations  2.16 us (1%)
    ppermute x58, waiting for transfers between devices, from_behind(): return lax.ppermute(value, axis, pairs)  82 us
    ppermute x58, starting transfers between devices, from_behind(): return lax.ppermute(value, axis, pairs)  32.2 us
    dot_general x32, matrix products, partial(): lax.dot_general(column_block(back), grad_out, contract, preferred_element...  13.2 us
    dot_general x16, matrix products, stream(): jnp.dot(column_block(back), piece, preferred_element_type=wide)  9.56 us
    ppermute x8, starting transfers between devices, send(): return lax.ppermute(value, 'fsdp', [(i, i ^ 1) for i in range(count)])  9.01 us
    ppermute x8, waiting for transfers between devices, send(): return lax.ppermute(value, 'fsdp', [(i, i ^ 1) for i in range(count)])  3.76 us
  transfers between devices with their start and end apart: 67, of which 47 were waited for; matrix products, arithmetic and copies ran while one was open for 23% of the time, Pallas kernels for 0%

profile of v5, /device:TPU:0, one launch (start us, length us, event | category | flops | bytes accessed | tf_op | source)
XLA Modules:
  0.0 178.9 jit_solution(17296641689220983071)
XLA Ops:
  3.6 2.9 %collective-permute-start.1 = (bf16[384,2048]{1,0:T(8,128)(2,1)}, bf16[384,2048]{1,0:T(8,128)(2,1)}, u32[]{:S(2)}, u32[]{:S(2)}) collective-permute-start(bf16[384,2048]{1,0:T(8,128)(2,1)} %pad_maximum_fusion), channel_id=1, source_target_pairs={{0,1},{1,0},{2,3},{3,2},{4,5},{5,4},{6,7},{7,6},{8,9},{9,8},{10,11... | collective-permute-start | bytes 4718600 | tf_op jit(solution)/shard_map/ppermute | solution.py:89
  16.4 2.1 %collective-permute-done.5 = bf16[512,128]{1,0:T(8,128)(2,1)} collective-permute-done((bf16[512,128]{1,0:T(8,128)(2,1)S(1)}, bf16[512,128]{1,0:T(8,128)(2,1)}, u32[]{:S(2)}, u32[]{:S(2)}) %collective-permute-start.5) | collective-permute-done | bytes 131104 | tf_op jit(solution)/shard_map/ppermute | solution.py:16
  19.1 2.2 %collective-permute-done.11 = bf16[512,128]{1,0:T(8,128)(2,1)} collective-permute-done((bf16[512,128]{1,0:T(8,128)(2,1)S(1)}, bf16[512,128]{1,0:T(8,128)(2,1)}, u32[]{:S(2)}, u32[]{:S(2)}) %collective-permute-start.11) | collective-permute-done | bytes 131104 | tf_op jit(solution)/shard_map/ppermute | solution.py:16
  21.3 2.8 %collective-permute-done.14 = bf16[512,128]{1,0:T(8,128)(2,1)} collective-permute-done((bf16[512,128]{1,0:T(8,128)(2,1)S(1)}, bf16[512,128]{1,0:T(8,128)(2,1)}, u32[]{:S(2)}, u32[]{:S(2)}) %collective-permute-start.14) | collective-permute-done | bytes 131104 | tf_op jit(solution)/shard_map/ppermute | solution.py:16
  24.2 2.8 %collective-permute-done.3 = bf16[512,128]{1,0:T(8,128)(2,1)} collective-permute-done((bf16[512,128]{1,0:T(8,128)(2,1)}, bf16[512,128]{1,0:T(8,128)(2,1)}, u32[]{:S(2)}, u32[]{:S(2)}) %collective-permute-start.3) | collective-permute-done | bytes 131104 | tf_op jit(solution)/shard_map/ppermute | solution.py:16
  27.0 2.8 %collective-permute-done.6 = bf16[512,128]{1,0:T(8,128)(2,1)} collective-permute-done((bf16[512,128]{1,0:T(8,128)(2,1)}, bf16[512,128]{1,0:T(8,128)(2,1)}, u32[]{:S(2)}, u32[]{:S(2)}) %collective-permute-start.6) | collective-permute-done | bytes 131104 | tf_op jit(solution)/shard_map/ppermute | solution.py:16
  32.9 2.5 %collective-permute-done.15 = bf16[512,128]{1,0:T(8,128)(2,1)} collective-permute-done((bf16[512,128]{1,0:T(8,128)(2,1)}, bf16[512,128]{1,0:T(8,128)(2,1)}, u32[]{:S(2)}, u32[]{:S(2)}) %collective-permute-start.15) | collective-permute-done | bytes 131104 | tf_op jit(solution)/shard_map/ppermute | solution.py:16
  35.4 2.8 %collective-permute-done.4 = bf16[512,128]{1,0:T(8,128)(2,1)} collective-permute-done((bf16[512,128]{1,0:T(8,128)(2,1)}, bf16[512,128]{1,0:T(8,128)(2,1)}, u32[]{:S(2)}, u32[]{:S(2)}) %collective-permute-start.4) | collective-permute-done | bytes 131104 | tf_op jit(solution)/shard_map/ppermute | solution.py:16
  45.1 1.8 %collective-permute-start.8 = (bf16[768,128]{1,0:T(8,128)(2,1)S(1)}, bf16[768,128]{1,0:T(8,128)(2,1)S(1)}, u32[]{:S(2)}, u32[]{:S(2)}) collective-permute-start(bf16[768,128]{1,0:T(8,128)(2,1)S(1)} %get-tuple-element.239), channel_id=1, source_target_pairs={{0,1},{1,0},{2,3},{3,2},{4,5},{5,4},{6,7},{7,6},{8,9},{9,8},{10,11... | collective-permute-start | bytes 589832 | tf_op jit(solution)/shard_map/ppermute | solution.py:70
  49.6 3.4 %collective-permute-done.8 = bf16[768,128]{1,0:T(8,128)(2,1)S(1)} collective-permute-done((bf16[768,128]{1,0:T(8,128)(2,1)S(1)}, bf16[768,128]{1,0:T(8,128)(2,1)S(1)}, u32[]{:S(2)}, u32[]{:S(2)}) %collective-permute-start.8) | collective-permute-done | bytes 196640 | tf_op jit(solution)/shard_map/ppermute | solution.py:70
  54.7 1.9 %collective-permute-start.9 = (bf16[512,128]{1,0:T(8,128)(2,1)S(1)}, bf16[512,128]{1,0:T(8,128)(2,1)S(1)}, u32[]{:S(2)}, u32[]{:S(2)}) collective-permute-start(bf16[512,128]{1,0:T(8,128)(2,1)S(1)} %convolution_convert_fusion.7), channel_id=1, source_target_pairs={{0,2},{1,3},{2,4},{3,5},{4,6},{5,7},{6,0},{7,1},{8,10},{9,11},{10,... | collective-permute-start | bytes 393224 | tf_op jit(solution)/shard_map/ppermute | solution.py:16
  86.0 4.4 %collective-permute-done.30 = bf16[512,128]{1,0:T(8,128)(2,1)S(1)} collective-permute-done((bf16[512,128]{1,0:T(8,128)(2,1)S(1)}, bf16[512,128]{1,0:T(8,128)(2,1)S(1)}, u32[]{:S(2)}, u32[]{:S(2)}) %collective-permute-start.30) | collective-permute-done | bytes 131104 | tf_op jit(solution)/shard_map/ppermute | solution.py:16
  90.9 2.3 %collective-permute-done.29 = bf16[512,128]{1,0:T(8,128)(2,1)S(1)} collective-permute-done((bf16[512,128]{1,0:T(8,128)(2,1)S(1)}, bf16[512,128]{1,0:T(8,128)(2,1)S(1)}, u32[]{:S(2)}, u32[]{:S(2)}) %collective-permute-start.29) | collective-permute-done | bytes 131104 | tf_op jit(solution)/shard_map/ppermute | solution.py:16
  93.9 2.1 %collective-permute-done.33 = bf16[512,128]{1,0:T(8,128)(2,1)S(1)} collective-permute-done((bf16[512,128]{1,0:T(8,128)(2,1)S(1)}, bf16[512,128]{1,0:T(8,128)(2,1)S(1)}, u32[]{:S(2)}, u32[]{:S(2)}) %collective-permute-start.33) | collective-permute-done | bytes 131104 | tf_op jit(solution)/shard_map/ppermute | solution.py:16
  96.4 2.1 %collective-permute-done.32 = bf16[512,128]{1,0:T(8,128)(2,1)S(1)} collective-permute-done((bf16[512,128]{1,0:T(8,128)(2,1)S(1)}, bf16[512,128]{1,0:T(8,128)(2,1)S(1)}, u32[]{:S(2)}, u32[]{:S(2)}) %collective-permute-start.32) | collective-permute-done | bytes 131104 | tf_op jit(solution)/shard_map/ppermute | solution.py:16
  99.2 2.1 %collective-permute-done.36 = bf16[512,128]{1,0:T(8,128)(2,1)S(1)} collective-permute-done((bf16[512,128]{1,0:T(8,128)(2,1)S(1)}, bf16[512,128]{1,0:T(8,128)(2,1)S(1)}, u32[]{:S(2)}, u32[]{:S(2)}) %collective-permute-start.36) | collective-permute-done | bytes 131104 | tf_op jit(solution)/shard_map/ppermute | solution.py:16
  101.3 2.9 %collective-permute-done.35 = bf16[512,128]{1,0:T(8,128)(2,1)S(1)} collective-permute-done((bf16[512,128]{1,0:T(8,128)(2,1)S(1)}, bf16[512,128]{1,0:T(8,128)(2,1)S(1)}, u32[]{:S(2)}, u32[]{:S(2)}) %collective-permute-start.35) | collective-permute-done | bytes 131104 | tf_op jit(solution)/shard_map/ppermute | solution.py:16
  106.4 1.7 collective-permute-start.37
  108.1 4.3 %collective-permute-start.41 = (bf16[512,128]{1,0:T(8,128)(2,1)S(1)}, bf16[512,128]{1,0:T(8,128)(2,1)S(1)}, u32[]{:S(2)}, u32[]{:S(2)}) collective-permute-start(bf16[512,128]{1,0:T(8,128)(2,1)S(1)} %collective-permute-done.39), channel_id=1, source_target_pairs={{0,2},{1,3},{2,4},{3,5},{4,6},{5,7},{6,0},{7,1},{8,10},{9,11},{10,... | collective-permute-start | bytes 393224 | tf_op jit(solution)/shard_map/ppermute | solution.py:16
  112.9 2.6 %collective-permute-done.43 = bf16[512,128]{1,0:T(8,128)(2,1)S(1)} collective-permute-done((bf16[512,128]{1,0:T(8,128)(2,1)S(1)}, bf16[512,128]{1,0:T(8,128)(2,1)S(1)}, u32[]{:S(2)}, u32[]{:S(2)}) %collective-permute-start.43) | collective-permute-done | bytes 131104 | tf_op jit(solution)/shard_map/ppermute | solution.py:16
  118.8 2.3 %collective-permute-done.41 = bf16[512,128]{1,0:T(8,128)(2,1)S(1)} collective-permute-done((bf16[512,128]{1,0:T(8,128)(2,1)S(1)}, bf16[512,128]{1,0:T(8,128)(2,1)S(1)}, u32[]{:S(2)}, u32[]{:S(2)}) %collective-permute-start.41) | collective-permute-done | bytes 131104 | tf_op jit(solution)/shard_map/ppermute | solution.py:16
  121.5 2.4 %collective-permute-done.40 = bf16[512,128]{1,0:T(8,128)(2,1)S(1)} collective-permute-done((bf16[512,128]{1,0:T(8,128)(2,1)S(1)}, bf16[512,128]{1,0:T(8,128)(2,1)S(1)}, u32[]{:S(2)}, u32[]{:S(2)}) %collective-permute-start.40) | collective-permute-done | bytes 131104 | tf_op jit(solution)/shard_map/ppermute | solution.py:16
  127.7 1.8 %collective-permute-done.45 = bf16[512,128]{1,0:T(8,128)(2,1)S(1)} collective-permute-done((bf16[512,128]{1,0:T(8,128)(2,1)S(1)}, bf16[512,128]{1,0:T(8,128)(2,1)S(1)}, u32[]{:S(2)}, u32[]{:S(2)}) %collective-permute-start.45) | collective-permute-done | bytes 131104 | tf_op jit(solution)/shard_map/ppermute | solution.py:16
  133.4 1.7 collective-permute-done.51
  143.2 2.1 %collective-permute-start.56 = (bf16[512,128]{1,0:T(8,128)(2,1)S(1)}, bf16[512,128]{1,0:T(8,128)(2,1)S(1)}, u32[]{:S(2)}, u32[]{:S(2)}) collective-permute-start(bf16[512,128]{1,0:T(8,128)(2,1)S(1)} %add_convert_fusion.5), channel_id=1, source_target_pairs={{0,2},{1,3},{2,4},{3,5},{4,6},{5,7},{6,0},{7,1},{8,10},{9,11},{10,... | collective-permute-start | bytes 393224 | tf_op jit(solution)/shard_map/ppermute | solution.py:16
  149.2 2.3 %collective-permute-done.52 = bf16[512,128]{1,0:T(8,128)(2,1)S(1)} collective-permute-done((bf16[512,128]{1,0:T(8,128)(2,1)S(1)}, bf16[512,128]{1,0:T(8,128)(2,1)S(1)}, u32[]{:S(2)}, u32[]{:S(2)}) %collective-permute-start.52) | collective-permute-done | bytes 131104 | tf_op jit(solution)/shard_map/ppermute | solution.py:16
  152.1 2.3 %collective-permute-done.56 = bf16[512,128]{1,0:T(8,128)(2,1)S(1)} collective-permute-done((bf16[512,128]{1,0:T(8,128)(2,1)S(1)}, bf16[512,128]{1,0:T(8,128)(2,1)S(1)}, u32[]{:S(2)}, u32[]{:S(2)}) %collective-permute-start.56) | collective-permute-done | bytes 131104 | tf_op jit(solution)/shard_map/ppermute | solution.py:16
  157.7 2.3 %collective-permute-done.59 = bf16[512,128]{1,0:T(8,128)(2,1)S(1)} collective-permute-done((bf16[512,128]{1,0:T(8,128)(2,1)S(1)}, bf16[512,128]{1,0:T(8,128)(2,1)S(1)}, u32[]{:S(2)}, u32[]{:S(2)}) %collective-permute-start.59) | collective-permute-done | bytes 131104 | tf_op jit(solution)/shard_map/ppermute | solution.py:16
  160.5 2.3 %collective-permute-done.58 = bf16[512,128]{1,0:T(8,128)(2,1)S(1)} collective-permute-done((bf16[512,128]{1,0:T(8,128)(2,1)S(1)}, bf16[512,128]{1,0:T(8,128)(2,1)S(1)}, u32[]{:S(2)}, u32[]{:S(2)}) %collective-permute-start.58) | collective-permute-done | bytes 131104 | tf_op jit(solution)/shard_map/ppermute | solution.py:16
  165.3 3.0 %collective-permute-done.62 = bf16[512,128]{1,0:T(8,128)(2,1)S(1)} collective-permute-done((bf16[512,128]{1,0:T(8,128)(2,1)S(1)}, bf16[512,128]{1,0:T(8,128)(2,1)S(1)}, u32[]{:S(2)}, u32[]{:S(2)}) %collective-permute-start.62) | collective-permute-done | bytes 131104 | tf_op jit(solution)/shard_map/ppermute | solution.py:16
  169.6 2.4 %collective-permute-done.65 = bf16[512,128]{1,0:T(8,128)(2,1)S(1)} collective-permute-done((bf16[512,128]{1,0:T(8,128)(2,1)S(1)}, bf16[512,128]{1,0:T(8,128)(2,1)S(1)}, u32[]{:S(2)}, u32[]{:S(2)}) %collective-permute-start.65) | collective-permute-done | bytes 131104 | tf_op jit(solution)/shard_map/ppermute | solution.py:16
  174.5 3.1 %collective-permute-done.66 = bf16[512,128]{1,0:T(8,128)(2,1)S(1)} collective-permute-done((bf16[512,128]{1,0:T(8,128)(2,1)S(1)}, bf16[512,128]{1,0:T(8,128)(2,1)S(1)}, u32[]{:S(2)}, u32[]{:S(2)}) %collective-permute-start.66) | collective-permute-done | bytes 131104 | tf_op jit(solution)/shard_map/ppermute | solution.py:16
  (215 shorter events, 96.0 us)
Async XLA Ops:
  3.6 37.6 %collective-permute-start.1 = (bf16[384,2048]{1,0:T(8,128)(2,1)}, bf16[384,2048]{1,0:T(8,128)(2,1)}, u32[]{:S(2)}, u32[]{:S(2)}) collective-permute-start(bf16[384,2048]{1,0:T(8,128)(2,1)} %pad_maximum_fusion), channel_id=1, source_target_pairs={{0,1},{1,0},{2,3},{3,2},{4,5},{5,4},{6,7},{7,6},{8,9},{9,8},{10,11... | collective-permute-start | bytes 4718600 | tf_op jit(solution)/shard_map/ppermute | solution.py:89
  9.0 9.6 %collective-permute-start.5 = (bf16[512,128]{1,0:T(8,128)(2,1)S(1)}, bf16[512,128]{1,0:T(8,128)(2,1)}, u32[]{:S(2)}, u32[]{:S(2)}) collective-permute-start(bf16[512,128]{1,0:T(8,128)(2,1)S(1)} %get-tuple-element.242), channel_id=1, source_target_pairs={{0,2},{1,3},{2,4},{3,5},{4,6},{5,7},{6,0},{7,1},{8,10},{9,11},{10,... | collective-permute-start | bytes 393224 | tf_op jit(solution)/shard_map/ppermute | solution.py:16
  10.6 10.8 %collective-permute-start.11 = (bf16[512,128]{1,0:T(8,128)(2,1)S(1)}, bf16[512,128]{1,0:T(8,128)(2,1)}, u32[]{:S(2)}, u32[]{:S(2)}) collective-permute-start(bf16[512,128]{1,0:T(8,128)(2,1)S(1)} %get-tuple-element.241), channel_id=1, source_target_pairs={{0,2},{1,3},{2,4},{3,5},{4,6},{5,7},{6,0},{7,1},{8,10},{9,11},{10,... | collective-permute-start | bytes 393224 | tf_op jit(solution)/shard_map/ppermute | solution.py:16
  12.1 12.0 %collective-permute-start.14 = (bf16[512,128]{1,0:T(8,128)(2,1)S(1)}, bf16[512,128]{1,0:T(8,128)(2,1)}, u32[]{:S(2)}, u32[]{:S(2)}) collective-permute-start(bf16[512,128]{1,0:T(8,128)(2,1)S(1)} %get-tuple-element.244), channel_id=1, source_target_pairs={{0,2},{1,3},{2,4},{3,5},{4,6},{5,7},{6,0},{7,1},{8,10},{9,11},{10,... | collective-permute-start | bytes 393224 | tf_op jit(solution)/shard_map/ppermute | solution.py:16
  15.7 11.2 %collective-permute-start.3 = (bf16[512,128]{1,0:T(8,128)(2,1)}, bf16[512,128]{1,0:T(8,128)(2,1)}, u32[]{:S(2)}, u32[]{:S(2)}) collective-permute-start(bf16[512,128]{1,0:T(8,128)(2,1)} %collective-permute-done.2), channel_id=1, source_target_pairs={{0,2},{1,3},{2,4},{3,5},{4,6},{5,7},{6,0},{7,1},{8,10},{9,11},{10,... | collective-permute-start | bytes 393224 | tf_op jit(solution)/shard_map/ppermute | solution.py:16
  18.5 11.2 %collective-permute-start.6 = (bf16[512,128]{1,0:T(8,128)(2,1)}, bf16[512,128]{1,0:T(8,128)(2,1)}, u32[]{:S(2)}, u32[]{:S(2)}) collective-permute-start(bf16[512,128]{1,0:T(8,128)(2,1)} %collective-permute-done.5), channel_id=1, source_target_pairs={{0,2},{1,3},{2,4},{3,5},{4,6},{5,7},{6,0},{7,1},{8,10},{9,11},{10,... | collective-permute-start | bytes 393224 | tf_op jit(solution)/shard_map/ppermute | solution.py:16
  21.3 11.4 %collective-permute-start.12 = (bf16[512,128]{1,0:T(8,128)(2,1)}, bf16[512,128]{1,0:T(8,128)(2,1)}, u32[]{:S(2)}, u32[]{:S(2)}) collective-permute-start(bf16[512,128]{1,0:T(8,128)(2,1)} %collective-permute-done.11), channel_id=1, source_target_pairs={{0,2},{1,3},{2,4},{3,5},{4,6},{5,7},{6,0},{7,1},{8,10},{9,11},{10,... | collective-permute-start | bytes 393224 | tf_op jit(solution)/shard_map/ppermute | solution.py:16
  24.1 11.2 %collective-permute-start.15 = (bf16[512,128]{1,0:T(8,128)(2,1)}, bf16[512,128]{1,0:T(8,128)(2,1)}, u32[]{:S(2)}, u32[]{:S(2)}) collective-permute-start(bf16[512,128]{1,0:T(8,128)(2,1)} %collective-permute-done.14), channel_id=1, source_target_pairs={{0,2},{1,3},{2,4},{3,5},{4,6},{5,7},{6,0},{7,1},{8,10},{9,11},{10,... | collective-permute-start | bytes 393224 | tf_op jit(solution)/shard_map/ppermute | solution.py:16
  27.0 11.2 %collective-permute-start.4 = (bf16[512,128]{1,0:T(8,128)(2,1)}, bf16[512,128]{1,0:T(8,128)(2,1)}, u32[]{:S(2)}, u32[]{:S(2)}) collective-permute-start(bf16[512,128]{1,0:T(8,128)(2,1)} %collective-permute-done.3), channel_id=1, source_target_pairs={{0,2},{1,3},{2,4},{3,5},{4,6},{5,7},{6,0},{7,1},{8,10},{9,11},{10,... | collective-permute-start | bytes 393224 | tf_op jit(solution)/shard_map/ppermute | solution.py:16
  29.8 9.9 %collective-permute-start.7 = (bf16[512,128]{1,0:T(8,128)(2,1)}, bf16[512,128]{1,0:T(8,128)(2,1)}, u32[]{:S(2)}, u32[]{:S(2)}) collective-permute-start(bf16[512,128]{1,0:T(8,128)(2,1)} %collective-permute-done.6), channel_id=1, source_target_pairs={{0,2},{1,3},{2,4},{3,5},{4,6},{5,7},{6,0},{7,1},{8,10},{9,11},{10,... | collective-permute-start | bytes 393224 | tf_op jit(solution)/shard_map/ppermute | solution.py:16
  32.8 14.5 %collective-permute-start = (f32[520,512]{1,0:T(8,128)S(1)}, f32[520,512]{1,0:T(8,128)S(1)}, u32[]{:S(2)}, u32[]{:S(2)}) collective-permute-start(f32[520,512]{1,0:T(8,128)S(1)} %concatenate.35), channel_id=1, source_target_pairs={{0,8},{8,16},{16,24},{24,0},{1,9},{9,17},{17,25},{25,1},{2,10},{10... | collective-permute-start | bytes 3194888 | tf_op jit(solution)/shard_map/ppermute | solution.py:16
  35.4 11.9 %collective-permute-start.13 = (bf16[512,128]{1,0:T(8,128)(2,1)}, bf16[512,128]{1,0:T(8,128)(2,1)S(1)}, u32[]{:S(2)}, u32[]{:S(2)}) collective-permute-start(bf16[512,128]{1,0:T(8,128)(2,1)} %collective-permute-done.12), channel_id=1, source_target_pairs={{0,2},{1,3},{2,4},{3,5},{4,6},{5,7},{6,0},{7,1},{8,10},{9,11},{10,... | collective-permute-start | bytes 393224 | tf_op jit(solution)/shard_map/ppermute | solution.py:16
  38.2 9.1 %collective-permute-start.16 = (bf16[512,128]{1,0:T(8,128)(2,1)}, bf16[512,128]{1,0:T(8,128)(2,1)S(1)}, u32[]{:S(2)}, u32[]{:S(2)}) collective-permute-start(bf16[512,128]{1,0:T(8,128)(2,1)} %collective-permute-done.15), channel_id=1, source_target_pairs={{0,2},{1,3},{2,4},{3,5},{4,6},{5,7},{6,0},{7,1},{8,10},{9,11},{10,... | collective-permute-start | bytes 393224 | tf_op jit(solution)/shard_map/ppermute | solution.py:16
  46.9 11.2 %collective-permute-start.10 = (bf16[768,128]{1,0:T(8,128)(2,1)S(1)}, bf16[768,128]{1,0:T(8,128)(2,1)S(1)}, u32[]{:S(2)}, u32[]{:S(2)}) collective-permute-start(bf16[768,128]{1,0:T(8,128)(2,1)S(1)} %get-tuple-element.112), channel_id=1, source_target_pairs={{0,1},{1,0},{2,3},{3,2},{4,5},{5,4},{6,7},{7,6},{8,9},{9,8},{10,11... | collective-permute-start | bytes 589832 | tf_op jit(solution)/shard_map/ppermute | solution.py:70
  63.4 8.7 %collective-permute-start.23 = (bf16[768,128]{1,0:T(8,128)(2,1)S(1)}, bf16[768,128]{1,0:T(8,128)(2,1)S(1)}, u32[]{:S(2)}, u32[]{:S(2)}) collective-permute-start(bf16[768,128]{1,0:T(8,128)(2,1)S(1)} %get-tuple-element.123), channel_id=1, source_target_pairs={{0,1},{1,0},{2,3},{3,2},{4,5},{5,4},{6,7},{7,6},{8,9},{9,8},{10,11... | collective-permute-start | bytes 589832 | tf_op jit(solution)/shard_map/ppermute | solution.py:70
  68.4 9.0 %collective-permute-start.21 = (bf16[512,128]{1,0:T(8,128)(2,1)S(1)}, bf16[512,128]{1,0:T(8,128)(2,1)S(1)}, u32[]{:S(2)}, u32[]{:S(2)}) collective-permute-start(bf16[512,128]{1,0:T(8,128)(2,1)S(1)} %add_convert_fusion.14), channel_id=1, source_target_pairs={{0,2},{1,3},{2,4},{3,5},{4,6},{5,7},{6,0},{7,1},{8,10},{9,11},{10,... | collective-permute-start | bytes 393224 | tf_op jit(solution)/shard_map/ppermute | solution.py:16
  83.6 9.5 %collective-permute-start.29 = (bf16[512,128]{1,0:T(8,128)(2,1)S(1)}, bf16[512,128]{1,0:T(8,128)(2,1)S(1)}, u32[]{:S(2)}, u32[]{:S(2)}) collective-permute-start(bf16[512,128]{1,0:T(8,128)(2,1)S(1)} %add_convert_fusion.9), channel_id=1, source_target_pairs={{0,2},{1,3},{2,4},{3,5},{4,6},{5,7},{6,0},{7,1},{8,10},{9,11},{10,... | collective-permute-start | bytes 393224 | tf_op jit(solution)/shard_map/ppermute | solution.py:16
  85.3 10.7 %collective-permute-start.33 = (bf16[512,128]{1,0:T(8,128)(2,1)S(1)}, bf16[512,128]{1,0:T(8,128)(2,1)S(1)}, u32[]{:S(2)}, u32[]{:S(2)}) collective-permute-start(bf16[512,128]{1,0:T(8,128)(2,1)S(1)} %divide_convert_fusion.3), channel_id=1, source_target_pairs={{0,2},{1,3},{2,4},{3,5},{4,6},{5,7},{6,0},{7,1},{8,10},{9,11},{10,... | collective-permute-start | bytes 393224 | tf_op jit(solution)/shard_map/ppermute | solution.py:16
  99.1 9.0 %collective-permute-start.39 = (bf16[512,128]{1,0:T(8,128)(2,1)S(1)}, bf16[512,128]{1,0:T(8,128)(2,1)S(1)}, u32[]{:S(2)}, u32[]{:S(2)}) collective-permute-start(bf16[512,128]{1,0:T(8,128)(2,1)S(1)} %divide_convert_fusion.1), channel_id=1, source_target_pairs={{0,2},{1,3},{2,4},{3,5},{4,6},{5,7},{6,0},{7,1},{8,10},{9,11},{10,... | collective-permute-start | bytes 393224 | tf_op jit(solution)/shard_map/ppermute | solution.py:16
  104.6 10.9 %collective-permute-start.43 = (bf16[512,128]{1,0:T(8,128)(2,1)S(1)}, bf16[512,128]{1,0:T(8,128)(2,1)S(1)}, u32[]{:S(2)}, u32[]{:S(2)}) collective-permute-start(bf16[512,128]{1,0:T(8,128)(2,1)S(1)} %collective-permute-done.35), channel_id=1, source_target_pairs={{0,2},{1,3},{2,4},{3,5},{4,6},{5,7},{6,0},{7,1},{8,10},{9,11},{10,... | collective-permute-start | bytes 393224 | tf_op jit(solution)/shard_map/ppermute | solution.py:16
  105.3 13.1 %collective-permute-start.42 = (bf16[512,128]{1,0:T(8,128)(2,1)S(1)}, bf16[512,128]{1,0:T(8,128)(2,1)S(1)}, u32[]{:S(2)}, u32[]{:S(2)}) collective-permute-start(bf16[512,128]{1,0:T(8,128)(2,1)S(1)} %get-tuple-element.163), channel_id=1, source_target_pairs={{0,2},{1,3},{2,4},{3,5},{4,6},{5,7},{6,0},{7,1},{8,10},{9,11},{10,... | collective-permute-start | bytes 393224 | tf_op jit(solution)/shard_map/ppermute | solution.py:16
  106.4 49.6 %collective-permute-start.37 = (bf16[528,512]{1,0:T(8,128)(2,1)S(1)}, bf16[528,512]{1,0:T(8,128)(2,1)S(1)}, u32[]{:S(2)}, u32[]{:S(2)}) collective-permute-start(bf16[528,512]{1,0:T(8,128)(2,1)S(1)} %pad_maximum_fusion.1), channel_id=1, source_target_pairs={{0,16},{8,24},{16,0},{24,8},{1,17},{9,25},{17,1},{25,9},{2,18},{10... | collective-permute-start | bytes 1622024 | tf_op jit(solution)/shard_map/ppermute | solution.py:16
  108.1 13.0 %collective-permute-start.41 = (bf16[512,128]{1,0:T(8,128)(2,1)S(1)}, bf16[512,128]{1,0:T(8,128)(2,1)S(1)}, u32[]{:S(2)}, u32[]{:S(2)}) collective-permute-start(bf16[512,128]{1,0:T(8,128)(2,1)S(1)} %collective-permute-done.39), channel_id=1, source_target_pairs={{0,2},{1,3},{2,4},{3,5},{4,6},{5,7},{6,0},{7,1},{8,10},{9,11},{10,... | collective-permute-start | bytes 393224 | tf_op jit(solution)/shard_map/ppermute | solution.py:16
  112.8 11.2 %collective-permute-start.40 = (bf16[512,128]{1,0:T(8,128)(2,1)S(1)}, bf16[512,128]{1,0:T(8,128)(2,1)S(1)}, u32[]{:S(2)}, u32[]{:S(2)}) collective-permute-start(bf16[512,128]{1,0:T(8,128)(2,1)S(1)} %collective-permute-done.38), channel_id=1, source_target_pairs={{0,2},{1,3},{2,4},{3,5},{4,6},{5,7},{6,0},{7,1},{8,10},{9,11},{10,... | collective-permute-start | bytes 393224 | tf_op jit(solution)/shard_map/ppermute | solution.py:16
  117.2 9.3 %collective-permute-start.47 = (bf16[768,128]{1,0:T(8,128)(2,1)S(1)}, bf16[768,128]{1,0:T(8,128)(2,1)S(1)}, u32[]{:S(2)}, u32[]{:S(2)}) collective-permute-start(bf16[768,128]{1,0:T(8,128)(2,1)S(1)} %get-tuple-element.170), channel_id=1, source_target_pairs={{0,1},{1,0},{2,3},{3,2},{4,5},{5,4},{6,7},{7,6},{8,9},{9,8},{10,11... | collective-permute-start | bytes 589832 | tf_op jit(solution)/shard_map/ppermute | solution.py:70
  127.0 9.8 %collective-permute-start.50 = (bf16[512,128]{1,0:T(8,128)(2,1)S(1)}, bf16[512,128]{1,0:T(8,128)(2,1)S(1)}, u32[]{:S(2)}, u32[]{:S(2)}) collective-permute-start(bf16[512,128]{1,0:T(8,128)(2,1)S(1)} %collective-permute-done.46), channel_id=1, source_target_pairs={{0,2},{1,3},{2,4},{3,5},{4,6},{5,7},{6,0},{7,1},{8,10},{9,11},{10,... | collective-permute-start | bytes 393224 | tf_op jit(solution)/shard_map/ppermute | solution.py:16
  131.2 8.8 %collective-permute-start.49 = (bf16[768,128]{1,0:T(8,128)(2,1)S(1)}, bf16[768,128]{1,0:T(8,128)(2,1)S(1)}, u32[]{:S(2)}, u32[]{:S(2)}) collective-permute-start(bf16[768,128]{1,0:T(8,128)(2,1)S(1)} %get-tuple-element.182), channel_id=1, source_target_pairs={{0,1},{1,0},{2,3},{3,2},{4,5},{5,4},{6,7},{7,6},{8,9},{9,8},{10,11... | collective-permute-start | bytes 589832 | tf_op jit(solution)/shard_map/ppermute | solution.py:70
  141.8 9.8 %collective-permute-start.52 = (bf16[512,128]{1,0:T(8,128)(2,1)S(1)}, bf16[512,128]{1,0:T(8,128)(2,1)S(1)}, u32[]{:S(2)}, u32[]{:S(2)}) collective-permute-start(bf16[512,128]{1,0:T(8,128)(2,1)S(1)} %add_convert_fusion.6), channel_id=1, source_target_pairs={{0,2},{1,3},{2,4},{3,5},{4,6},{5,7},{6,0},{7,1},{8,10},{9,11},{10,... | collective-permute-start | bytes 393224 | tf_op jit(solution)/shard_map/ppermute | solution.py:16
  143.2 11.2 %collective-permute-start.56 = (bf16[512,128]{1,0:T(8,128)(2,1)S(1)}, bf16[512,128]{1,0:T(8,128)(2,1)S(1)}, u32[]{:S(2)}, u32[]{:S(2)}) collective-permute-start(bf16[512,128]{1,0:T(8,128)(2,1)S(1)} %add_convert_fusion.5), channel_id=1, source_target_pairs={{0,2},{1,3},{2,4},{3,5},{4,6},{5,7},{6,0},{7,1},{8,10},{9,11},{10,... | collective-permute-start | bytes 393224 | tf_op jit(solution)/shard_map/ppermute | solution.py:16
  145.8 11.4 %collective-permute-start.60 = (bf16[512,128]{1,0:T(8,128)(2,1)S(1)}, bf16[512,128]{1,0:T(8,128)(2,1)S(1)}, u32[]{:S(2)}, u32[]{:S(2)}) collective-permute-start(bf16[512,128]{1,0:T(8,128)(2,1)S(1)} %convolution_convert_fusion), channel_id=1, source_target_pairs={{0,2},{1,3},{2,4},{3,5},{4,6},{5,7},{6,0},{7,1},{8,10},{9,11},{10,... | collective-permute-start | bytes 393224 | tf_op jit(solution)/shard_map/ppermute | solution.py:16
  149.2 10.8 %collective-permute-start.59 = (bf16[512,128]{1,0:T(8,128)(2,1)S(1)}, bf16[512,128]{1,0:T(8,128)(2,1)S(1)}, u32[]{:S(2)}, u32[]{:S(2)}) collective-permute-start(bf16[512,128]{1,0:T(8,128)(2,1)S(1)} %add_convert_fusion.4), channel_id=1, source_target_pairs={{0,2},{1,3},{2,4},{3,5},{4,6},{5,7},{6,0},{7,1},{8,10},{9,11},{10,... | collective-permute-start | bytes 393224 | tf_op jit(solution)/shard_map/ppermute | solution.py:16
  152.0 10.8 %collective-permute-start.58 = (bf16[512,128]{1,0:T(8,128)(2,1)S(1)}, bf16[512,128]{1,0:T(8,128)(2,1)S(1)}, u32[]{:S(2)}, u32[]{:S(2)}) collective-permute-start(bf16[512,128]{1,0:T(8,128)(2,1)S(1)} %add_convert_fusion.3), channel_id=1, source_target_pairs={{0,2},{1,3},{2,4},{3,5},{4,6},{5,7},{6,0},{7,1},{8,10},{9,11},{10,... | collective-permute-start | bytes 393224 | tf_op jit(solution)/shard_map/ppermute | solution.py:16
  (44 other events, 328.4 us)

commit v6 on v5

--- a/solution.py
+++ b/solution.py
@@ -83,18 +83,21 @@
         return jnp.concatenate(pieces, axis=1)
 
     def column_block(back):
-        return pair_tokens[:, back * block : (back + 1) * block]
+        return joined[0][:, back * block : (back + 1) * block]
 
     outgoing = half_columns(inputs, 1 - lane)
     theirs = lax.ppermute(outgoing, "fsdp", [(i, i ^ 1) for i in range(count)])
     params = after(params, outgoing)
     momentum = after(momentum, outgoing)
     zero = jnp.zeros((), lane.dtype)
-    pair_tokens = jnp.zeros((2 * rows, width // 2), inputs.dtype)
-    pair_tokens = lax.dynamic_update_slice(
-        pair_tokens, half_columns(after(inputs, outgoing), lane), (lane * rows, zero)
-    )
-    pair_tokens = lax.dynamic_update_slice(pair_tokens, theirs, ((1 - lane) * rows, zero))
+    mine = half_columns(after(inputs, outgoing), lane)
+
+    def in_lane_order(own, other):
+        both = jnp.zeros((2 * rows, own.shape[1]), own.dtype)
+        both = lax.dynamic_update_slice(both, own, (lane * rows, zero))
+        return lax.dynamic_update_slice(both, other, ((1 - lane) * rows, zero))
+
+    joined = []
     pair_targets = lax.dynamic_update_slice(
         jnp.zeros((2 * rows, features), targets.dtype), targets[0], (lane * rows, zero)
     )
@@ -145,7 +148,13 @@
             last = after(pieces[-1], issued[-1]) if issued else pieces[-1]
             both.append(jnp.concatenate(pieces[:-1] + [last], axis=0))
         both = after(jnp.concatenate(both, axis=1))
-        both = jnp.dot(pair_tokens, both, preferred_element_type=wide)
+        if joined:
+            both = jnp.dot(joined[0], both, preferred_element_type=wide)
+        else:
+            both = in_lane_order(
+                jnp.dot(mine, both, preferred_element_type=wide),
+                jnp.dot(theirs, both, preferred_element_type=wide),
+            )
         first_keys.extend([both[:, :part], both[:, part:]])
 
     multiply_first()
@@ -199,6 +208,7 @@
         value, link = streams[c].send(came[c])
         came[c] = send(value, link, 2 ** mixings[c])
         if len(issued) == 2:
+            joined.append(in_lane_order(mine, after(theirs, issued[-1])))
             while len(first_keys) < CHUNKS:
                 multiply_first()
             read_passed(0)

time: 179 us -> 177 us (0.989)
  waiting for transfers between devices: 86 us -> 83 us
  starting transfers between devices: 44.1 us -> 42.2 us
    ppermute x58, starting transfers between devices: 32.2 us -> 30.3 us  [from_behind(): return lax.ppermute(value, axis, pairs)]
  transfers between devices with their start and end apart: 67 -> 67, of which waited for: 47 -> 48; matrix products, arithmetic and copies ran while one was open for 23% -> 25% of each run, Pallas kernels for 0% -> 0%
where the time goes in v6:
time: 177 us
  waiting for transfers between devices  83 us (47%)
  starting transfers between devices  42.2 us (24%)
  matrix products  26.2 us (15%)
  other arithmetic  13.4 us (8%)
  local copies, waits for them, and re-layouts  9.56 us (5%)
  between operations  2.24 us (1%)
    ppermute x58, waiting for transfers between devices, from_behind(): return lax.ppermute(value, axis, pairs)  80.5 us
    ppermute x58, starting transfers between devices, from_behind(): return lax.ppermute(value, axis, pairs)  30.3 us
    dot_general x32, matrix products, partial(): lax.dot_general(column_block(back), grad_out, contract, preferred_element...  13.1 us
    dot_general x16, matrix products, stream(): jnp.dot(column_block(back), piece, preferred_element_type=wide)  9.55 us
    ppermute x8, starting transfers between devices, send(): return lax.ppermute(value, 'fsdp', [(i, i ^ 1) for i in range(count)])  8.94 us
  transfers between devices with their start and end apart: 67, of which 48 were waited for; matrix products, arithmetic and copies ran while one was open for 25% of the time, Pallas kernels for 0%

profile of v6, /device:TPU:0, one launch (start us, length us, event | category | flops | bytes accessed | tf_op | source)
XLA Modules:
  0.0 176.6 jit_solution(9842609384414304012)
XLA Ops:
  3.6 2.9 %collective-permute-start.7 = (bf16[384,2048]{1,0:T(8,128)(2,1)}, bf16[384,2048]{1,0:T(8,128)(2,1)}, u32[]{:S(2)}, u32[]{:S(2)}) collective-permute-start(bf16[384,2048]{1,0:T(8,128)(2,1)} %pad_maximum_fusion), channel_id=1, source_target_pairs={{0,1},{1,0},{2,3},{3,2},{4,5},{5,4},{6,7},{7,6},{8,9},{9,8},{10,11... | collective-permute-start | bytes 4718600 | tf_op jit(solution)/shard_map/ppermute | solution.py:89
  17.1 2.1 %collective-permute-done.1 = bf16[512,128]{1,0:T(8,128)(2,1)} collective-permute-done((bf16[512,128]{1,0:T(8,128)(2,1)S(1)}, bf16[512,128]{1,0:T(8,128)(2,1)}, u32[]{:S(2)}, u32[]{:S(2)}) %collective-permute-start.1) | collective-permute-done | bytes 131104 | tf_op jit(solution)/shard_map/ppermute | solution.py:16
  19.8 2.2 %collective-permute-done.14 = bf16[512,128]{1,0:T(8,128)(2,1)} collective-permute-done((bf16[512,128]{1,0:T(8,128)(2,1)}, bf16[512,128]{1,0:T(8,128)(2,1)}, u32[]{:S(2)}, u32[]{:S(2)}) %collective-permute-start.14) | collective-permute-done | bytes 131104 | tf_op jit(solution)/shard_map/ppermute | solution.py:16
  22.0 2.8 %collective-permute-done.11 = bf16[512,128]{1,0:T(8,128)(2,1)} collective-permute-done((bf16[512,128]{1,0:T(8,128)(2,1)}, bf16[512,128]{1,0:T(8,128)(2,1)}, u32[]{:S(2)}, u32[]{:S(2)}) %collective-permute-start.11) | collective-permute-done | bytes 131104 | tf_op jit(solution)/shard_map/ppermute | solution.py:16
  24.8 2.8 %collective-permute-done.5 = bf16[512,128]{1,0:T(8,128)(2,1)} collective-permute-done((bf16[512,128]{1,0:T(8,128)(2,1)}, bf16[512,128]{1,0:T(8,128)(2,1)}, u32[]{:S(2)}, u32[]{:S(2)}) %collective-permute-start.5) | collective-permute-done | bytes 131104 | tf_op jit(solution)/shard_map/ppermute | solution.py:16
  27.6 2.8 %collective-permute-done.2 = bf16[512,128]{1,0:T(8,128)(2,1)} collective-permute-done((bf16[512,128]{1,0:T(8,128)(2,1)}, bf16[512,128]{1,0:T(8,128)(2,1)}, u32[]{:S(2)}, u32[]{:S(2)}) %collective-permute-start.2) | collective-permute-done | bytes 131104 | tf_op jit(solution)/shard_map/ppermute | solution.py:16
  33.6 2.4 %collective-permute-done.12 = bf16[512,128]{1,0:T(8,128)(2,1)} collective-permute-done((bf16[512,128]{1,0:T(8,128)(2,1)}, bf16[512,128]{1,0:T(8,128)(2,1)}, u32[]{:S(2)}, u32[]{:S(2)}) %collective-permute-start.12) | collective-permute-done | bytes 131104 | tf_op jit(solution)/shard_map/ppermute | solution.py:16
  36.0 2.8 %collective-permute-done.6 = bf16[512,128]{1,0:T(8,128)(2,1)} collective-permute-done((bf16[512,128]{1,0:T(8,128)(2,1)}, bf16[512,128]{1,0:T(8,128)(2,1)}, u32[]{:S(2)}, u32[]{:S(2)}) %collective-permute-start.6) | collective-permute-done | bytes 131104 | tf_op jit(solution)/shard_map/ppermute | solution.py:16
  42.3 2.0 %convolution_dynamic-update-slice_fusion = f32[768,256]{1,0:T(8,128)S(1)} fusion(f32[768,256]{1,0:T(8,128)S(1)} %convolution_dynamic-update-slice_fusion.1, s32[]{:T(128)S(6)} %select_n.49, bf16[384,2048]{1,0:T(8,128)(2,1)} %collective-permute-done.7, bf16[2048,256]{1,0:T(8,128)(2,1)S(1)} %maximum_maximum_fusion), kind=kOutput, calls=%fused_computation.2 | convolution fusion | flops 402653184 | bytes 3014660 | tf_op jit(solution)/shard_map/dot_general | solution.py:156
  60.5 1.8 collective-permute-done.9
  65.5 1.8 %collective-permute-start.22 = (bf16[512,128]{1,0:T(8,128)(2,1)S(1)}, bf16[512,128]{1,0:T(8,128)(2,1)S(1)}, u32[]{:S(2)}, u32[]{:S(2)}) collective-permute-start(bf16[512,128]{1,0:T(8,128)(2,1)S(1)} %convolution_convert_fusion.5), channel_id=1, source_target_pairs={{0,2},{1,3},{2,4},{3,5},{4,6},{5,7},{6,0},{7,1},{8,10},{9,11},{10,... | collective-permute-start | bytes 393224 | tf_op jit(solution)/shard_map/ppermute | solution.py:16
  77.0 1.9 %collective-permute-start.27 = (bf16[512,128]{1,0:T(8,128)(2,1)S(1)}, bf16[512,128]{1,0:T(8,128)(2,1)S(1)}, u32[]{:S(2)}, u32[]{:S(2)}) collective-permute-start(bf16[512,128]{1,0:T(8,128)(2,1)S(1)} %add_convert_fusion.11), channel_id=1, source_target_pairs={{0,2},{1,3},{2,4},{3,5},{4,6},{5,7},{6,0},{7,1},{8,10},{9,11},{10,... | collective-permute-start | bytes 393224 | tf_op jit(solution)/shard_map/ppermute | solution.py:16
  85.7 4.3 %collective-permute-done.30 = bf16[512,128]{1,0:T(8,128)(2,1)S(1)} collective-permute-done((bf16[512,128]{1,0:T(8,128)(2,1)S(1)}, bf16[512,128]{1,0:T(8,128)(2,1)S(1)}, u32[]{:S(2)}, u32[]{:S(2)}) %collective-permute-start.30) | collective-permute-done | bytes 131104 | tf_op jit(solution)/shard_map/ppermute | solution.py:16
  90.5 2.3 %collective-permute-done.29 = bf16[512,128]{1,0:T(8,128)(2,1)S(1)} collective-permute-done((bf16[512,128]{1,0:T(8,128)(2,1)S(1)}, bf16[512,128]{1,0:T(8,128)(2,1)S(1)}, u32[]{:S(2)}, u32[]{:S(2)}) %collective-permute-start.29) | collective-permute-done | bytes 131104 | tf_op jit(solution)/shard_map/ppermute | solution.py:16
  93.5 2.1 %collective-permute-done.33 = bf16[512,128]{1,0:T(8,128)(2,1)S(1)} collective-permute-done((bf16[512,128]{1,0:T(8,128)(2,1)S(1)}, bf16[512,128]{1,0:T(8,128)(2,1)S(1)}, u32[]{:S(2)}, u32[]{:S(2)}) %collective-permute-start.33) | collective-permute-done | bytes 131104 | tf_op jit(solution)/shard_map/ppermute | solution.py:16
  96.3 1.8 %collective-permute-done.32 = bf16[512,128]{1,0:T(8,128)(2,1)S(1)} collective-permute-done((bf16[512,128]{1,0:T(8,128)(2,1)S(1)}, bf16[512,128]{1,0:T(8,128)(2,1)S(1)}, u32[]{:S(2)}, u32[]{:S(2)}) %collective-permute-start.32) | collective-permute-done | bytes 131104 | tf_op jit(solution)/shard_map/ppermute | solution.py:16
  99.2 1.8 collective-permute-done.36
  101.4 2.4 %collective-permute-done.35 = bf16[512,128]{1,0:T(8,128)(2,1)S(1)} collective-permute-done((bf16[512,128]{1,0:T(8,128)(2,1)S(1)}, bf16[512,128]{1,0:T(8,128)(2,1)S(1)}, u32[]{:S(2)}, u32[]{:S(2)}) %collective-permute-start.35) | collective-permute-done | bytes 131104 | tf_op jit(solution)/shard_map/ppermute | solution.py:16
  107.1 1.8 %collective-permute-start.41 = (bf16[512,128]{1,0:T(8,128)(2,1)S(1)}, bf16[512,128]{1,0:T(8,128)(2,1)S(1)}, u32[]{:S(2)}, u32[]{:S(2)}) collective-permute-start(bf16[512,128]{1,0:T(8,128)(2,1)S(1)} %collective-permute-done.39), channel_id=1, source_target_pairs={{0,2},{1,3},{2,4},{3,5},{4,6},{5,7},{6,0},{7,1},{8,10},{9,11},{10,... | collective-permute-start | bytes 393224 | tf_op jit(solution)/shard_map/ppermute | solution.py:16
  109.9 2.4 %collective-permute-start.40 = (bf16[512,128]{1,0:T(8,128)(2,1)S(1)}, bf16[512,128]{1,0:T(8,128)(2,1)S(1)}, u32[]{:S(2)}, u32[]{:S(2)}) collective-permute-start(bf16[512,128]{1,0:T(8,128)(2,1)S(1)} %collective-permute-done.38), channel_id=1, source_target_pairs={{0,2},{1,3},{2,4},{3,5},{4,6},{5,7},{6,0},{7,1},{8,10},{9,11},{10,... | collective-permute-start | bytes 393224 | tf_op jit(solution)/shard_map/ppermute | solution.py:16
  115.5 2.8 %collective-permute-done.41 = bf16[512,128]{1,0:T(8,128)(2,1)S(1)} collective-permute-done((bf16[512,128]{1,0:T(8,128)(2,1)S(1)}, bf16[512,128]{1,0:T(8,128)(2,1)S(1)}, u32[]{:S(2)}, u32[]{:S(2)}) %collective-permute-start.41) | collective-permute-done | bytes 131104 | tf_op jit(solution)/shard_map/ppermute | solution.py:16
  118.7 2.4 %collective-permute-done.40 = bf16[512,128]{1,0:T(8,128)(2,1)S(1)} collective-permute-done((bf16[512,128]{1,0:T(8,128)(2,1)S(1)}, bf16[512,128]{1,0:T(8,128)(2,1)S(1)}, u32[]{:S(2)}, u32[]{:S(2)}) %collective-permute-start.40) | collective-permute-done | bytes 131104 | tf_op jit(solution)/shard_map/ppermute | solution.py:16
  124.2 2.6 %collective-permute-done.45 = bf16[512,128]{1,0:T(8,128)(2,1)S(1)} collective-permute-done((bf16[512,128]{1,0:T(8,128)(2,1)S(1)}, bf16[512,128]{1,0:T(8,128)(2,1)S(1)}, u32[]{:S(2)}, u32[]{:S(2)}) %collective-permute-start.45) | collective-permute-done | bytes 131104 | tf_op jit(solution)/shard_map/ppermute | solution.py:16
  135.6 2.1 %collective-permute-start.54 = (bf16[768,128]{1,0:T(8,128)(2,1)S(1)}, bf16[768,128]{1,0:T(8,128)(2,1)S(1)}, u32[]{:S(2)}, u32[]{:S(2)}) collective-permute-start(bf16[768,128]{1,0:T(8,128)(2,1)S(1)} %get-tuple-element.190), channel_id=1, source_target_pairs={{0,1},{1,0},{2,3},{3,2},{4,5},{5,4},{6,7},{7,6},{8,9},{9,8},{10,11... | collective-permute-start | bytes 589832 | tf_op jit(solution)/shard_map/ppermute | solution.py:70
  142.9 2.0 %collective-permute-start.60 = (bf16[512,128]{1,0:T(8,128)(2,1)S(1)}, bf16[512,128]{1,0:T(8,128)(2,1)S(1)}, u32[]{:S(2)}, u32[]{:S(2)}) collective-permute-start(bf16[512,128]{1,0:T(8,128)(2,1)S(1)} %convolution_convert_fusion), channel_id=1, source_target_pairs={{0,2},{1,3},{2,4},{3,5},{4,6},{5,7},{6,0},{7,1},{8,10},{9,11},{10,... | collective-permute-start | bytes 393224 | tf_op jit(solution)/shard_map/ppermute | solution.py:16
  147.0 2.3 %collective-permute-done.52 = bf16[512,128]{1,0:T(8,128)(2,1)S(1)} collective-permute-done((bf16[512,128]{1,0:T(8,128)(2,1)S(1)}, bf16[512,128]{1,0:T(8,128)(2,1)S(1)}, u32[]{:S(2)}, u32[]{:S(2)}) %collective-permute-start.52) | collective-permute-done | bytes 131104 | tf_op jit(solution)/shard_map/ppermute | solution.py:16
  149.8 2.3 %collective-permute-done.56 = bf16[512,128]{1,0:T(8,128)(2,1)S(1)} collective-permute-done((bf16[512,128]{1,0:T(8,128)(2,1)S(1)}, bf16[512,128]{1,0:T(8,128)(2,1)S(1)}, u32[]{:S(2)}, u32[]{:S(2)}) %collective-permute-start.56) | collective-permute-done | bytes 131104 | tf_op jit(solution)/shard_map/ppermute | solution.py:16
  155.4 2.3 %collective-permute-done.59 = bf16[512,128]{1,0:T(8,128)(2,1)S(1)} collective-permute-done((bf16[512,128]{1,0:T(8,128)(2,1)S(1)}, bf16[512,128]{1,0:T(8,128)(2,1)S(1)}, u32[]{:S(2)}, u32[]{:S(2)}) %collective-permute-start.59) | collective-permute-done | bytes 131104 | tf_op jit(solution)/shard_map/ppermute | solution.py:16
  158.5 2.1 %collective-permute-done.58 = bf16[512,128]{1,0:T(8,128)(2,1)S(1)} collective-permute-done((bf16[512,128]{1,0:T(8,128)(2,1)S(1)}, bf16[512,128]{1,0:T(8,128)(2,1)S(1)}, u32[]{:S(2)}, u32[]{:S(2)}) %collective-permute-start.58) | collective-permute-done | bytes 131104 | tf_op jit(solution)/shard_map/ppermute | solution.py:16
  163.0 3.1 %collective-permute-done.62 = bf16[512,128]{1,0:T(8,128)(2,1)S(1)} collective-permute-done((bf16[512,128]{1,0:T(8,128)(2,1)S(1)}, bf16[512,128]{1,0:T(8,128)(2,1)S(1)}, u32[]{:S(2)}, u32[]{:S(2)}) %collective-permute-start.62) | collective-permute-done | bytes 131104 | tf_op jit(solution)/shard_map/ppermute | solution.py:16
  167.4 2.3 %collective-permute-done.65 = bf16[512,128]{1,0:T(8,128)(2,1)S(1)} collective-permute-done((bf16[512,128]{1,0:T(8,128)(2,1)S(1)}, bf16[512,128]{1,0:T(8,128)(2,1)S(1)}, u32[]{:S(2)}, u32[]{:S(2)}) %collective-permute-start.65) | collective-permute-done | bytes 131104 | tf_op jit(solution)/shard_map/ppermute | solution.py:16
  172.2 3.0 %collective-permute-done.66 = bf16[512,128]{1,0:T(8,128)(2,1)S(1)} collective-permute-done((bf16[512,128]{1,0:T(8,128)(2,1)S(1)}, bf16[512,128]{1,0:T(8,128)(2,1)S(1)}, u32[]{:S(2)}, u32[]{:S(2)}) %collective-permute-start.66) | collective-permute-done | bytes 131104 | tf_op jit(solution)/shard_map/ppermute | solution.py:16
  (231 shorter events, 98.0 us)
Async XLA Ops:
  3.6 38.7 %collective-permute-start.7 = (bf16[384,2048]{1,0:T(8,128)(2,1)}, bf16[384,2048]{1,0:T(8,128)(2,1)}, u32[]{:S(2)}, u32[]{:S(2)}) collective-permute-start(bf16[384,2048]{1,0:T(8,128)(2,1)} %pad_maximum_fusion), channel_id=1, source_target_pairs={{0,1},{1,0},{2,3},{3,2},{4,5},{5,4},{6,7},{7,6},{8,9},{9,8},{10,11... | collective-permute-start | bytes 4718600 | tf_op jit(solution)/shard_map/ppermute | solution.py:89
  9.6 9.6 %collective-permute-start.1 = (bf16[512,128]{1,0:T(8,128)(2,1)S(1)}, bf16[512,128]{1,0:T(8,128)(2,1)}, u32[]{:S(2)}, u32[]{:S(2)}) collective-permute-start(bf16[512,128]{1,0:T(8,128)(2,1)S(1)} %get-tuple-element.245), channel_id=1, source_target_pairs={{0,2},{1,3},{2,4},{3,5},{4,6},{5,7},{6,0},{7,1},{8,10},{9,11},{10,... | collective-permute-start | bytes 393224 | tf_op jit(solution)/shard_map/ppermute | solution.py:16
  11.2 10.8 %collective-permute-start.14 = (bf16[512,128]{1,0:T(8,128)(2,1)}, bf16[512,128]{1,0:T(8,128)(2,1)}, u32[]{:S(2)}, u32[]{:S(2)}) collective-permute-start(bf16[512,128]{1,0:T(8,128)(2,1)} %get-tuple-element.246), channel_id=1, source_target_pairs={{0,2},{1,3},{2,4},{3,5},{4,6},{5,7},{6,0},{7,1},{8,10},{9,11},{10,... | collective-permute-start | bytes 393224 | tf_op jit(solution)/shard_map/ppermute | solution.py:16
  12.8 12.0 %collective-permute-start.11 = (bf16[512,128]{1,0:T(8,128)(2,1)}, bf16[512,128]{1,0:T(8,128)(2,1)}, u32[]{:S(2)}, u32[]{:S(2)}) collective-permute-start(bf16[512,128]{1,0:T(8,128)(2,1)} %get-tuple-element.243), channel_id=1, source_target_pairs={{0,2},{1,3},{2,4},{3,5},{4,6},{5,7},{6,0},{7,1},{8,10},{9,11},{10,... | collective-permute-start | bytes 393224 | tf_op jit(solution)/shard_map/ppermute | solution.py:16
  16.4 11.2 %collective-permute-start.5 = (bf16[512,128]{1,0:T(8,128)(2,1)}, bf16[512,128]{1,0:T(8,128)(2,1)}, u32[]{:S(2)}, u32[]{:S(2)}) collective-permute-start(bf16[512,128]{1,0:T(8,128)(2,1)} %collective-permute-done.4), channel_id=1, source_target_pairs={{0,2},{1,3},{2,4},{3,5},{4,6},{5,7},{6,0},{7,1},{8,10},{9,11},{10,... | collective-permute-start | bytes 393224 | tf_op jit(solution)/shard_map/ppermute | solution.py:16
  19.2 11.2 %collective-permute-start.2 = (bf16[512,128]{1,0:T(8,128)(2,1)}, bf16[512,128]{1,0:T(8,128)(2,1)}, u32[]{:S(2)}, u32[]{:S(2)}) collective-permute-start(bf16[512,128]{1,0:T(8,128)(2,1)} %collective-permute-done.1), channel_id=1, source_target_pairs={{0,2},{1,3},{2,4},{3,5},{4,6},{5,7},{6,0},{7,1},{8,10},{9,11},{10,... | collective-permute-start | bytes 393224 | tf_op jit(solution)/shard_map/ppermute | solution.py:16
  22.0 11.6 %collective-permute-start.15 = (bf16[512,128]{1,0:T(8,128)(2,1)}, bf16[512,128]{1,0:T(8,128)(2,1)}, u32[]{:S(2)}, u32[]{:S(2)}) collective-permute-start(bf16[512,128]{1,0:T(8,128)(2,1)} %collective-permute-done.14), channel_id=1, source_target_pairs={{0,2},{1,3},{2,4},{3,5},{4,6},{5,7},{6,0},{7,1},{8,10},{9,11},{10,... | collective-permute-start | bytes 393224 | tf_op jit(solution)/shard_map/ppermute | solution.py:16
  24.8 11.2 %collective-permute-start.12 = (bf16[512,128]{1,0:T(8,128)(2,1)}, bf16[512,128]{1,0:T(8,128)(2,1)}, u32[]{:S(2)}, u32[]{:S(2)}) collective-permute-start(bf16[512,128]{1,0:T(8,128)(2,1)} %collective-permute-done.11), channel_id=1, source_target_pairs={{0,2},{1,3},{2,4},{3,5},{4,6},{5,7},{6,0},{7,1},{8,10},{9,11},{10,... | collective-permute-start | bytes 393224 | tf_op jit(solution)/shard_map/ppermute | solution.py:16
  27.6 11.2 %collective-permute-start.6 = (bf16[512,128]{1,0:T(8,128)(2,1)}, bf16[512,128]{1,0:T(8,128)(2,1)}, u32[]{:S(2)}, u32[]{:S(2)}) collective-permute-start(bf16[512,128]{1,0:T(8,128)(2,1)} %collective-permute-done.5), channel_id=1, source_target_pairs={{0,2},{1,3},{2,4},{3,5},{4,6},{5,7},{6,0},{7,1},{8,10},{9,11},{10,... | collective-permute-start | bytes 393224 | tf_op jit(solution)/shard_map/ppermute | solution.py:16
  30.4 9.8 %collective-permute-start.3 = (bf16[512,128]{1,0:T(8,128)(2,1)}, bf16[512,128]{1,0:T(8,128)(2,1)}, u32[]{:S(2)}, u32[]{:S(2)}) collective-permute-start(bf16[512,128]{1,0:T(8,128)(2,1)} %collective-permute-done.2), channel_id=1, source_target_pairs={{0,2},{1,3},{2,4},{3,5},{4,6},{5,7},{6,0},{7,1},{8,10},{9,11},{10,... | collective-permute-start | bytes 393224 | tf_op jit(solution)/shard_map/ppermute | solution.py:16
  33.5 15.4 %collective-permute-start = (f32[520,512]{1,0:T(8,128)S(1)}, f32[520,512]{1,0:T(8,128)S(1)}, u32[]{:S(2)}, u32[]{:S(2)}) collective-permute-start(f32[520,512]{1,0:T(8,128)S(1)} %concatenate.35), channel_id=1, source_target_pairs={{0,8},{8,16},{16,24},{24,0},{1,9},{9,17},{17,25},{25,1},{2,10},{10... | collective-permute-start | bytes 3194888 | tf_op jit(solution)/shard_map/ppermute | solution.py:16
  36.0 11.6 %collective-permute-start.16 = (bf16[512,128]{1,0:T(8,128)(2,1)}, bf16[512,128]{1,0:T(8,128)(2,1)S(1)}, u32[]{:S(2)}, u32[]{:S(2)}) collective-permute-start(bf16[512,128]{1,0:T(8,128)(2,1)} %collective-permute-done.15), channel_id=1, source_target_pairs={{0,2},{1,3},{2,4},{3,5},{4,6},{5,7},{6,0},{7,1},{8,10},{9,11},{10,... | collective-permute-start | bytes 393224 | tf_op jit(solution)/shard_map/ppermute | solution.py:16
  38.8 8.7 %collective-permute-start.13 = (bf16[512,128]{1,0:T(8,128)(2,1)}, bf16[512,128]{1,0:T(8,128)(2,1)S(1)}, u32[]{:S(2)}, u32[]{:S(2)}) collective-permute-start(bf16[512,128]{1,0:T(8,128)(2,1)} %collective-permute-done.12), channel_id=1, source_target_pairs={{0,2},{1,3},{2,4},{3,5},{4,6},{5,7},{6,0},{7,1},{8,10},{9,11},{10,... | collective-permute-start | bytes 393224 | tf_op jit(solution)/shard_map/ppermute | solution.py:16
  46.2 11.2 %collective-permute-start.10 = (bf16[768,128]{1,0:T(8,128)(2,1)S(1)}, bf16[768,128]{1,0:T(8,128)(2,1)S(1)}, u32[]{:S(2)}, u32[]{:S(2)}) collective-permute-start(bf16[768,128]{1,0:T(8,128)(2,1)S(1)} %get-tuple-element.113), channel_id=1, source_target_pairs={{0,1},{1,0},{2,3},{3,2},{4,5},{5,4},{6,7},{7,6},{8,9},{9,8},{10,11... | collective-permute-start | bytes 589832 | tf_op jit(solution)/shard_map/ppermute | solution.py:70
  62.8 8.7 %collective-permute-start.23 = (bf16[768,128]{1,0:T(8,128)(2,1)S(1)}, bf16[768,128]{1,0:T(8,128)(2,1)S(1)}, u32[]{:S(2)}, u32[]{:S(2)}) collective-permute-start(bf16[768,128]{1,0:T(8,128)(2,1)S(1)} %get-tuple-element.125), channel_id=1, source_target_pairs={{0,1},{1,0},{2,3},{3,2},{4,5},{5,4},{6,7},{7,6},{8,9},{9,8},{10,11... | collective-permute-start | bytes 589832 | tf_op jit(solution)/shard_map/ppermute | solution.py:70
  67.7 8.9 %collective-permute-start.21 = (bf16[512,128]{1,0:T(8,128)(2,1)S(1)}, bf16[512,128]{1,0:T(8,128)(2,1)S(1)}, u32[]{:S(2)}, u32[]{:S(2)}) collective-permute-start(bf16[512,128]{1,0:T(8,128)(2,1)S(1)} %add_convert_fusion.14), channel_id=1, source_target_pairs={{0,2},{1,3},{2,4},{3,5},{4,6},{5,7},{6,0},{7,1},{8,10},{9,11},{10,... | collective-permute-start | bytes 393224 | tf_op jit(solution)/shard_map/ppermute | solution.py:16
  83.0 9.8 %collective-permute-start.29 = (bf16[512,128]{1,0:T(8,128)(2,1)S(1)}, bf16[512,128]{1,0:T(8,128)(2,1)S(1)}, u32[]{:S(2)}, u32[]{:S(2)}) collective-permute-start(bf16[512,128]{1,0:T(8,128)(2,1)S(1)} %add_convert_fusion.9), channel_id=1, source_target_pairs={{0,2},{1,3},{2,4},{3,5},{4,6},{5,7},{6,0},{7,1},{8,10},{9,11},{10,... | collective-permute-start | bytes 393224 | tf_op jit(solution)/shard_map/ppermute | solution.py:16
  84.7 10.9 %collective-permute-start.33 = (bf16[512,128]{1,0:T(8,128)(2,1)S(1)}, bf16[512,128]{1,0:T(8,128)(2,1)S(1)}, u32[]{:S(2)}, u32[]{:S(2)}) collective-permute-start(bf16[512,128]{1,0:T(8,128)(2,1)S(1)} %divide_convert_fusion.3), channel_id=1, source_target_pairs={{0,2},{1,3},{2,4},{3,5},{4,6},{5,7},{6,0},{7,1},{8,10},{9,11},{10,... | collective-permute-start | bytes 393224 | tf_op jit(solution)/shard_map/ppermute | solution.py:16
  101.0 8.9 %collective-permute-start.38 = (bf16[512,128]{1,0:T(8,128)(2,1)S(1)}, bf16[512,128]{1,0:T(8,128)(2,1)S(1)}, u32[]{:S(2)}, u32[]{:S(2)}) collective-permute-start(bf16[512,128]{1,0:T(8,128)(2,1)S(1)} %collective-permute-done.36), channel_id=1, source_target_pairs={{0,2},{1,3},{2,4},{3,5},{4,6},{5,7},{6,0},{7,1},{8,10},{9,11},{10,... | collective-permute-start | bytes 393224 | tf_op jit(solution)/shard_map/ppermute | solution.py:16
  103.8 8.9 %collective-permute-start.43 = (bf16[512,128]{1,0:T(8,128)(2,1)S(1)}, bf16[512,128]{1,0:T(8,128)(2,1)S(1)}, u32[]{:S(2)}, u32[]{:S(2)}) collective-permute-start(bf16[512,128]{1,0:T(8,128)(2,1)S(1)} %collective-permute-done.35), channel_id=1, source_target_pairs={{0,2},{1,3},{2,4},{3,5},{4,6},{5,7},{6,0},{7,1},{8,10},{9,11},{10,... | collective-permute-start | bytes 393224 | tf_op jit(solution)/shard_map/ppermute | solution.py:16
  104.4 11.2 %collective-permute-start.42 = (bf16[512,128]{1,0:T(8,128)(2,1)S(1)}, bf16[512,128]{1,0:T(8,128)(2,1)S(1)}, u32[]{:S(2)}, u32[]{:S(2)}) collective-permute-start(bf16[512,128]{1,0:T(8,128)(2,1)S(1)} %get-tuple-element.165), channel_id=1, source_target_pairs={{0,2},{1,3},{2,4},{3,5},{4,6},{5,7},{6,0},{7,1},{8,10},{9,11},{10,... | collective-permute-start | bytes 393224 | tf_op jit(solution)/shard_map/ppermute | solution.py:16
  104.9 47.6 %collective-permute-start.37 = (bf16[528,512]{1,0:T(8,128)(2,1)S(1)}, bf16[528,512]{1,0:T(8,128)(2,1)S(1)}, u32[]{:S(2)}, u32[]{:S(2)}) collective-permute-start(bf16[528,512]{1,0:T(8,128)(2,1)S(1)} %pad_maximum_fusion.2), channel_id=1, source_target_pairs={{0,16},{8,24},{16,0},{24,8},{1,17},{9,25},{17,1},{25,9},{2,18},{10... | collective-permute-start | bytes 1622024 | tf_op jit(solution)/shard_map/ppermute | solution.py:16
  107.1 11.2 %collective-permute-start.41 = (bf16[512,128]{1,0:T(8,128)(2,1)S(1)}, bf16[512,128]{1,0:T(8,128)(2,1)S(1)}, u32[]{:S(2)}, u32[]{:S(2)}) collective-permute-start(bf16[512,128]{1,0:T(8,128)(2,1)S(1)} %collective-permute-done.39), channel_id=1, source_target_pairs={{0,2},{1,3},{2,4},{3,5},{4,6},{5,7},{6,0},{7,1},{8,10},{9,11},{10,... | collective-permute-start | bytes 393224 | tf_op jit(solution)/shard_map/ppermute | solution.py:16
  109.9 11.2 %collective-permute-start.40 = (bf16[512,128]{1,0:T(8,128)(2,1)S(1)}, bf16[512,128]{1,0:T(8,128)(2,1)S(1)}, u32[]{:S(2)}, u32[]{:S(2)}) collective-permute-start(bf16[512,128]{1,0:T(8,128)(2,1)S(1)} %collective-permute-done.38), channel_id=1, source_target_pairs={{0,2},{1,3},{2,4},{3,5},{4,6},{5,7},{6,0},{7,1},{8,10},{9,11},{10,... | collective-permute-start | bytes 393224 | tf_op jit(solution)/shard_map/ppermute | solution.py:16
  114.4 9.1 %collective-permute-start.47 = (bf16[768,128]{1,0:T(8,128)(2,1)S(1)}, bf16[768,128]{1,0:T(8,128)(2,1)S(1)}, u32[]{:S(2)}, u32[]{:S(2)}) collective-permute-start(bf16[768,128]{1,0:T(8,128)(2,1)S(1)} %get-tuple-element.172), channel_id=1, source_target_pairs={{0,1},{1,0},{2,3},{3,2},{4,5},{5,4},{6,7},{7,6},{8,9},{9,8},{10,11... | collective-permute-start | bytes 589832 | tf_op jit(solution)/shard_map/ppermute | solution.py:70
  124.0 9.9 %collective-permute-start.50 = (bf16[512,128]{1,0:T(8,128)(2,1)S(1)}, bf16[512,128]{1,0:T(8,128)(2,1)S(1)}, u32[]{:S(2)}, u32[]{:S(2)}) collective-permute-start(bf16[512,128]{1,0:T(8,128)(2,1)S(1)} %collective-permute-done.46), channel_id=1, source_target_pairs={{0,2},{1,3},{2,4},{3,5},{4,6},{5,7},{6,0},{7,1},{8,10},{9,11},{10,... | collective-permute-start | bytes 393224 | tf_op jit(solution)/shard_map/ppermute | solution.py:16
  128.4 9.3 %collective-permute-start.49 = (bf16[768,128]{1,0:T(8,128)(2,1)S(1)}, bf16[768,128]{1,0:T(8,128)(2,1)S(1)}, u32[]{:S(2)}, u32[]{:S(2)}) collective-permute-start(bf16[768,128]{1,0:T(8,128)(2,1)S(1)} %get-tuple-element.184), channel_id=1, source_target_pairs={{0,1},{1,0},{2,3},{3,2},{4,5},{5,4},{6,7},{7,6},{8,9},{9,8},{10,11... | collective-permute-start | bytes 589832 | tf_op jit(solution)/shard_map/ppermute | solution.py:70
  139.3 10.0 %collective-permute-start.52 = (bf16[512,128]{1,0:T(8,128)(2,1)S(1)}, bf16[512,128]{1,0:T(8,128)(2,1)S(1)}, u32[]{:S(2)}, u32[]{:S(2)}) collective-permute-start(bf16[512,128]{1,0:T(8,128)(2,1)S(1)} %add_convert_fusion.6), channel_id=1, source_target_pairs={{0,2},{1,3},{2,4},{3,5},{4,6},{5,7},{6,0},{7,1},{8,10},{9,11},{10,... | collective-permute-start | bytes 393224 | tf_op jit(solution)/shard_map/ppermute | solution.py:16
  140.9 11.2 %collective-permute-start.56 = (bf16[512,128]{1,0:T(8,128)(2,1)S(1)}, bf16[512,128]{1,0:T(8,128)(2,1)S(1)}, u32[]{:S(2)}, u32[]{:S(2)}) collective-permute-start(bf16[512,128]{1,0:T(8,128)(2,1)S(1)} %add_convert_fusion.5), channel_id=1, source_target_pairs={{0,2},{1,3},{2,4},{3,5},{4,6},{5,7},{6,0},{7,1},{8,10},{9,11},{10,... | collective-permute-start | bytes 393224 | tf_op jit(solution)/shard_map/ppermute | solution.py:16
  142.9 12.0 %collective-permute-start.60 = (bf16[512,128]{1,0:T(8,128)(2,1)S(1)}, bf16[512,128]{1,0:T(8,128)(2,1)S(1)}, u32[]{:S(2)}, u32[]{:S(2)}) collective-permute-start(bf16[512,128]{1,0:T(8,128)(2,1)S(1)} %convolution_convert_fusion), channel_id=1, source_target_pairs={{0,2},{1,3},{2,4},{3,5},{4,6},{5,7},{6,0},{7,1},{8,10},{9,11},{10,... | collective-permute-start | bytes 393224 | tf_op jit(solution)/shard_map/ppermute | solution.py:16
  146.9 10.8 %collective-permute-start.59 = (bf16[512,128]{1,0:T(8,128)(2,1)S(1)}, bf16[512,128]{1,0:T(8,128)(2,1)S(1)}, u32[]{:S(2)}, u32[]{:S(2)}) collective-permute-start(bf16[512,128]{1,0:T(8,128)(2,1)S(1)} %add_convert_fusion.4), channel_id=1, source_target_pairs={{0,2},{1,3},{2,4},{3,5},{4,6},{5,7},{6,0},{7,1},{8,10},{9,11},{10,... | collective-permute-start | bytes 393224 | tf_op jit(solution)/shard_map/ppermute | solution.py:16
  149.7 10.8 %collective-permute-start.58 = (bf16[512,128]{1,0:T(8,128)(2,1)S(1)}, bf16[512,128]{1,0:T(8,128)(2,1)S(1)}, u32[]{:S(2)}, u32[]{:S(2)}) collective-permute-start(bf16[512,128]{1,0:T(8,128)(2,1)S(1)} %add_convert_fusion.3), channel_id=1, source_target_pairs={{0,2},{1,3},{2,4},{3,5},{4,6},{5,7},{6,0},{7,1},{8,10},{9,11},{10,... | collective-permute-start | bytes 393224 | tf_op jit(solution)/shard_map/ppermute | solution.py:16
  (51 other events, 379.8 us)

commit v7 on v6

--- a/solution.py
+++ b/solution.py
@@ -7,7 +7,7 @@
 CHUNKS = 4
 OCCUPANCY = {"gather": 2.75, "scatter": 2.75, "pair": 3.95, "group": 2.0}
 PREPARE = {"gather": 1.4, "scatter": 1.8, "pair": 2.6, "group": 2.2}
-LATENCY = 3.2
+LATENCY = 4.2
 
 
 def from_behind(value, axis, steps):

time: 177 us -> 181 us (1.023)
  starting transfers between devices: 42.2 us -> 45 us
    ppermute x58, starting transfers between devices: 30.3 us -> 33.9 us  [from_behind(): return lax.ppermute(value, axis, pairs)]
    convert_element_type x7 -> x8, other arithmetic: 3.28 us -> 4.32 us  [stream(): grad_out = (key_scale * (residual + received.astype(wide))).astype(narrow)]
  transfers between devices with their start and end apart: 67 -> 67, of which waited for: 48 -> 43; matrix products, arithmetic and copies ran while one was open for 25% -> 25% of each run, Pallas kernels for 0% -> 0%
where the time goes in v7:
time: 181 us; the launch traced here: 180 us
  waiting for transfers between devices  83 us (46%)
  starting transfers between devices  45 us (25%)
  matrix products  26.2 us (14%)
  other arithmetic  14.3 us (8%)
  local copies, waits for them, and re-layouts  9.56 us (5%)
  between operations  2.19 us (1%)
    ppermute x58, waiting for transfers between devices, from_behind(): return lax.ppermute(value, axis, pairs)  79.8 us
    ppermute x58, starting transfers between devices, from_behind(): return lax.ppermute(value, axis, pairs)  33.9 us
    dot_general x32, matrix products, partial(): lax.dot_general(column_block(back), grad_out, contract, preferred_element...  13.2 us
    dot_general x16, matrix products, stream(): jnp.dot(column_block(back), piece, preferred_element_type=wide)  9.53 us
    ppermute x8, starting transfers between devices, send(): return lax.ppermute(value, 'fsdp', [(i, i ^ 1) for i in range(count)])  8.15 us
    convert_element_type x8, other arithmetic, stream(): grad_out = (key_scale * (residual + received.astype(wide))).astype(narrow)  4.32 us
  transfers between devices with their start and end apart: 67, of which 43 were waited for; matrix products, arithmetic and copies ran while one was open for 25% of the time, Pallas kernels for 0%

profile of v7, /device:TPU:0, one launch (start us, length us, event | category | flops | bytes accessed | tf_op | source)
XLA Modules:
  0.0 180.3 jit_solution(16280413771527602869)
XLA Ops:
  3.6 2.9 %collective-permute-start.7 = (bf16[384,2048]{1,0:T(8,128)(2,1)}, bf16[384,2048]{1,0:T(8,128)(2,1)}, u32[]{:S(2)}, u32[]{:S(2)}) collective-permute-start(bf16[384,2048]{1,0:T(8,128)(2,1)} %pad_maximum_fusion), channel_id=1, source_target_pairs={{0,1},{1,0},{2,3},{3,2},{4,5},{5,4},{6,7},{7,6},{8,9},{9,8},{10,11... | collective-permute-start | bytes 4718600 | tf_op jit(solution)/shard_map/ppermute | solution.py:89
  17.1 2.1 %collective-permute-done.1 = bf16[512,128]{1,0:T(8,128)(2,1)} collective-permute-done((bf16[512,128]{1,0:T(8,128)(2,1)S(1)}, bf16[512,128]{1,0:T(8,128)(2,1)}, u32[]{:S(2)}, u32[]{:S(2)}) %collective-permute-start.1) | collective-permute-done | bytes 131104 | tf_op jit(solution)/shard_map/ppermute | solution.py:16
  19.8 2.2 %collective-permute-done.12 = bf16[512,128]{1,0:T(8,128)(2,1)} collective-permute-done((bf16[512,128]{1,0:T(8,128)(2,1)}, bf16[512,128]{1,0:T(8,128)(2,1)}, u32[]{:S(2)}, u32[]{:S(2)}) %collective-permute-start.12) | collective-permute-done | bytes 131104 | tf_op jit(solution)/shard_map/ppermute | solution.py:16
  22.0 2.8 %collective-permute-done.9 = bf16[512,128]{1,0:T(8,128)(2,1)} collective-permute-done((bf16[512,128]{1,0:T(8,128)(2,1)}, bf16[512,128]{1,0:T(8,128)(2,1)}, u32[]{:S(2)}, u32[]{:S(2)}) %collective-permute-start.9) | collective-permute-done | bytes 131104 | tf_op jit(solution)/shard_map/ppermute | solution.py:16
  24.8 2.8 %collective-permute-done.5 = bf16[512,128]{1,0:T(8,128)(2,1)} collective-permute-done((bf16[512,128]{1,0:T(8,128)(2,1)}, bf16[512,128]{1,0:T(8,128)(2,1)}, u32[]{:S(2)}, u32[]{:S(2)}) %collective-permute-start.5) | collective-permute-done | bytes 131104 | tf_op jit(solution)/shard_map/ppermute | solution.py:16
  27.6 2.8 %collective-permute-done.2 = bf16[512,128]{1,0:T(8,128)(2,1)} collective-permute-done((bf16[512,128]{1,0:T(8,128)(2,1)}, bf16[512,128]{1,0:T(8,128)(2,1)}, u32[]{:S(2)}, u32[]{:S(2)}) %collective-permute-start.2) | collective-permute-done | bytes 131104 | tf_op jit(solution)/shard_map/ppermute | solution.py:16
  33.6 2.4 %collective-permute-done.10 = bf16[512,128]{1,0:T(8,128)(2,1)} collective-permute-done((bf16[512,128]{1,0:T(8,128)(2,1)}, bf16[512,128]{1,0:T(8,128)(2,1)}, u32[]{:S(2)}, u32[]{:S(2)}) %collective-permute-start.10) | collective-permute-done | bytes 131104 | tf_op jit(solution)/shard_map/ppermute | solution.py:16
  36.0 2.8 %collective-permute-done.6 = bf16[512,128]{1,0:T(8,128)(2,1)} collective-permute-done((bf16[512,128]{1,0:T(8,128)(2,1)}, bf16[512,128]{1,0:T(8,128)(2,1)}, u32[]{:S(2)}, u32[]{:S(2)}) %collective-permute-start.6) | collective-permute-done | bytes 131104 | tf_op jit(solution)/shard_map/ppermute | solution.py:16
  42.3 2.0 %convolution_dynamic-update-slice_fusion = f32[768,256]{1,0:T(8,128)S(1)} fusion(f32[768,256]{1,0:T(8,128)S(1)} %convolution_dynamic-update-slice_fusion.1, s32[]{:T(128)S(6)} %select_n.49, bf16[384,2048]{1,0:T(8,128)(2,1)} %collective-permute-done.7, bf16[2048,256]{1,0:T(8,128)(2,1)S(1)} %maximum_maximum_fusion), kind=kOutput, calls=%fused_computation.2 | convolution fusion | flops 402653184 | bytes 3014660 | tf_op jit(solution)/shard_map/dot_general | solution.py:156
  74.5 1.8 collective-permute-done.25
  76.8 2.3 %collective-permute-done.24 = bf16[512,128]{1,0:T(8,128)(2,1)S(1)} collective-permute-done((bf16[512,128]{1,0:T(8,128)(2,1)S(1)}, bf16[512,128]{1,0:T(8,128)(2,1)S(1)}, u32[]{:S(2)}, u32[]{:S(2)}) %collective-permute-start.24) | collective-permute-done | bytes 131104 | tf_op jit(solution)/shard_map/ppermute | solution.py:16
  79.6 2.3 %collective-permute-done.23 = bf16[512,128]{1,0:T(8,128)(2,1)S(1)} collective-permute-done((bf16[512,128]{1,0:T(8,128)(2,1)S(1)}, bf16[512,128]{1,0:T(8,128)(2,1)S(1)}, u32[]{:S(2)}, u32[]{:S(2)}) %collective-permute-start.23) | collective-permute-done | bytes 131104 | tf_op jit(solution)/shard_map/ppermute | solution.py:16
  82.6 2.1 %collective-permute-done.22 = bf16[512,128]{1,0:T(8,128)(2,1)S(1)} collective-permute-done((bf16[512,128]{1,0:T(8,128)(2,1)S(1)}, bf16[512,128]{1,0:T(8,128)(2,1)S(1)}, u32[]{:S(2)}, u32[]{:S(2)}) %collective-permute-start.22) | collective-permute-done | bytes 131104 | tf_op jit(solution)/shard_map/ppermute | solution.py:16
  85.2 2.3 %collective-permute-done.29 = bf16[512,128]{1,0:T(8,128)(2,1)S(1)} collective-permute-done((bf16[512,128]{1,0:T(8,128)(2,1)S(1)}, bf16[512,128]{1,0:T(8,128)(2,1)S(1)}, u32[]{:S(2)}, u32[]{:S(2)}) %collective-permute-start.29) | collective-permute-done | bytes 131104 | tf_op jit(solution)/shard_map/ppermute | solution.py:16
  93.6 3.6 %collective-permute-done.32 = bf16[512,128]{1,0:T(8,128)(2,1)S(1)} collective-permute-done((bf16[512,128]{1,0:T(8,128)(2,1)S(1)}, bf16[512,128]{1,0:T(8,128)(2,1)S(1)}, u32[]{:S(2)}, u32[]{:S(2)}) %collective-permute-start.32) | collective-permute-done | bytes 131104 | tf_op jit(solution)/shard_map/ppermute | solution.py:16
  100.1 2.6 %collective-permute-done.34 = bf16[512,128]{1,0:T(8,128)(2,1)S(1)} collective-permute-done((bf16[512,128]{1,0:T(8,128)(2,1)S(1)}, bf16[512,128]{1,0:T(8,128)(2,1)S(1)}, u32[]{:S(2)}, u32[]{:S(2)}) %collective-permute-start.34) | collective-permute-done | bytes 131104 | tf_op jit(solution)/shard_map/ppermute | solution.py:16
  111.8 2.8 %collective-permute-done.41 = bf16[512,128]{1,0:T(8,128)(2,1)S(1)} collective-permute-done((bf16[512,128]{1,0:T(8,128)(2,1)S(1)}, bf16[512,128]{1,0:T(8,128)(2,1)S(1)}, u32[]{:S(2)}, u32[]{:S(2)}) %collective-permute-start.41) | collective-permute-done | bytes 131104 | tf_op jit(solution)/shard_map/ppermute | solution.py:16
  114.6 2.8 %collective-permute-done.44 = bf16[512,128]{1,0:T(8,128)(2,1)S(1)} collective-permute-done((bf16[512,128]{1,0:T(8,128)(2,1)S(1)}, bf16[512,128]{1,0:T(8,128)(2,1)S(1)}, u32[]{:S(2)}, u32[]{:S(2)}) %collective-permute-start.44) | collective-permute-done | bytes 131104 | tf_op jit(solution)/shard_map/ppermute | solution.py:16
  117.8 2.4 %collective-permute-done.43 = bf16[512,128]{1,0:T(8,128)(2,1)S(1)} collective-permute-done((bf16[512,128]{1,0:T(8,128)(2,1)S(1)}, bf16[512,128]{1,0:T(8,128)(2,1)S(1)}, u32[]{:S(2)}, u32[]{:S(2)}) %collective-permute-start.43) | collective-permute-done | bytes 131104 | tf_op jit(solution)/shard_map/ppermute | solution.py:16
  122.8 3.0 %collective-permute-done.42 = bf16[512,128]{1,0:T(8,128)(2,1)S(1)} collective-permute-done((bf16[512,128]{1,0:T(8,128)(2,1)S(1)}, bf16[512,128]{1,0:T(8,128)(2,1)S(1)}, u32[]{:S(2)}, u32[]{:S(2)}) %collective-permute-start.42) | collective-permute-done | bytes 131104 | tf_op jit(solution)/shard_map/ppermute | solution.py:16
  131.9 2.9 %collective-permute-done.45 = bf16[768,128]{1,0:T(8,128)(2,1)S(1)} collective-permute-done((bf16[768,128]{1,0:T(8,128)(2,1)S(1)}, bf16[768,128]{1,0:T(8,128)(2,1)S(1)}, u32[]{:S(2)}, u32[]{:S(2)}) %collective-permute-start.45) | collective-permute-done | bytes 196640 | tf_op jit(solution)/shard_map/ppermute | solution.py:70
  140.9 3.5 %collective-permute-start.53 = (bf16[512,128]{1,0:T(8,128)(2,1)S(1)}, bf16[512,128]{1,0:T(8,128)(2,1)S(1)}, u32[]{:S(2)}, u32[]{:S(2)}) collective-permute-start(bf16[512,128]{1,0:T(8,128)(2,1)S(1)} %convolution_convert_fusion.1), channel_id=1, source_target_pairs={{0,2},{1,3},{2,4},{3,5},{4,6},{5,7},{6,0},{7,1},{8,10},{9,11},{10,... | collective-permute-start | bytes 393224 | tf_op jit(solution)/shard_map/ppermute | solution.py:16
  146.2 2.1 %collective-permute-start.60 = (bf16[512,128]{1,0:T(8,128)(2,1)S(1)}, bf16[512,128]{1,0:T(8,128)(2,1)S(1)}, u32[]{:S(2)}, u32[]{:S(2)}) collective-permute-start(bf16[512,128]{1,0:T(8,128)(2,1)S(1)} %convolution_convert_fusion), channel_id=1, source_target_pairs={{0,2},{1,3},{2,4},{3,5},{4,6},{5,7},{6,0},{7,1},{8,10},{9,11},{10,... | collective-permute-start | bytes 393224 | tf_op jit(solution)/shard_map/ppermute | solution.py:16
  149.5 2.1 %collective-permute-start.59 = (bf16[512,128]{1,0:T(8,128)(2,1)S(1)}, bf16[512,128]{1,0:T(8,128)(2,1)S(1)}, u32[]{:S(2)}, u32[]{:S(2)}) collective-permute-start(bf16[512,128]{1,0:T(8,128)(2,1)S(1)} %add_convert_fusion.4), channel_id=1, source_target_pairs={{0,2},{1,3},{2,4},{3,5},{4,6},{5,7},{6,0},{7,1},{8,10},{9,11},{10,... | collective-permute-start | bytes 393224 | tf_op jit(solution)/shard_map/ppermute | solution.py:16
  151.6 1.8 collective-permute-done.52
  154.3 1.8 %collective-permute-done.56 = bf16[512,128]{1,0:T(8,128)(2,1)S(1)} collective-permute-done((bf16[512,128]{1,0:T(8,128)(2,1)S(1)}, bf16[512,128]{1,0:T(8,128)(2,1)S(1)}, u32[]{:S(2)}, u32[]{:S(2)}) %collective-permute-start.56) | collective-permute-done | bytes 131104 | tf_op jit(solution)/shard_map/ppermute | solution.py:16
  157.0 2.0 %collective-permute-done.60 = bf16[512,128]{1,0:T(8,128)(2,1)S(1)} collective-permute-done((bf16[512,128]{1,0:T(8,128)(2,1)S(1)}, bf16[512,128]{1,0:T(8,128)(2,1)S(1)}, u32[]{:S(2)}, u32[]{:S(2)}) %collective-permute-start.60) | collective-permute-done | bytes 131104 | tf_op jit(solution)/shard_map/ppermute | solution.py:16
  159.7 2.1 %collective-permute-done.59 = bf16[512,128]{1,0:T(8,128)(2,1)S(1)} collective-permute-done((bf16[512,128]{1,0:T(8,128)(2,1)S(1)}, bf16[512,128]{1,0:T(8,128)(2,1)S(1)}, u32[]{:S(2)}, u32[]{:S(2)}) %collective-permute-start.59) | collective-permute-done | bytes 131104 | tf_op jit(solution)/shard_map/ppermute | solution.py:16
  162.4 1.7 collective-permute-done.58
  166.7 2.6 %collective-permute-done.62 = bf16[512,128]{1,0:T(8,128)(2,1)S(1)} collective-permute-done((bf16[512,128]{1,0:T(8,128)(2,1)S(1)}, bf16[512,128]{1,0:T(8,128)(2,1)S(1)}, u32[]{:S(2)}, u32[]{:S(2)}) %collective-permute-start.62) | collective-permute-done | bytes 131104 | tf_op jit(solution)/shard_map/ppermute | solution.py:16
  170.7 2.8 %collective-permute-done.65 = bf16[512,128]{1,0:T(8,128)(2,1)S(1)} collective-permute-done((bf16[512,128]{1,0:T(8,128)(2,1)S(1)}, bf16[512,128]{1,0:T(8,128)(2,1)S(1)}, u32[]{:S(2)}, u32[]{:S(2)}) %collective-permute-start.65) | collective-permute-done | bytes 131104 | tf_op jit(solution)/shard_map/ppermute | solution.py:16
  175.0 3.9 %collective-permute-done.66 = bf16[512,128]{1,0:T(8,128)(2,1)S(1)} collective-permute-done((bf16[512,128]{1,0:T(8,128)(2,1)S(1)}, bf16[512,128]{1,0:T(8,128)(2,1)S(1)}, u32[]{:S(2)}, u32[]{:S(2)}) %collective-permute-start.66) | collective-permute-done | bytes 131104 | tf_op jit(solution)/shard_map/ppermute | solution.py:16
  (232 shorter events, 97.7 us)
Async XLA Ops:
  3.6 38.7 %collective-permute-start.7 = (bf16[384,2048]{1,0:T(8,128)(2,1)}, bf16[384,2048]{1,0:T(8,128)(2,1)}, u32[]{:S(2)}, u32[]{:S(2)}) collective-permute-start(bf16[384,2048]{1,0:T(8,128)(2,1)} %pad_maximum_fusion), channel_id=1, source_target_pairs={{0,1},{1,0},{2,3},{3,2},{4,5},{5,4},{6,7},{7,6},{8,9},{9,8},{10,11... | collective-permute-start | bytes 4718600 | tf_op jit(solution)/shard_map/ppermute | solution.py:89
  9.6 9.6 %collective-permute-start.1 = (bf16[512,128]{1,0:T(8,128)(2,1)S(1)}, bf16[512,128]{1,0:T(8,128)(2,1)}, u32[]{:S(2)}, u32[]{:S(2)}) collective-permute-start(bf16[512,128]{1,0:T(8,128)(2,1)S(1)} %get-tuple-element.245), channel_id=1, source_target_pairs={{0,2},{1,3},{2,4},{3,5},{4,6},{5,7},{6,0},{7,1},{8,10},{9,11},{10,... | collective-permute-start | bytes 393224 | tf_op jit(solution)/shard_map/ppermute | solution.py:16
  11.2 10.8 %collective-permute-start.12 = (bf16[512,128]{1,0:T(8,128)(2,1)}, bf16[512,128]{1,0:T(8,128)(2,1)}, u32[]{:S(2)}, u32[]{:S(2)}) collective-permute-start(bf16[512,128]{1,0:T(8,128)(2,1)} %get-tuple-element.246), channel_id=1, source_target_pairs={{0,2},{1,3},{2,4},{3,5},{4,6},{5,7},{6,0},{7,1},{8,10},{9,11},{10,... | collective-permute-start | bytes 393224 | tf_op jit(solution)/shard_map/ppermute | solution.py:16
  12.8 12.0 %collective-permute-start.9 = (bf16[512,128]{1,0:T(8,128)(2,1)}, bf16[512,128]{1,0:T(8,128)(2,1)}, u32[]{:S(2)}, u32[]{:S(2)}) collective-permute-start(bf16[512,128]{1,0:T(8,128)(2,1)} %get-tuple-element.243), channel_id=1, source_target_pairs={{0,2},{1,3},{2,4},{3,5},{4,6},{5,7},{6,0},{7,1},{8,10},{9,11},{10,... | collective-permute-start | bytes 393224 | tf_op jit(solution)/shard_map/ppermute | solution.py:16
  16.4 11.2 %collective-permute-start.5 = (bf16[512,128]{1,0:T(8,128)(2,1)}, bf16[512,128]{1,0:T(8,128)(2,1)}, u32[]{:S(2)}, u32[]{:S(2)}) collective-permute-start(bf16[512,128]{1,0:T(8,128)(2,1)} %collective-permute-done.4), channel_id=1, source_target_pairs={{0,2},{1,3},{2,4},{3,5},{4,6},{5,7},{6,0},{7,1},{8,10},{9,11},{10,... | collective-permute-start | bytes 393224 | tf_op jit(solution)/shard_map/ppermute | solution.py:16
  19.2 11.2 %collective-permute-start.2 = (bf16[512,128]{1,0:T(8,128)(2,1)}, bf16[512,128]{1,0:T(8,128)(2,1)}, u32[]{:S(2)}, u32[]{:S(2)}) collective-permute-start(bf16[512,128]{1,0:T(8,128)(2,1)} %collective-permute-done.1), channel_id=1, source_target_pairs={{0,2},{1,3},{2,4},{3,5},{4,6},{5,7},{6,0},{7,1},{8,10},{9,11},{10,... | collective-permute-start | bytes 393224 | tf_op jit(solution)/shard_map/ppermute | solution.py:16
  22.0 11.6 %collective-permute-start.13 = (bf16[512,128]{1,0:T(8,128)(2,1)}, bf16[512,128]{1,0:T(8,128)(2,1)}, u32[]{:S(2)}, u32[]{:S(2)}) collective-permute-start(bf16[512,128]{1,0:T(8,128)(2,1)} %collective-permute-done.12), channel_id=1, source_target_pairs={{0,2},{1,3},{2,4},{3,5},{4,6},{5,7},{6,0},{7,1},{8,10},{9,11},{10,... | collective-permute-start | bytes 393224 | tf_op jit(solution)/shard_map/ppermute | solution.py:16
  24.8 11.2 %collective-permute-start.10 = (bf16[512,128]{1,0:T(8,128)(2,1)}, bf16[512,128]{1,0:T(8,128)(2,1)}, u32[]{:S(2)}, u32[]{:S(2)}) collective-permute-start(bf16[512,128]{1,0:T(8,128)(2,1)} %collective-permute-done.9), channel_id=1, source_target_pairs={{0,2},{1,3},{2,4},{3,5},{4,6},{5,7},{6,0},{7,1},{8,10},{9,11},{10,... | collective-permute-start | bytes 393224 | tf_op jit(solution)/shard_map/ppermute | solution.py:16
  27.6 11.2 %collective-permute-start.6 = (bf16[512,128]{1,0:T(8,128)(2,1)}, bf16[512,128]{1,0:T(8,128)(2,1)}, u32[]{:S(2)}, u32[]{:S(2)}) collective-permute-start(bf16[512,128]{1,0:T(8,128)(2,1)} %collective-permute-done.5), channel_id=1, source_target_pairs={{0,2},{1,3},{2,4},{3,5},{4,6},{5,7},{6,0},{7,1},{8,10},{9,11},{10,... | collective-permute-start | bytes 393224 | tf_op jit(solution)/shard_map/ppermute | solution.py:16
  30.4 9.8 %collective-permute-start.3 = (bf16[512,128]{1,0:T(8,128)(2,1)}, bf16[512,128]{1,0:T(8,128)(2,1)}, u32[]{:S(2)}, u32[]{:S(2)}) collective-permute-start(bf16[512,128]{1,0:T(8,128)(2,1)} %collective-permute-done.2), channel_id=1, source_target_pairs={{0,2},{1,3},{2,4},{3,5},{4,6},{5,7},{6,0},{7,1},{8,10},{9,11},{10,... | collective-permute-start | bytes 393224 | tf_op jit(solution)/shard_map/ppermute | solution.py:16
  33.5 19.1 %collective-permute-start = (f32[520,512]{1,0:T(8,128)S(1)}, f32[520,512]{1,0:T(8,128)S(1)}, u32[]{:S(2)}, u32[]{:S(2)}) collective-permute-start(f32[520,512]{1,0:T(8,128)S(1)} %concatenate.35), channel_id=1, source_target_pairs={{0,8},{8,16},{16,24},{24,0},{1,9},{9,17},{17,25},{25,1},{2,10},{10... | collective-permute-start | bytes 3194888 | tf_op jit(solution)/shard_map/ppermute | solution.py:16
  36.0 11.6 %collective-permute-start.14 = (bf16[512,128]{1,0:T(8,128)(2,1)}, bf16[512,128]{1,0:T(8,128)(2,1)S(1)}, u32[]{:S(2)}, u32[]{:S(2)}) collective-permute-start(bf16[512,128]{1,0:T(8,128)(2,1)} %collective-permute-done.13), channel_id=1, source_target_pairs={{0,2},{1,3},{2,4},{3,5},{4,6},{5,7},{6,0},{7,1},{8,10},{9,11},{10,... | collective-permute-start | bytes 393224 | tf_op jit(solution)/shard_map/ppermute | solution.py:16
  46.2 10.7 %collective-permute-start.17 = (bf16[768,128]{1,0:T(8,128)(2,1)S(1)}, bf16[768,128]{1,0:T(8,128)(2,1)S(1)}, u32[]{:S(2)}, u32[]{:S(2)}) collective-permute-start(bf16[768,128]{1,0:T(8,128)(2,1)S(1)} %get-tuple-element.113), channel_id=1, source_target_pairs={{0,1},{1,0},{2,3},{3,2},{4,5},{5,4},{6,7},{7,6},{8,9},{9,8},{10,11... | collective-permute-start | bytes 589832 | tf_op jit(solution)/shard_map/ppermute | solution.py:70
  68.6 10.5 %collective-permute-start.24 = (bf16[512,128]{1,0:T(8,128)(2,1)S(1)}, bf16[512,128]{1,0:T(8,128)(2,1)S(1)}, u32[]{:S(2)}, u32[]{:S(2)}) collective-permute-start(bf16[512,128]{1,0:T(8,128)(2,1)S(1)} %convolution_convert_fusion.4), channel_id=1, source_target_pairs={{0,2},{1,3},{2,4},{3,5},{4,6},{5,7},{6,0},{7,1},{8,10},{9,11},{10,... | collective-permute-start | bytes 393224 | tf_op jit(solution)/shard_map/ppermute | solution.py:16
  71.1 10.8 %collective-permute-start.23 = (bf16[512,128]{1,0:T(8,128)(2,1)S(1)}, bf16[512,128]{1,0:T(8,128)(2,1)S(1)}, u32[]{:S(2)}, u32[]{:S(2)}) collective-permute-start(bf16[512,128]{1,0:T(8,128)(2,1)S(1)} %add_convert_fusion.13), channel_id=1, source_target_pairs={{0,2},{1,3},{2,4},{3,5},{4,6},{5,7},{6,0},{7,1},{8,10},{9,11},{10,... | collective-permute-start | bytes 393224 | tf_op jit(solution)/shard_map/ppermute | solution.py:16
  73.9 10.8 %collective-permute-start.22 = (bf16[512,128]{1,0:T(8,128)(2,1)S(1)}, bf16[512,128]{1,0:T(8,128)(2,1)S(1)}, u32[]{:S(2)}, u32[]{:S(2)}) collective-permute-start(bf16[512,128]{1,0:T(8,128)(2,1)S(1)} %add_convert_fusion.12), channel_id=1, source_target_pairs={{0,2},{1,3},{2,4},{3,5},{4,6},{5,7},{6,0},{7,1},{8,10},{9,11},{10,... | collective-permute-start | bytes 393224 | tf_op jit(solution)/shard_map/ppermute | solution.py:16
  76.7 10.8 %collective-permute-start.29 = (bf16[512,128]{1,0:T(8,128)(2,1)S(1)}, bf16[512,128]{1,0:T(8,128)(2,1)S(1)}, u32[]{:S(2)}, u32[]{:S(2)}) collective-permute-start(bf16[512,128]{1,0:T(8,128)(2,1)S(1)} %add_convert_fusion.11), channel_id=1, source_target_pairs={{0,2},{1,3},{2,4},{3,5},{4,6},{5,7},{6,0},{7,1},{8,10},{9,11},{10,... | collective-permute-start | bytes 393224 | tf_op jit(solution)/shard_map/ppermute | solution.py:16
  79.5 9.5 %collective-permute-start.28 = (bf16[512,128]{1,0:T(8,128)(2,1)S(1)}, bf16[512,128]{1,0:T(8,128)(2,1)S(1)}, u32[]{:S(2)}, u32[]{:S(2)}) collective-permute-start(bf16[512,128]{1,0:T(8,128)(2,1)S(1)} %add_convert_fusion.10), channel_id=1, source_target_pairs={{0,2},{1,3},{2,4},{3,5},{4,6},{5,7},{6,0},{7,1},{8,10},{9,11},{10,... | collective-permute-start | bytes 393224 | tf_op jit(solution)/shard_map/ppermute | solution.py:16
  92.6 10.2 %collective-permute-start.34 = (bf16[512,128]{1,0:T(8,128)(2,1)S(1)}, bf16[512,128]{1,0:T(8,128)(2,1)S(1)}, u32[]{:S(2)}, u32[]{:S(2)}) collective-permute-start(bf16[512,128]{1,0:T(8,128)(2,1)S(1)} %divide_convert_fusion.2), channel_id=1, source_target_pairs={{0,2},{1,3},{2,4},{3,5},{4,6},{5,7},{6,0},{7,1},{8,10},{9,11},{10,... | collective-permute-start | bytes 393224 | tf_op jit(solution)/shard_map/ppermute | solution.py:16
  103.6 10.9 %collective-permute-start.41 = (bf16[512,128]{1,0:T(8,128)(2,1)S(1)}, bf16[512,128]{1,0:T(8,128)(2,1)S(1)}, u32[]{:S(2)}, u32[]{:S(2)}) collective-permute-start(bf16[512,128]{1,0:T(8,128)(2,1)S(1)} %get-tuple-element.163), channel_id=1, source_target_pairs={{0,2},{1,3},{2,4},{3,5},{4,6},{5,7},{6,0},{7,1},{8,10},{9,11},{10,... | collective-permute-start | bytes 393224 | tf_op jit(solution)/shard_map/ppermute | solution.py:16
  104.4 49.8 %collective-permute-start.36 = (bf16[528,512]{1,0:T(8,128)(2,1)S(1)}, bf16[528,512]{1,0:T(8,128)(2,1)S(1)}, u32[]{:S(2)}, u32[]{:S(2)}) collective-permute-start(bf16[528,512]{1,0:T(8,128)(2,1)S(1)} %pad_maximum_fusion.2), channel_id=1, source_target_pairs={{0,16},{8,24},{16,0},{24,8},{1,17},{9,25},{17,1},{25,9},{2,18},{10... | collective-permute-start | bytes 1622024 | tf_op jit(solution)/shard_map/ppermute | solution.py:16
  106.1 11.2 %collective-permute-start.44 = (bf16[512,128]{1,0:T(8,128)(2,1)S(1)}, bf16[512,128]{1,0:T(8,128)(2,1)S(1)}, u32[]{:S(2)}, u32[]{:S(2)}) collective-permute-start(bf16[512,128]{1,0:T(8,128)(2,1)S(1)} %collective-permute-done.39), channel_id=1, source_target_pairs={{0,2},{1,3},{2,4},{3,5},{4,6},{5,7},{6,0},{7,1},{8,10},{9,11},{10,... | collective-permute-start | bytes 393224 | tf_op jit(solution)/shard_map/ppermute | solution.py:16
  109.0 11.2 %collective-permute-start.43 = (bf16[512,128]{1,0:T(8,128)(2,1)S(1)}, bf16[512,128]{1,0:T(8,128)(2,1)S(1)}, u32[]{:S(2)}, u32[]{:S(2)}) collective-permute-start(bf16[512,128]{1,0:T(8,128)(2,1)S(1)} %collective-permute-done.38), channel_id=1, source_target_pairs={{0,2},{1,3},{2,4},{3,5},{4,6},{5,7},{6,0},{7,1},{8,10},{9,11},{10,... | collective-permute-start | bytes 393224 | tf_op jit(solution)/shard_map/ppermute | solution.py:16
  111.8 14.1 %collective-permute-start.40 = (bf16[512,128]{1,0:T(8,128)(2,1)S(1)}, bf16[512,128]{1,0:T(8,128)(2,1)S(1)}, u32[]{:S(2)}, u32[]{:S(2)}) collective-permute-start(bf16[512,128]{1,0:T(8,128)(2,1)S(1)} %collective-permute-done.37), channel_id=1, source_target_pairs={{0,2},{1,3},{2,4},{3,5},{4,6},{5,7},{6,0},{7,1},{8,10},{9,11},{10,... | collective-permute-start | bytes 393224 | tf_op jit(solution)/shard_map/ppermute | solution.py:16
  114.6 11.2 %collective-permute-start.42 = (bf16[512,128]{1,0:T(8,128)(2,1)S(1)}, bf16[512,128]{1,0:T(8,128)(2,1)S(1)}, u32[]{:S(2)}, u32[]{:S(2)}) collective-permute-start(bf16[512,128]{1,0:T(8,128)(2,1)S(1)} %collective-permute-done.41), channel_id=1, source_target_pairs={{0,2},{1,3},{2,4},{3,5},{4,6},{5,7},{6,0},{7,1},{8,10},{9,11},{10,... | collective-permute-start | bytes 393224 | tf_op jit(solution)/shard_map/ppermute | solution.py:16
  117.4 11.6 %collective-permute-start.46 = (bf16[512,128]{1,0:T(8,128)(2,1)S(1)}, bf16[512,128]{1,0:T(8,128)(2,1)S(1)}, u32[]{:S(2)}, u32[]{:S(2)}) collective-permute-start(bf16[512,128]{1,0:T(8,128)(2,1)S(1)} %collective-permute-done.44), channel_id=1, source_target_pairs={{0,2},{1,3},{2,4},{3,5},{4,6},{5,7},{6,0},{7,1},{8,10},{9,11},{10,... | collective-permute-start | bytes 393224 | tf_op jit(solution)/shard_map/ppermute | solution.py:16
  125.8 12.0 %collective-permute-start.50 = (bf16[512,128]{1,0:T(8,128)(2,1)S(1)}, bf16[512,128]{1,0:T(8,128)(2,1)S(1)}, u32[]{:S(2)}, u32[]{:S(2)}) collective-permute-start(bf16[512,128]{1,0:T(8,128)(2,1)S(1)} %collective-permute-done.42), channel_id=1, source_target_pairs={{0,2},{1,3},{2,4},{3,5},{4,6},{5,7},{6,0},{7,1},{8,10},{9,11},{10,... | collective-permute-start | bytes 393224 | tf_op jit(solution)/shard_map/ppermute | solution.py:16
  130.6 9.8 %collective-permute-start.49 = (bf16[768,128]{1,0:T(8,128)(2,1)S(1)}, bf16[768,128]{1,0:T(8,128)(2,1)S(1)}, u32[]{:S(2)}, u32[]{:S(2)}) collective-permute-start(bf16[768,128]{1,0:T(8,128)(2,1)S(1)} %get-tuple-element.184), channel_id=1, source_target_pairs={{0,1},{1,0},{2,3},{3,2},{4,5},{5,4},{6,7},{7,6},{8,9},{9,8},{10,11... | collective-permute-start | bytes 589832 | tf_op jit(solution)/shard_map/ppermute | solution.py:70
  145.6 10.6 %collective-permute-start.56 = (bf16[512,128]{1,0:T(8,128)(2,1)S(1)}, bf16[512,128]{1,0:T(8,128)(2,1)S(1)}, u32[]{:S(2)}, u32[]{:S(2)}) collective-permute-start(bf16[512,128]{1,0:T(8,128)(2,1)S(1)} %add_convert_fusion.5), channel_id=1, source_target_pairs={{0,2},{1,3},{2,4},{3,5},{4,6},{5,7},{6,0},{7,1},{8,10},{9,11},{10,... | collective-permute-start | bytes 393224 | tf_op jit(solution)/shard_map/ppermute | solution.py:16
  146.2 12.8 %collective-permute-start.60 = (bf16[512,128]{1,0:T(8,128)(2,1)S(1)}, bf16[512,128]{1,0:T(8,128)(2,1)S(1)}, u32[]{:S(2)}, u32[]{:S(2)}) collective-permute-start(bf16[512,128]{1,0:T(8,128)(2,1)S(1)} %convolution_convert_fusion), channel_id=1, source_target_pairs={{0,2},{1,3},{2,4},{3,5},{4,6},{5,7},{6,0},{7,1},{8,10},{9,11},{10,... | collective-permute-start | bytes 393224 | tf_op jit(solution)/shard_map/ppermute | solution.py:16
  149.5 12.4 %collective-permute-start.59 = (bf16[512,128]{1,0:T(8,128)(2,1)S(1)}, bf16[512,128]{1,0:T(8,128)(2,1)S(1)}, u32[]{:S(2)}, u32[]{:S(2)}) collective-permute-start(bf16[512,128]{1,0:T(8,128)(2,1)S(1)} %add_convert_fusion.4), channel_id=1, source_target_pairs={{0,2},{1,3},{2,4},{3,5},{4,6},{5,7},{6,0},{7,1},{8,10},{9,11},{10,... | collective-permute-start | bytes 393224 | tf_op jit(solution)/shard_map/ppermute | solution.py:16
  153.8 10.3 %collective-permute-start.58 = (bf16[512,128]{1,0:T(8,128)(2,1)S(1)}, bf16[512,128]{1,0:T(8,128)(2,1)S(1)}, u32[]{:S(2)}, u32[]{:S(2)}) collective-permute-start(bf16[512,128]{1,0:T(8,128)(2,1)S(1)} %add_convert_fusion.3), channel_id=1, source_target_pairs={{0,2},{1,3},{2,4},{3,5},{4,6},{5,7},{6,0},{7,1},{8,10},{9,11},{10,... | collective-permute-start | bytes 393224 | tf_op jit(solution)/shard_map/ppermute | solution.py:16
  (51 other events, 381.4 us)
